TPU v7x, 32 devices: a whole 2x2x4 slice. The times are simulated.
32 devices in a mesh: row: 4 (over x, core), col: 8 (over z, y).
Axes of the slice: x: 2, y: 2, z: 4, core: 2. Of those that a mesh axis runs over, the one named last changes fastest.
Arguments:
- inv_diag: float32 [2, 2048, 2048], P(None, 'row', 'col'), may hold values from -1 to 2, as said below
- coupling: float32 [2048, 2048], P('row', 'col'), may hold values from -0.125 to 0.125
- top_rhs: float32 [2, 2048, 1024], P(None, 'row', 'col'), may hold values from -6 to 6
- panel: float32 [2, 4096, 2048], P(None, 'row', 'col'), may hold values from -0.125 to 0.125
- rhs: float32 [4096, 1024], P('row', 'col'), may hold values from -6 to 6
Outputs:
- solved: float32 [2, 2048, 1024], P(None, 'row', 'col')
- trailing: float32 [4096, 1024], P('row', 'col')
Inputs may be any that keep to these rules, and one draw needn't show every extreme that they name: `inv_diag`: each of the two blocks is lower triangular with its diagonal in 1 to 2.
All inputs are finite; a program needn't handle non-finite values.
Results may differ from a plain program's by a relative error of at most 0.000073.
Values sent between devices are 32-bit elements; how exact they have to be, the bound alone decides.
No kernel may reach another device: no remote copies, remote signals or barrier semaphores. Data moves between devices by JAX's collectives and lax.ppermute only.
A program may use at most 64 MiB of HBM per device.

v0:
```python
import jax
import jax.numpy as jnp
from jax import lax
from jax.sharding import PartitionSpec as P


def product(left, right):
    return jnp.dot(left, right, precision=lax.Precision.HIGHEST, preferred_element_type=jnp.float32)


def folder(full_rows, piece):
    return product(piece, full_rows)


def body(inv_diag, coupling, top_rhs, panel, rhs):
    first_full_rhs = lax.all_gather(top_rhs[0], "row", axis=0, tiled=True)
    solved_one = folder(first_full_rhs, lax.all_gather(inv_diag[0], "col", axis=1, tiled=True))
    full_one = lax.all_gather(solved_one, "row", axis=0, tiled=True)
    reduced = top_rhs[1] - folder(full_one, lax.all_gather(coupling, "col", axis=1, tiled=True))
    reduced_full = lax.all_gather(reduced, "row", axis=0, tiled=True)
    solved_two = folder(reduced_full, lax.all_gather(inv_diag[1], "col", axis=1, tiled=True))
    full_two = lax.all_gather(solved_two, "row", axis=0, tiled=True)
    solved = jnp.stack([solved_one, solved_two])
    stacked_full = jnp.stack([full_one, full_two])
    all_times = lax.all_to_all(stacked_full, "col", split_axis=1, concat_axis=2, tiled=True)
    whole_term = jnp.einsum(
        "krw,kwt->rt",
        panel,
        all_times,
        precision=lax.Precision.HIGHEST,
        preferred_element_type=jnp.float32,
    )
    update = lax.psum_scatter(whole_term, "col", scatter_dimension=1, tiled=True)
    trailing = rhs - update
    return (solved, trailing)


def solution(mesh):
    in_specs = (
        P(None, "row", "col"),
        P("row", "col"),
        P(None, "row", "col"),
        P(None, "row", "col"),
        P("row", "col"),
    )
    out_specs = (P(None, "row", "col"), P("row", "col"))
    return jax.shard_map(body, mesh=mesh, in_specs=in_specs, out_specs=out_specs, check_vma=False)
```

profile of v0, /device:TPU:2, one launch (start us, length us, event | category | flops | bytes accessed | tf_op | source)
XLA Modules:
  0.0 486.9 jit_solution(668021510197324780)
XLA Ops:
  7.2 1.8 slice.13
  9.1 2.2 fusion.6
  11.4 0.7 all-gather.13.cloned.1.call-update
  12.2 14.2 %all-gather.21.cloned.1.call-done = f32[1,2048,128]{2,1,0:T(8,128)} async-done(((f32[1,512,128]{2,1,0:T(8,128)}), f32[1,2048,128]{2,1,0:T(8,128)}) %all-gather.21.cloned.1.call-update) | async-done | bytes 1048592 | tf_op jit(solution)/shard_map/all_gather | solution.py:16
  26.4 78.8 %all-gather.19.cloned.1.call-done = f32[1,512,2048]{2,1,0:T(8,128)} async-done(((f32[1,512,256]{2,1,0:T(8,128)}), f32[1,512,2048]{2,1,0:T(8,128)}) %all-gather.19.cloned.1.call-update) | async-done | bytes 4194320 | tf_op jit(solution)/shard_map/all_gather | solution.py:17
  105.2 6.6 %fusion.2 = f32[512,128]{1,0:T(8,128)} fusion(f32[1,512,2048]{2,1,0:T(8,128)} %all-gather.19.cloned.1.call-done, f32[1,2048,128]{2,1,0:T(8,128)} %all-gather.21.cloned.1.call-done), kind=kOutput, calls=%fused_computation.2 | convolution fusion | flops 1610612736 | bytes 5505024 | tf_op jit(solution)/shard_map/dot_general | solution.py:8
  111.9 0.5 all-gather.23.cloned.1.call-update
  112.5 68.0 %all-gather.13.cloned.1.call-done = f32[512,2048]{1,0:T(8,128)} async-done(((f32[512,256]{1,0:T(8,128)}), f32[512,2048]{1,0:T(8,128)}) %all-gather.13.cloned.1.call-update) | async-done | bytes 4194320 | tf_op jit(solution)/shard_map/all_gather | solution.py:19
  180.5 15.8 %all-gather.11.cloned.1.call-done = f32[2048,128]{1,0:T(8,128)} async-done(((f32[512,128]{1,0:T(8,128)}), f32[2048,128]{1,0:T(8,128)}) %all-gather.11.cloned.1.call-update) | async-done | bytes 1048592 | tf_op jit(solution)/shard_map/all_gather | solution.py:18
  196.3 6.6 %fusion.4 = f32[512,128]{1,0:T(8,128)} fusion(f32[2048,128]{1,0:T(8,128)} %all-gather.11.cloned.1.call-done, f32[512,2048]{1,0:T(8,128)} %all-gather.13.cloned.1.call-done, f32[2,512,128]{2,1,0:T(8,128)S(1)} %copy-done.4), kind=kOutput, calls=%fused_computation.7 | convolution fusion | flops 1610678272 | bytes 5767168 | tf_op jit(solution)/shard_map/dot_general | solution.py:8
  203.0 72.0 %all-gather.23.cloned.1.call-done = f32[1,512,2048]{2,1,0:T(8,128)} async-done(((f32[1,512,256]{2,1,0:T(8,128)}), f32[1,512,2048]{2,1,0:T(8,128)}) %all-gather.23.cloned.1.call-update) | async-done | bytes 4194320 | tf_op jit(solution)/shard_map/all_gather | solution.py:21
  275.0 15.2 %all-gather.15.cloned.1.call-done = f32[2048,128]{1,0:T(8,128)} async-done(((f32[512,128]{1,0:T(8,128)}), f32[2048,128]{1,0:T(8,128)}) %all-gather.15.cloned.1.call-update) | async-done | bytes 1048592 | tf_op jit(solution)/shard_map/all_gather | solution.py:20
  290.2 6.6 %fusion = f32[128,512]{0,1:T(8,128)} fusion(f32[2048,128]{1,0:T(8,128)} %all-gather.15.cloned.1.call-done, f32[1,512,2048]{2,1,0:T(8,128)} %all-gather.23.cloned.1.call-done), kind=kOutput, calls=%fused_computation | convolution fusion | flops 1610612736 | bytes 5505024 | tf_op jit(solution)/shard_map/dot_general | solution.py:8
  297.0 16.7 %all-gather.17.cloned.1.call-done = f32[2048,128]{1,0:T(8,128)} async-done(((f32[512,128]{1,0:T(8,128)}), f32[2048,128]{1,0:T(8,128)}) %all-gather.17.cloned.1.call-update) | async-done | bytes 1048592 | tf_op jit(solution)/shard_map/all_gather | solution.py:22
  313.7 1.4 pad_maximum_fusion
  315.1 7.6 %copy.12 = f32[2,2048,128]{2,0,1:T(2,128)S(1)} copy(f32[2,2048,128]{2,1,0:T(8,128)S(1)} %pad_maximum_fusion) | data formatting | bytes 4194304 | tf_op jit(solution)/shard_map/stack | solution.py:24
  322.7 54.2 %all_to_all.18 = f32[2,2048,128]{2,0,1:T(2,128)} all-to-all(f32[2,2048,128]{2,0,1:T(2,128)S(1)} %copy.12), channel_id=1, replica_groups=mesh['row'=4,'col'=8] {'col'}, dimensions={1} | all-to-all | bytes 4194304 | tf_op jit(solution)/shard_map/all_to_all | solution.py:25
  376.9 4.1 copy.13
  381.0 9.7 %convolution_bitcast_fusion = f32[1024,1024]{0,1:T(8,128)} fusion(f32[2,256,1024]{1,2,0:T(8,128)} %bitcast.35, f32[2,1024,256]{2,1,0:T(8,128)S(1)} %copy-done), kind=kOutput, calls=%fused_computation.4 | convolution fusion | flops 6442450944 | bytes 8388608 | tf_op jit(solution)/shard_map/krw,kwt->rt/dot_general | solution.py:26
  390.7 1.3 copy.14
  392.1 0.8 pad_maximum_fusion.1
  392.9 85.1 %reduce-scatter.2.cloned.1.call-done = f32[1024,128]{0,1:T(8,128)} async-done(((f32[1024,1024]{0,1:T(8,128)}), f32[1024,128]{0,1:T(8,128)}) %reduce-scatter.2.cloned.1.call-update) | async-done | bytes 524304 | tf_op jit(solution)/shard_map/reduce_scatter | solution.py:33
  478.0 1.1 sub.7
  479.1 1.0 copy.15
  (24 shorter events, 0.6 us)
Async XLA Ops:
  7.2 373.9 %copy-start = (f32[2,1024,256]{2,1,0:T(8,128)S(1)}, f32[2,1024,256]{2,1,0:T(8,128)}, u32[]{:S(2)}) copy-start(f32[2,1024,256]{2,1,0:T(8,128)} %param.8) | copy-start | bytes 6291460
  7.2 19.2 %all-gather.21.cloned.1.call-start = ((), (), s32[]{:S(2)}) async-start(), calls=%async_computation.8 | async-start | bytes 1310720 | tf_op jit(solution)/shard_map/all_gather | solution.py:16
  9.1 96.2 %all-gather.19.cloned.1.call-start = ((), (), s32[]{:S(2)}) async-start(), calls=%async_computation.7 | async-start | bytes 4718592 | tf_op jit(solution)/shard_map/all_gather | solution.py:17
  11.3 184.9 %copy-start.4 = (f32[2,512,128]{2,1,0:T(8,128)S(1)}, f32[2,512,128]{2,1,0:T(8,128)}, u32[]{:S(2)}) copy-start(f32[2,512,128]{2,1,0:T(8,128)} %param.7) | copy-start | bytes 1572868
  11.4 169.1 %all-gather.13.cloned.1.call-start = ((), (), s32[]{:S(2)}) async-start(), calls=%async_computation.3 | async-start | bytes 4718592 | tf_op jit(solution)/shard_map/all_gather | solution.py:19
  12.1 184.2 %all-gather.11.cloned.1.call-start = ((), (), s32[]{:S(2)}) async-start(), calls=%async_computation.2 | async-start | bytes 1310720 | tf_op jit(solution)/shard_map/all_gather | solution.py:18
  111.9 163.1 %all-gather.23.cloned.1.call-start = ((), (), s32[]{:S(2)}) async-start(), calls=%async_computation.9 | async-start | bytes 4718592 | tf_op jit(solution)/shard_map/all_gather | solution.py:21
  112.5 177.7 %all-gather.15.cloned.1.call-start = ((), (), s32[]{:S(2)}) async-start(), calls=%async_computation.4 | async-start | bytes 1310720 | tf_op jit(solution)/shard_map/all_gather | solution.py:20
  202.9 110.8 %copy-start.1 = (f32[2048,128]{1,0:T(8,128)S(1)}, f32[2048,128]{1,0:T(8,128)}, u32[]{:S(2)}) copy-start(f32[2048,128]{1,0:T(8,128)} %all-gather.11.cloned.1.call-done) | copy-start | bytes 3145732
  202.9 110.8 %all-gather.17.cloned.1.call-start = ((), (), s32[]{:S(2)}) async-start(), calls=%async_computation.5 | async-start | bytes 1310720 | tf_op jit(solution)/shard_map/all_gather | solution.py:22
  296.8 181.2 %reduce-scatter.2.cloned.1.call-start = ((), (), s32[]{:S(2)}) async-start(), calls=%async_computation.6 | async-start | bytes 4718592 | tf_op jit(solution)/shard_map/reduce_scatter | solution.py:33
  390.7 1.3 copy-start.2
  390.7 1.3 copy-start.3
Sparse Core Ops, SparseCore 0:
  9.6 16.7 all-gather.20
  29.0 76.1 all-gather.18
  107.3 73.1 all-gather.12
  182.5 13.7 all-gather.10
  198.8 76.1 all-gather.22
  276.4 13.7 all-gather.14
  296.9 16.7 all-gather.16
  390.9 87.0 reduce-scatter.1
where the time goes:
time: 489 us; the launch traced here: 487 us
  waiting for transfers between devices  367 us (75%)
  blocking collectives  54.2 us (11%)
  matrix products  29.5 us (6%)
  local copies, waits for them, and re-layouts  18.1 us (4%)
  between operations  14.2 us (3%)
    reduce_scatter x1, waiting for transfers between devices, body(): lax.psum_scatter(whole_term, 'col', scatter_dimension=1, tiled=True)  85.1 us
    all_gather x1, waiting for transfers between devices, body(): lax.all_gather(inv_diag[0], 'col', axis=1, tiled=True)  78.8 us
    all_gather x1, waiting for transfers between devices, body(): lax.all_gather(inv_diag[1], 'col', axis=1, tiled=True)  72 us
    all_gather x1, waiting for transfers between devices, body(): lax.all_gather(coupling, 'col', axis=1, tiled=True)  68 us
    all_to_all x1, blocking collectives, body(): lax.all_to_all(stacked_full, 'col', split_axis=1, concat_axis=2, tiled=True)  54.2 us
    dot_general x3, matrix products, product(): jnp.dot(left, right, precision=lax.Precision.HIGHEST, preferred_element_t...  19.9 us
    all_gather x1, waiting for transfers between devices, body(): full_two = lax.all_gather(solved_two, 'row', axis=0, tiled=True)  16.7 us
    all_gather x1, waiting for transfers between devices, body(): full_one = lax.all_gather(solved_one, 'row', axis=0, tiled=True)  15.8 us
  transfers between devices with their start and end apart: 8, of which 8 were waited for; matrix products, arithmetic and copies ran while one was open for 4% of the time, Pallas kernels for 0%

commit v1 on v0

v1 whole, which is shorter than its diff:
```python
import functools

import jax
import jax.numpy as jnp
from jax import lax
from jax.experimental import pallas as pl
from jax.experimental.pallas import tpu as pltpu
from jax.sharding import PartitionSpec as P

F32 = jnp.float32
BF16 = jnp.bfloat16
VMEM_LIMIT = 48 * 1024 * 1024


def split(value):
    high = value.astype(BF16)
    return high, (value - high.astype(F32)).astype(BF16)


def dot(left, right):
    return jnp.dot(left, right, preferred_element_type=F32)


def product(left, right):
    left_high, left_low = split(left)
    right_high, right_low = split(right)
    return dot(left_high, right_high) + (dot(left_high, right_low) + dot(left_low, right_high))


def stage_kernel(parts, where_ref, *refs):
    matrices, vector_ref, out_ref = refs[:parts], refs[parts], refs[parts + 1]
    blocks, shards, rows, depth = matrices[0].shape
    pieces = []
    for b in range(shards):
        start = pl.multiple_of(where_ref[b] * depth, depth)
        pieces.append(split(vector_ref[pl.ds(start, depth), :]))
    for part in range(parts):
        for k in range(blocks):
            total = None
            for b in range(shards):
                high, low = split(matrices[part][k, b])
                v_high, v_low = pieces[b]
                term = dot(high, v_high) + (dot(high, v_low) + dot(low, v_high))
                total = term if total is None else total + term
            out_ref[k, part * rows:(part + 1) * rows, :] = total


def stage(matrices, vector, where):
    parts = len(matrices)
    blocks, shards, rows, depth = matrices[0].shape
    width = vector.shape[1]
    return pl.pallas_call(
        functools.partial(stage_kernel, parts),
        out_shape=jax.ShapeDtypeStruct((blocks, parts * rows, width), F32),
        in_specs=[pl.BlockSpec(memory_space=pltpu.SMEM)]
        + [pl.BlockSpec(memory_space=pltpu.VMEM)] * (parts + 1),
        out_specs=pl.BlockSpec(memory_space=pltpu.VMEM),
        compiler_params=pltpu.CompilerParams(vmem_limit_bytes=VMEM_LIMIT),
        cost_estimate=pl.CostEstimate(
            flops=6 * blocks * shards * parts * rows * depth * width,
            bytes_accessed=4 * parts * blocks * shards * rows * depth + 4 * blocks * parts * rows * width,
            transcendentals=0,
        ),
    )(where, *matrices, vector)


def panel_kernel(shards, where_ref, *refs):
    panels, solved_refs, out_ref = refs[:shards], refs[shards:shards + 2], refs[shards + 2]
    depth = panels[0].shape[2]
    blocks = out_ref.shape[0]
    total = [None] * blocks
    for half in range(2):
        for b in range(shards):
            high, low = split(panels[b][half])
            start = pl.multiple_of(where_ref[b] * depth, depth)
            for k in range(blocks):
                v_high, v_low = split(solved_refs[half][k, pl.ds(start, depth), :])
                term = dot(high, v_high) + (dot(high, v_low) + dot(low, v_high))
                if half == 0 and b == 0:
                    out_ref[k] = term
                else:
                    out_ref[k] += term


def panel_product(panels, first, second, where):
    shards = len(panels)
    blocks, _, width = first.shape
    _, rows, depth = panels[0].shape
    return pl.pallas_call(
        functools.partial(panel_kernel, shards),
        out_shape=jax.ShapeDtypeStruct((blocks, rows, width), F32),
        in_specs=[pl.BlockSpec(memory_space=pltpu.SMEM)]
        + [pl.BlockSpec(memory_space=pltpu.VMEM)] * (shards + 2),
        out_specs=pl.BlockSpec(memory_space=pltpu.VMEM),
        compiler_params=pltpu.CompilerParams(vmem_limit_bytes=VMEM_LIMIT),
        cost_estimate=pl.CostEstimate(
            flops=12 * blocks * shards * rows * depth * width,
            bytes_accessed=8 * shards * rows * depth + 4 * blocks * rows * width,
            transcendentals=0,
        ),
    )(where, *panels, first, second)


def bits(count):
    found = []
    bit = count // 2
    while bit >= 1:
        found.append(bit)
        bit //= 2
    return found


def after(value, *earlier):
    return lax.optimization_barrier((value, *earlier))[0]


class Grid:
    def __init__(self, mesh):
        self.rows = mesh.shape["row"]
        self.cols = mesh.shape["col"]
        self.shards = self.cols // self.rows

    def move(self, value, target):
        pairs = []
        for r in range(self.rows):
            for a in range(self.rows):
                for b in range(self.shards):
                    to = target(r, a, b)
                    if to is not None:
                        pairs.append((
                            r * self.cols + a * self.shards + b,
                            to[0] * self.cols + to[1] * self.shards + to[2],
                        ))
        return lax.ppermute(value, ("row", "col"), pairs)

    def swap(self, value):
        return self.move(value, lambda r, a, b: (a, r, b))

    def row_bit(self, value, bit):
        return self.move(value, lambda r, a, b: (r ^ bit, a, b))

    def b_bit(self, value, bit):
        return self.move(value, lambda r, a, b: (r, a, b ^ bit))

    def gather_b(self, value, axis):
        for bit in reversed(bits(self.shards)):
            value = jnp.concatenate([value, self.b_bit(value, bit)], axis)
        return value

    def gather_row_far(self, value, axis):
        for bit in bits(self.rows)[:-1]:
            value = jnp.concatenate([value, self.row_bit(value, bit)], axis)
        return value

    def gather_row_near(self, value, axis):
        return jnp.concatenate([value, self.row_bit(value, 1)], axis)

    def row_order(self):
        order = [0]
        for bit in bits(self.rows):
            order = order + [o ^ bit for o in order]
        return order

    def gather_matrix(self, value):
        half = value.shape[0] // 2
        upper = value[:half][None, None]
        lower = value[half:][None, None]
        upper = self.gather_row_far(self.gather_b(upper, 1), 0)
        lower = self.gather_b(self.gather_row_far(lower, 0), 1)
        return self.gather_row_near(upper, 0), self.gather_row_near(lower, 0)

    def line_sum(self, block, a, two_way):
        n = self.rows
        right, left = None, None
        for step in range(1, n):
            send = block(jnp.clip(n - step + a, 0, n - 1))
            if right is not None:
                send = send + right
            right = self.move(
                send, lambda r, p, b: (r, p + 1, b) if p <= min(step - 1, n - 2) else None
            )
            if two_way:
                send = block(jnp.clip(step - 1 - (n - 1 - a), 0, n - 1))
                if left is not None:
                    send = send + left
                left = self.move(
                    send, lambda r, p, b: (r, p - 1, b) if p >= max(n - step, 1) else None
                )
        total = block(a) + right
        return total + left if two_way else total


def solution(mesh):
    grid = Grid(mesh)
    order = grid.row_order()
    place = [order.index(o) for o in range(grid.rows)]

    def body(inv_diag, coupling, top_rhs, panel, rhs):
        r = lax.axis_index("row")
        c = lax.axis_index("col")
        a, b = c // grid.shards, c % grid.shards
        places = jnp.array(place, jnp.int32)
        where = jnp.stack([b ^ o for o in range(grid.shards)]).astype(jnp.int32)

        def picker(blocks):
            def pick(j):
                return lax.dynamic_index_in_dim(blocks, places[j ^ r], 0, keepdims=False)

            return pick

        record_one = grid.swap(top_rhs[0])
        inverse_one = grid.gather_matrix(inv_diag[0])
        coupled = grid.gather_matrix(after(coupling, inverse_one[0]))
        record_two = grid.swap(after(top_rhs[1], record_one))
        inverse_two = grid.gather_matrix(after(inv_diag[1], coupled[0]))
        panels = [panel]
        gathered = after(panel, inverse_two[0])
        for o in range(1, grid.shards):
            panels.append(grid.b_bit(gathered, o))

        first = grid.line_sum(picker(stage(inverse_one, record_one, where)), a, False)
        term = grid.line_sum(picker(stage(coupled, first, where)), a, True)
        reduced = record_two - term
        first_all = grid.gather_row_near(grid.gather_row_far(first[None], 0), 0)
        solved_one = grid.swap(first)
        second = grid.line_sum(picker(stage(inverse_two, reduced, where)), a, False)
        second_all = grid.gather_row_near(grid.gather_row_far(second[None], 0), 0)
        solved_two = grid.swap(after(second, second_all))
        update = grid.line_sum(picker(panel_product(panels, first_all, second_all, where)), a, True)
        return jnp.stack([solved_one, solved_two]), rhs - update

    in_specs = (
        P(None, "row", "col"),
        P("row", "col"),
        P(None, "row", "col"),
        P(None, "row", "col"),
        P("row", "col"),
    )
    out_specs = (P(None, "row", "col"), P("row", "col"))
    return jax.shard_map(body, mesh=mesh, in_specs=in_specs, out_specs=out_specs, check_vma=False)
```

time: 489 us -> 304 us (0.62)
  waiting for transfers between devices: 367 us -> 141 us
  starting transfers between devices: 0.5 us -> 96.8 us
  blocking collectives: 54.2 us -> 0 us
  matrix products: 29.5 us -> 0 us
  other arithmetic: 3.29 us -> 26 us
  Pallas kernels: 0 us -> 16.1 us
  local copies, waits for them, and re-layouts: 18.1 us -> 8.17 us
    all_gather x7 -> x0, waiting for transfers between devices: 281 us -> none  [the longest x1 78.8 us: body(): lax.all_gather(inv_diag[0], 'col', axis=1, tiled=True)]
    ppermute x0 -> x45, waiting for transfers between devices: none -> 141 us  [move(): return lax.ppermute(value, ('row', 'col'), pairs)]
    ppermute x0 -> x45, starting transfers between devices: none -> 96.8 us  [move(): return lax.ppermute(value, ('row', 'col'), pairs)]
    reduce_scatter x1 -> x0, waiting for transfers between devices: 85.1 us -> none  [body(): lax.psum_scatter(whole_term, 'col', scatter_dimension=1, tiled=True)]
    all_to_all x1 -> x0, blocking collectives: 54.2 us -> none  [body(): lax.all_to_all(stacked_full, 'col', split_axis=1, concat_axis=2, tiled=True)]
    dot_general x4 -> x0, matrix products: 29.5 us -> none  [the longest x3 19.9 us: product(): jnp.dot(left, right, precision=lax.Precision.HIGHEST, preferred_element_t...]
    concatenate x0 -> x22, other arithmetic: none -> 19.4 us  [the longest x8 7.89 us: gather_row_near(): return jnp.concatenate([value, self.row_bit(value, 1)], axis)]
    pallas_call x0 -> x4, Pallas kernels: none -> 16.1 us  [the longest x1 8.97 us: panel_product(): pl.pallas_call(functools.partial(panel_kernel, shards), out_shape=jax.Sha...]
  transfers between devices with their start and end apart: 8 -> 45, of which waited for: 8 -> 23; matrix products, arithmetic and copies ran while one was open for 4% -> 9% of each run, Pallas kernels for 0% -> 2%
where the time goes in v1:
time: 304 us; the launch traced here: 303 us
  waiting for transfers between devices  141 us (46%)
  starting transfers between devices  96.8 us (32%)
  other arithmetic  26 us (9%)
  Pallas kernels  16.1 us (5%)
  between operations  14.7 us (5%)
  local copies, waits for them, and re-layouts  8.17 us (3%)
    ppermute x45, waiting for transfers between devices, move(): return lax.ppermute(value, ('row', 'col'), pairs)  141 us
    ppermute x45, starting transfers between devices, move(): return lax.ppermute(value, ('row', 'col'), pairs)  96.8 us
    pallas_call x1, Pallas kernels, panel_product(): pl.pallas_call(functools.partial(panel_kernel, shards), out_shape=jax.Sha...  8.97 us
    concatenate x8, other arithmetic, gather_row_near(): return jnp.concatenate([value, self.row_bit(value, 1)], axis)  7.89 us
    pallas_call x3, Pallas kernels, stage(): pl.pallas_call(functools.partial(stage_kernel, parts), out_shape=jax.Shap...  7.15 us
    concatenate x6, other arithmetic, gather_b(): value = jnp.concatenate([value, self.b_bit(value, bit)], axis)  6.17 us
  transfers between devices with their start and end apart: 45, of which 23 were waited for; matrix products, arithmetic and copies ran while one was open for 9% of the time, Pallas kernels for 2%

profile of v1, /device:TPU:2, one launch (start us, length us, event | category | flops | bytes accessed | tf_op | source)
XLA Modules:
  0.0 302.9 jit_solution(6868070547604561340)
XLA Ops:
  3.3 6.5 %collective-permute-done = f32[1,1,256,256]{3,2,1,0:T(8,128)S(1)} collective-permute-done((f32[1,1,256,256]{3,2,1,0:T(8,128)S(1)}, f32[1,1,256,256]{3,2,1,0:T(8,128)S(1)}, u32[]{:S(2)}, u32[]{:S(2)}) %collective-permute-start) | collective-permute-done | bytes 262176 | tf_op jit(solution)/shard_map/ppermute | solution.py:134
  11.9 12.8 %collective-permute-done.1 = f32[1,2,256,256]{3,2,1,0:T(8,128)S(1)} collective-permute-done((f32[1,2,256,256]{3,2,1,0:T(8,128)S(1)}, f32[1,2,256,256]{3,2,1,0:T(8,128)S(1)}, u32[]{:S(2)}, u32[]{:S(2)}) %collective-permute-start.1) | collective-permute-done | bytes 524320 | tf_op jit(solution)/shard_map/ppermute | solution.py:134
  29.9 10.4 %collective-permute-done.4 = f32[2,1,256,256]{3,2,1,0:T(8,128)S(1)} collective-permute-done((f32[2,1,256,256]{3,2,1,0:T(8,128)S(1)}, f32[2,1,256,256]{3,2,1,0:T(8,128)S(1)}, u32[]{:S(2)}, u32[]{:S(2)}) %collective-permute-start.4) | collective-permute-done | bytes 524320 | tf_op jit(solution)/shard_map/ppermute | solution.py:134
  45.6 4.5 %collective-permute-start.6 = (f32[512,128]{1,0:T(8,128)}, f32[512,128]{1,0:T(8,128)S(1)}, u32[]{:S(2)}, u32[]{:S(2)}) collective-permute-start(f32[512,128]{1,0:T(8,128)} %get-tuple-element.24), channel_id=1, source_target_pairs={{0,0},{1,1},{2,8},{3,9},{4,16},{5,17},{6,24},{7,25},{8,2},{9,3},{1... | collective-permute-start | bytes 786440 | tf_op jit(solution)/shard_map/ppermute | solution.py:134
  58.4 5.4 %collective-permute-done.6.refs_2_ = f32[512,128]{1,0:T(8,128)S(1)} collective-permute-done((f32[512,128]{1,0:T(8,128)}, f32[512,128]{1,0:T(8,128)S(1)}, u32[]{:S(2)}, u32[]{:S(2)}) %collective-permute-start.6) | collective-permute-done | bytes 262176 | tf_op jit(solution)/shard_map/ppermute | solution.py:134
  68.7 7.8 %collective-permute-done.21 = f32[1,1,256,256]{3,2,1,0:T(8,128)S(1)} collective-permute-done((f32[1,1,256,256]{3,2,1,0:T(8,128)}, f32[1,1,256,256]{3,2,1,0:T(8,128)S(1)}, u32[]{:S(2)}, u32[]{:S(2)}) %collective-permute-start.21) | collective-permute-done | bytes 262176 | tf_op jit(solution)/shard_map/ppermute | solution.py:134
  87.5 4.2 %collective-permute-done.22 = f32[2,1,256,256]{3,2,1,0:T(8,128)S(1)} collective-permute-done((f32[2,1,256,256]{3,2,1,0:T(8,128)S(1)}, f32[2,1,256,256]{3,2,1,0:T(8,128)S(1)}, u32[]{:S(2)}, u32[]{:S(2)}) %collective-permute-start.22) | collective-permute-done | bytes 524320 | tf_op jit(solution)/shard_map/ppermute | solution.py:134
  110.0 4.3 %collective-permute-start.24 = (f32[512,128]{1,0:T(8,128)S(1)}, f32[512,128]{1,0:T(8,128)S(1)}, u32[]{:S(2)}, u32[]{:S(2)}) collective-permute-start(f32[512,128]{1,0:T(8,128)S(1)} %get-tuple-element.18), channel_id=1, source_target_pairs={{0,2},{1,3},{8,10},{9,11},{16,18},{17,19},{24,26},{25,27}} | collective-permute-start | bytes 786440 | tf_op jit(solution)/shard_map/ppermute | solution.py:134
  135.2 6.3 %collective-permute-start.20 = (f32[512,128]{1,0:T(8,128)}, f32[512,128]{1,0:T(8,128)S(1)}, u32[]{:S(2)}, u32[]{:S(2)}) collective-permute-start(f32[512,128]{1,0:T(8,128)} %get-tuple-element.9), channel_id=1, source_target_pairs={{0,0},{1,1},{2,8},{3,9},{4,16},{5,17},{6,24},{7,25},{8,2},{9,3},{1... | collective-permute-start | bytes 786440 | tf_op jit(solution)/shard_map/ppermute | solution.py:134
  146.4 8.1 %collective-permute-done.20 = f32[512,128]{1,0:T(8,128)S(1)} collective-permute-done((f32[512,128]{1,0:T(8,128)}, f32[512,128]{1,0:T(8,128)S(1)}, u32[]{:S(2)}, u32[]{:S(2)}) %collective-permute-start.20) | collective-permute-done | bytes 262176 | tf_op jit(solution)/shard_map/ppermute | solution.py:134
  160.6 6.7 %collective-permute-start.30 = (f32[512,128]{1,0:T(8,128)S(1)}, f32[512,128]{1,0:T(8,128)S(1)}, u32[]{:S(2)}, u32[]{:S(2)}) collective-permute-start(f32[512,128]{1,0:T(8,128)S(1)} %dynamic-slice_bitcast_fusion.2), channel_id=1, source_target_pairs={{0,2},{1,3},{8,10},{9,11},{16,18},{17,19},{24,26},{25,27}} | collective-permute-start | bytes 786440 | tf_op jit(solution)/shard_map/ppermute | solution.py:134
  168.9 3.9 %collective-permute-done.30 = f32[512,128]{1,0:T(8,128)S(1)} collective-permute-done((f32[512,128]{1,0:T(8,128)S(1)}, f32[512,128]{1,0:T(8,128)S(1)}, u32[]{:S(2)}, u32[]{:S(2)}) %collective-permute-start.30) | collective-permute-done | bytes 262176 | tf_op jit(solution)/shard_map/ppermute | solution.py:134
  172.9 4.4 %collective-permute-start.31 = (f32[512,128]{1,0:T(8,128)S(1)}, f32[512,128]{1,0:T(8,128)S(1)}, u32[]{:S(2)}, u32[]{:S(2)}) collective-permute-start(f32[512,128]{1,0:T(8,128)S(1)} %bitcast_add_fusion.5), channel_id=1, source_target_pairs={{0,2},{1,3},{2,4},{3,5},{8,10},{9,11},{10,12},{11,13},{16,18},{17,... | collective-permute-start | bytes 786440 | tf_op jit(solution)/shard_map/ppermute | solution.py:134
  177.3 4.6 %collective-permute-done.31 = f32[512,128]{1,0:T(8,128)S(1)} collective-permute-done((f32[512,128]{1,0:T(8,128)S(1)}, f32[512,128]{1,0:T(8,128)S(1)}, u32[]{:S(2)}, u32[]{:S(2)}) %collective-permute-start.31) | collective-permute-done | bytes 262176 | tf_op jit(solution)/shard_map/ppermute | solution.py:134
  181.9 4.6 %collective-permute-start.32 = (f32[512,128]{1,0:T(8,128)S(1)}, f32[512,128]{1,0:T(8,128)S(1)}, u32[]{:S(2)}, u32[]{:S(2)}) collective-permute-start(f32[512,128]{1,0:T(8,128)S(1)} %bitcast_add_fusion.6), channel_id=1, source_target_pairs={{0,2},{1,3},{2,4},{3,5},{4,6},{5,7},{8,10},{9,11},{10,12},{11,13},... | collective-permute-start | bytes 786440 | tf_op jit(solution)/shard_map/ppermute | solution.py:134
  191.7 3.9 %collective-permute-done.37 = f32[1,512,128]{2,1,0:T(8,128)S(1)} collective-permute-done((f32[1,512,128]{2,1,0:T(8,128)S(1)}, f32[1,512,128]{2,1,0:T(8,128)S(1)}, u32[]{:S(2)}, u32[]{:S(2)}) %collective-permute-start.37) | collective-permute-done | bytes 262176 | tf_op jit(solution)/shard_map/ppermute | solution.py:134
  200.4 14.0 %collective-permute-done.36.refs_1_ = f32[2,1024,256]{2,1,0:T(8,128)S(1)} collective-permute-done((f32[2,1024,256]{2,1,0:T(8,128)S(1)}, f32[2,1024,256]{2,1,0:T(8,128)S(1)}, u32[]{:S(2)}, u32[]{:S(2)}) %collective-permute-start.36) | collective-permute-done | bytes 2097184 | tf_op jit(solution)/shard_map/ppermute | solution.py:134
  215.8 9.0 %shard_map.80 = f32[4,1024,128]{2,1,0:T(8,128)S(1)} custom-call(s32[2]{0:T(128)S(1)} %pad_add_fusion.where_ref, f32[2,1024,256]{2,1,0:T(8,128)} %refs_0_.1, f32[2,1024,256]{2,1,0:T(8,128)} %copy-done.14, f32[4,512,128]{2,1,0:T(8,128)S(1)} %pad_maximum_fusion.13.refs_2_, f32[4,512,128]{2,1,0:T(8,128)S(1)} %pad_maximum_fusion.12.refs_3_), custom_call_target="tpu_custom_call" | custom-call | flops 3221225472 | bytes 6291456 | tf_op jit(solution)/shard_map/pallas_call | solution.py:89
  227.1 9.5 %collective-permute-done.39 = f32[1024,128]{1,0:T(8,128)S(1)} collective-permute-done((f32[1024,128]{1,0:T(8,128)S(1)}, f32[1024,128]{1,0:T(8,128)S(1)}, u32[]{:S(2)}, u32[]{:S(2)}) %collective-permute-start.39) | collective-permute-done | bytes 524320 | tf_op jit(solution)/shard_map/ppermute | solution.py:134
  236.7 4.4 %collective-permute-start.40 = (f32[1024,128]{1,0:T(8,128)S(1)}, f32[1024,128]{1,0:T(8,128)S(1)}, u32[]{:S(2)}, u32[]{:S(2)}) collective-permute-start(f32[1024,128]{1,0:T(8,128)S(1)} %bitcast_add_fusion.2), channel_id=1, source_target_pairs={{0,2},{1,3},{2,4},{3,5},{8,10},{9,11},{10,12},{11,13},{16,18},{17,... | collective-permute-start | bytes 1572872 | tf_op jit(solution)/shard_map/ppermute | solution.py:134
  241.1 9.2 %collective-permute-done.40 = f32[1024,128]{1,0:T(8,128)S(1)} collective-permute-done((f32[1024,128]{1,0:T(8,128)S(1)}, f32[1024,128]{1,0:T(8,128)S(1)}, u32[]{:S(2)}, u32[]{:S(2)}) %collective-permute-start.40) | collective-permute-done | bytes 524320 | tf_op jit(solution)/shard_map/ppermute | solution.py:134
  251.3 5.0 %collective-permute-start.41 = (f32[1024,128]{1,0:T(8,128)S(1)}, f32[1024,128]{1,0:T(8,128)S(1)}, u32[]{:S(2)}, u32[]{:S(2)}) collective-permute-start(f32[1024,128]{1,0:T(8,128)S(1)} %get-tuple-element.12), channel_id=1, source_target_pairs={{0,2},{1,3},{2,4},{3,5},{4,6},{5,7},{8,10},{9,11},{10,12},{11,13},... | collective-permute-start | bytes 1572872 | tf_op jit(solution)/shard_map/ppermute | solution.py:134
  257.7 14.8 %collective-permute-start.10 = (f32[512,128]{1,0:T(8,128)S(1)}, f32[512,128]{1,0:T(8,128)S(1)}, u32[]{:S(2)}, u32[]{:S(2)}) collective-permute-start(f32[512,128]{1,0:T(8,128)S(1)} %bitcast_add_fusion.15.refs_2_), channel_id=1, source_target_pairs={{0,0},{1,1},{2,8},{3,9},{4,16},{5,17},{6,24},{7,25},{8,2},{9,3},{1... | collective-permute-start | bytes 786440 | tf_op jit(solution)/shard_map/ppermute | solution.py:134
  274.4 23.9 %collective-permute-done.10 = f32[512,128]{1,0:T(8,128)S(1)} collective-permute-done((f32[512,128]{1,0:T(8,128)S(1)}, f32[512,128]{1,0:T(8,128)S(1)}, u32[]{:S(2)}, u32[]{:S(2)}) %collective-permute-start.10) | collective-permute-done | bytes 262176 | tf_op jit(solution)/shard_map/ppermute | solution.py:134
  (148 shorter events, 100.1 us)
Async XLA Ops:
  9.8 14.9 %collective-permute-start.1 = (f32[1,2,256,256]{3,2,1,0:T(8,128)S(1)}, f32[1,2,256,256]{3,2,1,0:T(8,128)S(1)}, u32[]{:S(2)}, u32[]{:S(2)}) collective-permute-start(f32[1,2,256,256]{3,2,1,0:T(8,128)S(1)} %pad_maximum_fusion.14), channel_id=1, source_target_pairs={{0,16},{1,17},{2,18},{3,19},{4,20},{5,21},{6,22},{7,23},{8,24},{9,... | collective-permute-start | bytes 1572872 | tf_op jit(solution)/shard_map/ppermute | solution.py:134
  10.2 18.1 %collective-permute-start.3 = (f32[1,1,256,256]{3,2,1,0:T(8,128)S(1)}, f32[1,1,256,256]{3,2,1,0:T(8,128)S(1)}, u32[]{:S(2)}, u32[]{:S(2)}) collective-permute-start(f32[1,1,256,256]{3,2,1,0:T(8,128)S(1)} %get-tuple-element.20), channel_id=1, source_target_pairs={{0,16},{1,17},{2,18},{3,19},{4,20},{5,21},{6,22},{7,23},{8,24},{9,... | collective-permute-start | bytes 786440 | tf_op jit(solution)/shard_map/ppermute | solution.py:134
  24.9 16.6 %collective-permute-start.2 = (f32[2,2,256,256]{3,2,1,0:T(8,128)S(1)}, f32[2,2,256,256]{3,2,1,0:T(8,128)S(1)}, u32[]{:S(2)}, u32[]{:S(2)}) collective-permute-start(f32[2,2,256,256]{3,2,1,0:T(8,128)S(1)} %pad_maximum_fusion.6), channel_id=1, source_target_pairs={{0,8},{1,9},{2,10},{3,11},{4,12},{5,13},{6,14},{7,15},{8,0},{9,1},... | collective-permute-start | bytes 3145736 | tf_op jit(solution)/shard_map/ppermute | solution.py:134
  41.5 15.3 %collective-permute-start.5 = (f32[2,2,256,256]{3,2,1,0:T(8,128)}, f32[2,2,256,256]{3,2,1,0:T(8,128)}, u32[]{:S(2)}, u32[]{:S(2)}) collective-permute-start(f32[2,2,256,256]{3,2,1,0:T(8,128)} %pad_maximum_fusion.7), channel_id=1, source_target_pairs={{0,8},{1,9},{2,10},{3,11},{4,12},{5,13},{6,14},{7,15},{8,0},{9,1},... | collective-permute-start | bytes 3145736 | tf_op jit(solution)/shard_map/ppermute | solution.py:134
  45.6 18.2 %collective-permute-start.6 = (f32[512,128]{1,0:T(8,128)}, f32[512,128]{1,0:T(8,128)S(1)}, u32[]{:S(2)}, u32[]{:S(2)}) collective-permute-start(f32[512,128]{1,0:T(8,128)} %get-tuple-element.24), channel_id=1, source_target_pairs={{0,0},{1,1},{2,8},{3,9},{4,16},{5,17},{6,24},{7,25},{8,2},{9,3},{1... | collective-permute-start | bytes 786440 | tf_op jit(solution)/shard_map/ppermute | solution.py:134
  52.1 28.6 %collective-permute-start.12 = (f32[1,2,256,256]{3,2,1,0:T(8,128)}, f32[1,2,256,256]{3,2,1,0:T(8,128)}, u32[]{:S(2)}, u32[]{:S(2)}) collective-permute-start(f32[1,2,256,256]{3,2,1,0:T(8,128)} %pad_maximum_fusion.16), channel_id=1, source_target_pairs={{0,16},{1,17},{2,18},{3,19},{4,20},{5,21},{6,22},{7,23},{8,24},{9,... | collective-permute-start | bytes 1572872 | tf_op jit(solution)/shard_map/ppermute | solution.py:134
  55.7 20.8 %collective-permute-start.21 = (f32[1,1,256,256]{3,2,1,0:T(8,128)}, f32[1,1,256,256]{3,2,1,0:T(8,128)S(1)}, u32[]{:S(2)}, u32[]{:S(2)}) collective-permute-start(f32[1,1,256,256]{3,2,1,0:T(8,128)} %get-tuple-element.22), channel_id=1, source_target_pairs={{0,16},{1,17},{2,18},{3,19},{4,20},{5,21},{6,22},{7,23},{8,24},{9,... | collective-permute-start | bytes 786440 | tf_op jit(solution)/shard_map/ppermute | solution.py:134
  66.2 16.7 %collective-permute-start.7 = (f32[512,128]{1,0:T(8,128)S(1)}, f32[512,128]{1,0:T(8,128)S(1)}, u32[]{:S(2)}, u32[]{:S(2)}) collective-permute-start(f32[512,128]{1,0:T(8,128)S(1)} %dynamic-slice_bitcast_fusion.5), channel_id=1, source_target_pairs={{0,2},{1,3},{8,10},{9,11},{16,18},{17,19},{24,26},{25,27}} | collective-permute-start | bytes 786440 | tf_op jit(solution)/shard_map/ppermute | solution.py:134
  78.2 13.5 %collective-permute-start.22 = (f32[2,1,256,256]{3,2,1,0:T(8,128)S(1)}, f32[2,1,256,256]{3,2,1,0:T(8,128)S(1)}, u32[]{:S(2)}, u32[]{:S(2)}) collective-permute-start(f32[2,1,256,256]{3,2,1,0:T(8,128)S(1)} %pad_maximum_fusion.19), channel_id=1, source_target_pairs={{0,1},{1,0},{2,3},{3,2},{4,5},{5,4},{6,7},{7,6},{8,9},{9,8},{10,11... | collective-permute-start | bytes 1572872 | tf_op jit(solution)/shard_map/ppermute | solution.py:134
  82.9 19.9 %collective-permute-start.13 = (f32[2,2,256,256]{3,2,1,0:T(8,128)}, f32[2,2,256,256]{3,2,1,0:T(8,128)}, u32[]{:S(2)}, u32[]{:S(2)}) collective-permute-start(f32[2,2,256,256]{3,2,1,0:T(8,128)} %pad_maximum_fusion.8), channel_id=1, source_target_pairs={{0,8},{1,9},{2,10},{3,11},{4,12},{5,13},{6,14},{7,15},{8,0},{9,1},... | collective-permute-start | bytes 3145736 | tf_op jit(solution)/shard_map/ppermute | solution.py:134
  104.5 13.2 %collective-permute-start.14 = (f32[1,1,256,256]{3,2,1,0:T(8,128)S(1)}, f32[1,1,256,256]{3,2,1,0:T(8,128)S(1)}, u32[]{:S(2)}, u32[]{:S(2)}) collective-permute-start(f32[1,1,256,256]{3,2,1,0:T(8,128)S(1)} %get-tuple-element.27), channel_id=1, source_target_pairs={{0,1},{1,0},{2,3},{3,2},{4,5},{5,4},{6,7},{7,6},{8,9},{9,8},{10,11... | collective-permute-start | bytes 786440 | tf_op jit(solution)/shard_map/ppermute | solution.py:134
  118.6 13.2 %collective-permute-start.15 = (f32[1,2,256,256]{3,2,1,0:T(8,128)}, f32[1,2,256,256]{3,2,1,0:T(8,128)S(1)}, u32[]{:S(2)}, u32[]{:S(2)}) collective-permute-start(f32[1,2,256,256]{3,2,1,0:T(8,128)} %pad_maximum_fusion.17), channel_id=1, source_target_pairs={{0,16},{1,17},{2,18},{3,19},{4,20},{5,21},{6,22},{7,23},{8,24},{9,... | collective-permute-start | bytes 1572872 | tf_op jit(solution)/shard_map/ppermute | solution.py:134
  128.5 26.7 %collective-permute-start.19 = (f32[2,2,256,256]{3,2,1,0:T(8,128)}, f32[2,2,256,256]{3,2,1,0:T(8,128)}, u32[]{:S(2)}, u32[]{:S(2)}) collective-permute-start(f32[2,2,256,256]{3,2,1,0:T(8,128)} %pad_maximum_fusion.10), channel_id=1, source_target_pairs={{0,8},{1,9},{2,10},{3,11},{4,12},{5,13},{6,14},{7,15},{8,0},{9,1},... | collective-permute-start | bytes 3145736 | tf_op jit(solution)/shard_map/ppermute | solution.py:134
  130.4 13.7 %collective-permute-start.28 = (f32[512,128]{1,0:T(8,128)}, f32[512,128]{1,0:T(8,128)}, u32[]{:S(2)}, u32[]{:S(2)}) collective-permute-start(f32[512,128]{1,0:T(8,128)} %get-tuple-element.17), channel_id=1, source_target_pairs={{4,2},{5,3},{6,4},{7,5},{12,10},{13,11},{14,12},{15,13},{20,18},{2... | collective-permute-start | bytes 786440 | tf_op jit(solution)/shard_map/ppermute | solution.py:134
  132.8 23.9 %collective-permute-start.16 = (f32[2,2,256,256]{3,2,1,0:T(8,128)}, f32[2,2,256,256]{3,2,1,0:T(8,128)}, u32[]{:S(2)}, u32[]{:S(2)}) collective-permute-start(f32[2,2,256,256]{3,2,1,0:T(8,128)} %pad_maximum_fusion.9), channel_id=1, source_target_pairs={{0,8},{1,9},{2,10},{3,11},{4,12},{5,13},{6,14},{7,15},{8,0},{9,1},... | collective-permute-start | bytes 3145736 | tf_op jit(solution)/shard_map/ppermute | solution.py:134
  135.2 19.3 %collective-permute-start.20 = (f32[512,128]{1,0:T(8,128)}, f32[512,128]{1,0:T(8,128)S(1)}, u32[]{:S(2)}, u32[]{:S(2)}) collective-permute-start(f32[512,128]{1,0:T(8,128)} %get-tuple-element.9), channel_id=1, source_target_pairs={{0,0},{1,1},{2,8},{3,9},{4,16},{5,17},{6,24},{7,25},{8,2},{9,3},{1... | collective-permute-start | bytes 786440 | tf_op jit(solution)/shard_map/ppermute | solution.py:134
  141.5 13.0 %collective-permute-start.26 = (f32[512,128]{1,0:T(8,128)}, f32[512,128]{1,0:T(8,128)S(1)}, u32[]{:S(2)}, u32[]{:S(2)}) collective-permute-start(f32[512,128]{1,0:T(8,128)} %get-tuple-element.16), channel_id=1, source_target_pairs={{0,2},{1,3},{2,4},{3,5},{4,6},{5,7},{8,10},{9,11},{10,12},{11,13},... | collective-permute-start | bytes 786440 | tf_op jit(solution)/shard_map/ppermute | solution.py:134
  167.4 47.1 %collective-permute-start.36 = (f32[2,1024,256]{2,1,0:T(8,128)S(1)}, f32[2,1024,256]{2,1,0:T(8,128)S(1)}, u32[]{:S(2)}, u32[]{:S(2)}) collective-permute-start(f32[2,1024,256]{2,1,0:T(8,128)S(1)} %copy-done.13), channel_id=1, source_target_pairs={{0,1},{1,0},{2,3},{3,2},{4,5},{5,4},{6,7},{7,6},{8,9},{9,8},{10,11... | collective-permute-start | bytes 6291464 | tf_op jit(solution)/shard_map/ppermute | solution.py:134
  226.4 14.7 %collective-permute-start.42 = (f32[1024,128]{1,0:T(8,128)S(1)}, f32[1024,128]{1,0:T(8,128)S(1)}, u32[]{:S(2)}, u32[]{:S(2)}) collective-permute-start(f32[1024,128]{1,0:T(8,128)S(1)} %get-tuple-element.15), channel_id=1, source_target_pairs={{6,4},{7,5},{14,12},{15,13},{22,20},{23,21},{30,28},{31,29}} | collective-permute-start | bytes 1572872 | tf_op jit(solution)/shard_map/ppermute | solution.py:134
  236.7 13.7 %collective-permute-start.40 = (f32[1024,128]{1,0:T(8,128)S(1)}, f32[1024,128]{1,0:T(8,128)S(1)}, u32[]{:S(2)}, u32[]{:S(2)}) collective-permute-start(f32[1024,128]{1,0:T(8,128)S(1)} %bitcast_add_fusion.2), channel_id=1, source_target_pairs={{0,2},{1,3},{2,4},{3,5},{8,10},{9,11},{10,12},{11,13},{16,18},{17,... | collective-permute-start | bytes 1572872 | tf_op jit(solution)/shard_map/ppermute | solution.py:134
  251.3 50.6 %collective-permute-start.41 = (f32[1024,128]{1,0:T(8,128)S(1)}, f32[1024,128]{1,0:T(8,128)S(1)}, u32[]{:S(2)}, u32[]{:S(2)}) collective-permute-start(f32[1024,128]{1,0:T(8,128)S(1)} %get-tuple-element.12), channel_id=1, source_target_pairs={{0,2},{1,3},{2,4},{3,5},{4,6},{5,7},{8,10},{9,11},{10,12},{11,13},... | collective-permute-start | bytes 1572872 | tf_op jit(solution)/shard_map/ppermute | solution.py:134
  256.4 45.5 %collective-permute-start.44 = (f32[1024,128]{1,0:T(8,128)S(1)}, f32[1024,128]{1,0:T(8,128)S(1)}, u32[]{:S(2)}, u32[]{:S(2)}) collective-permute-start(f32[1024,128]{1,0:T(8,128)S(1)} %bitcast_add_fusion.1), channel_id=1, source_target_pairs={{2,0},{3,1},{4,2},{5,3},{6,4},{7,5},{10,8},{11,9},{12,10},{13,11},... | collective-permute-start | bytes 1572872 | tf_op jit(solution)/shard_map/ppermute | solution.py:134
  257.7 40.6 %collective-permute-start.10 = (f32[512,128]{1,0:T(8,128)S(1)}, f32[512,128]{1,0:T(8,128)S(1)}, u32[]{:S(2)}, u32[]{:S(2)}) collective-permute-start(f32[512,128]{1,0:T(8,128)S(1)} %bitcast_add_fusion.15.refs_2_), channel_id=1, source_target_pairs={{0,0},{1,1},{2,8},{3,9},{4,16},{5,17},{6,24},{7,25},{8,2},{9,3},{1... | collective-permute-start | bytes 786440 | tf_op jit(solution)/shard_map/ppermute | solution.py:134
  272.5 28.6 %collective-permute-start.35 = (f32[512,128]{1,0:T(8,128)S(1)}, f32[512,128]{1,0:T(8,128)S(1)}, u32[]{:S(2)}, u32[]{:S(2)}) collective-permute-start(f32[512,128]{1,0:T(8,128)S(1)} %bitcast_add_fusion.7), channel_id=1, source_target_pairs={{0,0},{1,1},{2,8},{3,9},{4,16},{5,17},{6,24},{7,25},{8,2},{9,3},{1... | collective-permute-start | bytes 786440 | tf_op jit(solution)/shard_map/ppermute | solution.py:134
  (36 other events, 348.7 us)

commit v2 on v0

v2 whole, which is shorter than its diff:
```python
import functools

import jax
import jax.numpy as jnp
from jax import lax
from jax.experimental import pallas as pl
from jax.experimental.pallas import tpu as pltpu
from jax.sharding import PartitionSpec as P

F32 = jnp.float32
BF16 = jnp.bfloat16
VMEM_LIMIT = 32 * 1024 * 1024
SMEM = pl.BlockSpec(memory_space=pltpu.SMEM)
HBM = pl.BlockSpec(memory_space=pltpu.HBM)


def split(value):
    high = value.astype(BF16)
    return high, (value - high.astype(F32)).astype(BF16)


def dot(left, right):
    return jnp.dot(left, right, preferred_element_type=F32)


def product(left, right):
    return dot(left[0], right[0]) + (dot(left[0], right[1]) + dot(left[1], right[0]))


def shape(dtype, *dims):
    return jax.ShapeDtypeStruct(dims, dtype)


def call(kernel, outs, scratch, flops, where, *operands):
    moved = sum(v.size * v.dtype.itemsize for v in (*operands, *outs))
    return pl.pallas_call(
        kernel,
        out_shape=outs,
        in_specs=[SMEM] + [HBM] * len(operands),
        out_specs=[HBM] * len(outs),
        scratch_shapes=scratch,
        compiler_params=pltpu.CompilerParams(vmem_limit_bytes=VMEM_LIMIT),
        cost_estimate=pl.CostEstimate(flops=flops, bytes_accessed=moved, transcendentals=0),
    )(where, *operands)


def start(source, target, sem):
    copy = pltpu.make_async_copy(source, target, sem)
    copy.start()
    return copy


def stage_kernel(places, shards, blocks, record, where_ref, *refs):
    count = len(places)
    pieces, given = refs[:count], refs[count:-blocks - 7]
    vector_out, outs = refs[-blocks - 7], refs[-blocks - 6:-6]
    matrix_ref, given_ref, vector_ref, product_ref, sems, given_sems = refs[-6:]
    arrivals = [start(ref, given_ref.at[i], given_sems.at[i]) for i, ref in enumerate(given)] if not record else []
    core = where_ref[shards + 1]
    if record:
        width = given[0].shape[1]
        for i, side in enumerate((core, 1 - core)):
            lanes = pl.ds(pl.multiple_of(side * width, width), width)
            arrivals.append(start(given[i], vector_ref.at[:, lanes], given_sems.at[i]))
        arrivals += [start(ref, given_ref.at[i], given_sems.at[2 + i]) for i, ref in enumerate(given[2:])]
    copies = [start(pieces[i], matrix_ref.at[place], sems.at[i]) for i, place in enumerate(places)]
    offset = where_ref[shards]
    for copy in arrivals:
        copy.wait()
    if not record:
        vector_ref[...] = given_ref[0] + given_ref[1]
    elif len(given) > 2:
        vector_ref[...] = vector_ref[...] - (given_ref[0] + given_ref[1])
    leaving = [start(vector_ref, vector_out, given_sems.at[0])]
    product_ref[blocks // 2] = jnp.zeros_like(product_ref[blocks // 2])
    depth = vector_ref.shape[0] // shards
    parts = [
        split(vector_ref[pl.ds(pl.multiple_of(where_ref[o] * depth, depth), depth), :]) for o in range(shards)
    ]
    for k in range(blocks // 2):
        for i, place in enumerate(places):
            if place[0] == k:
                copies[i].wait()
        sums = [product(split(matrix_ref[k, o]), parts[o]) for o in range(shards)]
        product_ref[k] = sum(sums[1:], sums[0])
    for d in range(blocks):
        k = jnp.bitwise_xor(offset, d) // 2
        if d == 0:
            k = jnp.where(lax.rem(offset, 2) == 1, blocks // 2, k)
        leaving.append(start(product_ref.at[k], outs[d], sems.at[d]))
    for copy in leaving:
        copy.wait()


def stage(blocks, where, matrix, *given, record):
    shards = len(matrix) * 2 // blocks
    rows, depth = matrix[0, 0].shape
    width = given[0].shape[1] * (2 if record else 1)
    outs = [shape(F32, shards * depth, width)] + [shape(F32, rows, width)] * blocks
    scratch = [
        pltpu.VMEM((blocks // 2, shards, rows, depth), F32),
        pltpu.VMEM((2, shards * depth, width), F32),
        pltpu.VMEM((shards * depth, width), F32),
        pltpu.VMEM((blocks // 2 + 1, rows, width), F32),
        pltpu.SemaphoreType.DMA((max(len(matrix), blocks),)),
        pltpu.SemaphoreType.DMA((4,)),
    ]
    kernel = functools.partial(stage_kernel, list(matrix), shards, blocks, record)
    flops = 3 * blocks * rows * shards * depth * width
    found = call(kernel, outs, scratch, flops, where, *matrix.values(), *given)
    return found[0], list(found[1:])


def panel_kernel(shards, blocks, parts, where_ref, *refs):
    panels, pairs = refs[:shards], refs[shards:shards + blocks // 2 * parts]
    earlier = refs[shards + len(pairs):-blocks - 9]
    outs = refs[-blocks - 9:-9]
    panel_ref, pair_ref, p_high, p_low, v_high, v_low, total_ref, sems, out_sems = refs[-9:]
    width, depth = total_ref.shape[2], panel_ref.shape[2]
    copies = [start(ref, pair_ref.at[i], sems.at[i]) for i, ref in enumerate(pairs)]
    copies += [start(ref, panel_ref.at[o], sems.at[len(pairs) + o]) for o, ref in enumerate(panels)]
    loads = [start(ref, total_ref.at[d], out_sems.at[d]) for d, ref in enumerate(earlier)]
    for copy in copies[:len(pairs)]:
        copy.wait()
    for k in range(blocks // 2):
        for o in range(shards):
            rows = pl.ds(pl.multiple_of(where_ref[blocks + o] * depth, depth), depth)
            value = pair_ref[k * parts, rows, :]
            for i in range(1, parts):
                value = value + pair_ref[k * parts + i, rows, :]
            high, low = split(value)
            for side in range(2):
                lanes = slice(side * width, (side + 1) * width)
                v_high[2 * k + side, o * depth:(o + 1) * depth, :] = high[:, lanes]
                v_low[2 * k + side, o * depth:(o + 1) * depth, :] = low[:, lanes]
    for o, copy in enumerate(copies[len(pairs):]):
        copy.wait()
        p_high[:, o * depth:(o + 1) * depth], p_low[:, o * depth:(o + 1) * depth] = split(panel_ref[o])
    leaving = []
    for d in reversed(range(blocks)):
        k = where_ref[d]
        high, low = v_high[k], v_low[k]
        both = dot(p_high[...], jnp.concatenate([high, low], 1))
        total = both[:, :width] + (both[:, width:] + dot(p_low[...], high))
        if earlier:
            loads[d].wait()
            total = total_ref[d] + total
        total_ref[d] = total
        leaving.append(start(total_ref.at[d], outs[d], out_sems.at[d]))
    for copy in leaving:
        copy.wait()


def panel_product(where, panel, pairs, earlier):
    shards, blocks, parts = len(panel), len(pairs) * 2, len(pairs[0])
    rows, depth = panel[0].shape
    width = pairs[0][0].shape[1]
    given = [part for pair in pairs for part in pair]
    outs = [shape(F32, rows, width // 2)] * blocks
    scratch = [
        pltpu.VMEM((shards, rows, depth), F32),
        pltpu.VMEM((len(given), shards * depth, width), F32),
        pltpu.VMEM((rows, shards * depth), BF16),
        pltpu.VMEM((rows, shards * depth), BF16),
        pltpu.VMEM((blocks, shards * depth, width // 2), BF16),
        pltpu.VMEM((blocks, shards * depth, width // 2), BF16),
        pltpu.VMEM((blocks, rows, width // 2), F32),
        pltpu.SemaphoreType.DMA((len(given) + shards,)),
        pltpu.SemaphoreType.DMA((blocks,)),
    ]
    kernel = functools.partial(panel_kernel, shards, blocks, parts)
    flops = 3 * blocks * rows * shards * depth * width
    return list(call(kernel, outs, scratch, flops, where, *panel, *given, *earlier))


def after(value, *earlier):
    return lax.optimization_barrier((value, *earlier))[0]


def together(*values):
    return list(lax.optimization_barrier(values))


class Grid:
    def __init__(self, mesh):
        self.rows = mesh.shape["row"]
        self.cols = mesh.shape["col"]
        self.shards = self.cols // self.rows

    def move(self, value, target):
        pairs = []
        for r in range(self.rows):
            for a in range(self.rows):
                for b in range(self.shards):
                    to = target(r, a, b)
                    if to is not None:
                        pairs.append((
                            r * self.cols + a * self.shards + b,
                            to[0] * self.cols + to[1] * self.shards + to[2],
                        ))
        return lax.ppermute(value, ("row", "col"), pairs)

    def swap(self, value):
        return self.move(value, lambda r, a, b: (a, r, b))

    def row_bit(self, value, bit):
        return self.move(value, lambda r, a, b: (r ^ bit, a, b))

    def gather_b(self, value):
        return {(0, o): self.b_bit(value, o) if o else value for o in range(self.shards)}

    def b_bit(self, value, bit):
        return self.move(value, lambda r, a, b: (r, a, b ^ bit))

    def gather_row(self, pieces):
        found = dict(pieces)
        for k in range(2, self.rows, 2):
            for (_, o), piece in pieces.items():
                found[k // 2, o] = self.row_bit(piece, k)
        return found

    def send(self, blocks, two_way):
        total = blocks[0]
        got = []
        for d in reversed(range(1, self.rows)):
            got.append(self.move(
                blocks[d],
                lambda r, a, b: (r, a ^ d, b)
                if (r ^ a ^ d) % 2 == 0 and (two_way or (a ^ d) > a) else None,
            ))
        for block in got:
            total = total + block
        return total

    def both(self, total):
        return total, self.row_bit(total, 1)

    def pair_send(self, blocks, last):
        sums = {d: blocks[d] for d in range(0, self.rows, 2)}
        for d in reversed(range(3, self.rows, 2)):
            sums[d - 1] = sums[d - 1] + self.move(blocks[d], lambda r, a, b: (r, a ^ 1, b))
        got = [self.move(after(blocks[1], *last), lambda r, a, b: (r, a ^ 1, b))]
        for d in reversed(range(2, self.rows, 2)):
            got.append(self.move(sums[d], lambda r, a, b: (r, a ^ d, b)))
        return [blocks[0], *got]


def solution(mesh):
    grid = Grid(mesh)
    rows, shards = grid.rows, grid.shards

    def body(inv_diag, coupling, top_rhs, panel, rhs):
        r = lax.axis_index("row")
        c = lax.axis_index("col")
        a, b = c // shards, c % shards
        where = jnp.stack([b ^ o for o in range(shards)] + [a ^ r, r % 2]).astype(jnp.int32)
        planes = [a ^ d for d in range(rows)]
        slots = [(j ^ r) // 2 * 2 + j % 2 for j in planes] + [b ^ o for o in range(shards)]
        slots = jnp.stack(slots).astype(jnp.int32)
        run = functools.partial(stage, rows, where)
        width = top_rhs.shape[2]

        record_one = grid.swap(top_rhs[0])
        inverse_one = grid.gather_b(inv_diag[0])
        far = {(k // 2, 0): grid.row_bit(inv_diag[0], k) for k in range(2, rows, 2)}
        early = [record_one, *inverse_one.values(), *far.values()]
        for k in range(2, rows, 2):
            for o in range(1, shards):
                far[k // 2, o] = grid.move(inv_diag[0], lambda r, a, b: (r ^ k, a, b ^ o))
        inverse_one |= far
        held = after(coupling, *early)
        coupled = grid.gather_b(held)
        coupled |= {(k // 2, 0): grid.row_bit(held, k) for k in range(2, rows, 2)}
        record_two = grid.swap(after(top_rhs[1], *early))
        first_in = grid.both(record_one)
        first_in = together(*first_in, record_two)[:2]
        _, blocks = run(inverse_one, *first_in, record=True)

        for k in range(2, rows, 2):
            for o in range(1, shards):
                coupled[k // 2, o] = grid.row_bit(after(coupled[0, o], blocks[0]), k)
        panel_one = grid.gather_b(after(panel[0], *inverse_one.values()))
        held = after(inv_diag[1], *coupled.values())
        sums = list(grid.both(grid.send(blocks, False)))
        sums[0] = after(sums[0], *panel_one.values())
        first, blocks = run(coupled, *sums, record=False)
        inverse_two = grid.gather_row(grid.gather_b(held))
        panel_two = grid.gather_b(after(panel[1], *panel_one.values()))
        sums = list(grid.both(grid.send(blocks, True)))
        sums[0] = after(sums[0], *panel_two.values())
        firsts = [[grid.row_bit(first, k) if k else first] for k in range(0, rows, 2)]
        _, blocks = run(inverse_two, *grid.both(record_two), *sums, record=True)
        earlier = panel_product(slots, list(panel_one.values()), firsts, [])
        total = grid.send(blocks, False)
        total = after(total, *earlier)
        seconds = [list(grid.both(grid.row_bit(total, k) if k else total)) for k in range(0, rows, 2)]
        second = seconds[0][0] + seconds[0][1]
        solved = grid.swap(lax.dynamic_slice_in_dim(jnp.stack([first, second]), r % 2 * width, width, 2))
        blocks = panel_product(slots, list(panel_two.values()), seconds, earlier)
        arrived = grid.pair_send(blocks, [solved])
        return solved, rhs - sum(arrived[1:], arrived[0])

    in_specs = (
        P(None, "row", "col"),
        P("row", "col"),
        P(None, "row", "col"),
        P(None, "row", "col"),
        P("row", "col"),
    )
    out_specs = (P(None, "row", "col"), P("row", "col"))
    return jax.shard_map(body, mesh=mesh, in_specs=in_specs, out_specs=out_specs, check_vma=False)
```

time: 489 us -> 215 us (0.44)
  waiting for transfers between devices: 367 us -> 114 us
  starting transfers between devices: 0.5 us -> 62.8 us
  blocking collectives: 54.2 us -> 0 us
  matrix products: 29.5 us -> 0 us
  Pallas kernels: 0 us -> 21.5 us
  between operations: 14.2 us -> 1.09 us
  local copies, waits for them, and re-layouts: 18.1 us -> 7.44 us
    all_gather x7 -> x0, waiting for transfers between devices: 281 us -> none  [the longest x1 78.8 us: body(): lax.all_gather(inv_diag[0], 'col', axis=1, tiled=True)]
    ppermute x0 -> x34, waiting for transfers between devices: none -> 114 us  [move(): return lax.ppermute(value, ('row', 'col'), pairs)]
    reduce_scatter x1 -> x0, waiting for transfers between devices: 85.1 us -> none  [body(): lax.psum_scatter(whole_term, 'col', scatter_dimension=1, tiled=True)]
    ppermute x0 -> x34, starting transfers between devices: none -> 62.8 us  [move(): return lax.ppermute(value, ('row', 'col'), pairs)]
    all_to_all x1 -> x0, blocking collectives: 54.2 us -> none  [body(): lax.all_to_all(stacked_full, 'col', split_axis=1, concat_axis=2, tiled=True)]
    dot_general x4 -> x0, matrix products: 29.5 us -> none  [the longest x3 19.9 us: product(): jnp.dot(left, right, precision=lax.Precision.HIGHEST, preferred_element_t...]
    pallas_call x0 -> x5, Pallas kernels: none -> 21.5 us  [call(): pl.pallas_call(kernel, out_shape=outs, in_specs=[SMEM] + [HBM] * len(oper...]
    another operation x1, local copies, waits for them, and re-layouts: 7.6 us -> 0.08 us  [body(): slots = jnp.stack(slots).astype(jnp.int32)]
  transfers between devices with their start and end apart: 8 -> 34, of which waited for: 8 -> 14; matrix products, arithmetic and copies ran while one was open for 4% -> 1% of each run, Pallas kernels for 0% -> 10%
where the time goes in v2:
time: 215 us; the launch traced here: 211 us
  waiting for transfers between devices  114 us (53%)
  starting transfers between devices  62.8 us (29%)
  Pallas kernels  21.5 us (10%)
  local copies, waits for them, and re-layouts  7.44 us (3%)
  other arithmetic  4.01 us (2%)
    ppermute x34, waiting for transfers between devices, move(): return lax.ppermute(value, ('row', 'col'), pairs)  114 us
    ppermute x34, starting transfers between devices, move(): return lax.ppermute(value, ('row', 'col'), pairs)  62.8 us
    pallas_call x5, Pallas kernels, call(): pl.pallas_call(kernel, out_shape=outs, in_specs=[SMEM] + [HBM] * len(oper...  21.5 us
    unnamed x35, local copies, waits for them, and re-layouts  5.12 us
  transfers between devices with their start and end apart: 34, of which 14 were waited for; matrix products, arithmetic and copies ran while one was open for 1% of the time, Pallas kernels for 10%

profile of v2, /device:TPU:2, one launch (start us, length us, event | category | flops | bytes accessed | tf_op | source)
XLA Modules:
  0.0 211.3 jit_solution(18254463735142467390)
XLA Ops:
  4.9 5.4 %collective-permute-start = (f32[512,128]{1,0:T(8,128)S(1)}, f32[512,128]{1,0:T(8,128)}, u32[]{:S(2)}, u32[]{:S(2)}) collective-permute-start(f32[512,128]{1,0:T(8,128)S(1)} %get-tuple-element.73), channel_id=1, source_target_pairs={{0,0},{1,1},{2,8},{3,9},{4,16},{5,17},{6,24},{7,25},{8,2},{9,3},{1... | collective-permute-start | bytes 786440 | tf_op jit(solution)/shard_map/ppermute | solution.py:201
  10.4 12.4 %collective-permute-done.refs_4_ = f32[512,128]{1,0:T(8,128)} collective-permute-done((f32[512,128]{1,0:T(8,128)S(1)}, f32[512,128]{1,0:T(8,128)}, u32[]{:S(2)}, u32[]{:S(2)}) %collective-permute-start) | collective-permute-done | bytes 262176 | tf_op jit(solution)/shard_map/ppermute | solution.py:201
  22.8 4.1 %collective-permute-start.7 = (f32[512,128]{1,0:T(8,128)}, f32[512,128]{1,0:T(8,128)S(1)}, u32[]{:S(2)}, u32[]{:S(2)}) collective-permute-start(f32[512,128]{1,0:T(8,128)} %get-tuple-element.36), channel_id=1, source_target_pairs={{0,0},{1,1},{2,8},{3,9},{4,16},{5,17},{6,24},{7,25},{8,2},{9,3},{1... | collective-permute-start | bytes 786440 | tf_op jit(solution)/shard_map/ppermute | solution.py:201
  28.6 12.2 %collective-permute-done.7.refs_4_ = f32[512,128]{1,0:T(8,128)S(1)} collective-permute-done((f32[512,128]{1,0:T(8,128)}, f32[512,128]{1,0:T(8,128)S(1)}, u32[]{:S(2)}, u32[]{:S(2)}) %collective-permute-start.7) | collective-permute-done | bytes 262176 | tf_op jit(solution)/shard_map/ppermute | solution.py:201
  40.8 3.8 %shard_map.68 = (f32[512,256]{1,0:T(8,128)}, f32[512,256]{1,0:T(8,128)S(1)}, f32[512,256]{1,0:T(8,128)S(1)}, f32[512,256]{1,0:T(8,128)S(1)}, f32[512,256]{1,0:T(8,128)S(1)}) custom-call(s32[4]{0:T(128)S(1)} %pad_add_fusion.where_ref, f32[512,256]{1,0:T(8,128)S(1)} %get-tuple-element.71.refs_0_, f32[512,256]{1,0:T(8,128)S(1)} %collective-permute-done.1.refs_1_, ...), custom_call_target="tpu_custom_call" | custom-call | flops 805306368 | bytes 5242880 | tf_op jit(solution)/shard_map/pallas_call | solution.py:36
  50.5 7.9 %collective-permute-done.10 = f32[512,256]{1,0:T(8,128)S(1)} collective-permute-done((f32[512,256]{1,0:T(8,128)S(1)}, f32[512,256]{1,0:T(8,128)S(1)}, u32[]{:S(2)}, u32[]{:S(2)}) %collective-permute-start.10) | collective-permute-done | bytes 524320 | tf_op jit(solution)/shard_map/ppermute | solution.py:201
  61.1 11.2 %collective-permute-done.8.refs_3_ = f32[512,256]{1,0:T(8,128)S(1)} collective-permute-done((f32[512,256]{1,0:T(8,128)S(1)}, f32[512,256]{1,0:T(8,128)S(1)}, u32[]{:S(2)}, u32[]{:S(2)}) %collective-permute-start.8) | collective-permute-done | bytes 524320 | tf_op jit(solution)/shard_map/ppermute | solution.py:201
  75.4 3.1 %shard_map.69 = (f32[512,256]{1,0:T(8,128)}, f32[512,256]{1,0:T(8,128)S(1)}, f32[512,256]{1,0:T(8,128)S(1)}, f32[512,256]{1,0:T(8,128)S(1)}, f32[512,256]{1,0:T(8,128)S(1)}) custom-call(s32[4]{0:T(128)S(1)} %pad_add_fusion.where_ref, f32[512,256]{1,0:T(8,128)S(1)} %copy-done.10, f32[512,256]{1,0:T(8,128)S(1)} %collective-permute-done.3.refs_1_, ...), custom_call_target="tpu_custom_call" | custom-call | flops 805306368 | bytes 5767168 | tf_op jit(solution)/shard_map/pallas_call | solution.py:36
  79.8 7.0 %collective-permute-start.19 = (f32[512,256]{1,0:T(8,128)S(1)}, f32[512,256]{1,0:T(8,128)S(1)}, u32[]{:S(2)}, u32[]{:S(2)}) collective-permute-start(f32[512,256]{1,0:T(8,128)S(1)} %get-tuple-element.50), channel_id=1, source_target_pairs={{0,4},{1,5},{4,0},{5,1},{10,14},{11,15},{14,10},{15,11},{16,20},{1... | collective-permute-start | bytes 1572872 | tf_op jit(solution)/shard_map/ppermute | solution.py:201
  94.7 3.0 %collective-permute-start.16 = (f32[512,256]{1,0:T(8,128)S(1)}, f32[512,256]{1,0:T(8,128)S(1)}, u32[]{:S(2)}, u32[]{:S(2)}) collective-permute-start(f32[512,256]{1,0:T(8,128)S(1)} %collective-permute-done.14.refs_1_), channel_id=1, source_target_pairs={{0,16},{1,17},{2,18},{3,19},{4,20},{5,21},{6,22},{7,23},{8,24},{9,... | collective-permute-start | bytes 1572872 | tf_op jit(solution)/shard_map/ppermute | solution.py:201
  97.7 4.7 %collective-permute-done.19 = f32[512,256]{1,0:T(8,128)S(1)} collective-permute-done((f32[512,256]{1,0:T(8,128)S(1)}, f32[512,256]{1,0:T(8,128)S(1)}, u32[]{:S(2)}, u32[]{:S(2)}) %collective-permute-start.19) | collective-permute-done | bytes 524320 | tf_op jit(solution)/shard_map/ppermute | solution.py:201
  102.4 3.4 %collective-permute-done.20 = f32[512,256]{1,0:T(8,128)S(1)} collective-permute-done((f32[512,256]{1,0:T(8,128)S(1)}, f32[512,256]{1,0:T(8,128)S(1)}, u32[]{:S(2)}, u32[]{:S(2)}) %collective-permute-start.20) | collective-permute-done | bytes 524320 | tf_op jit(solution)/shard_map/ppermute | solution.py:201
  106.5 3.1 %collective-permute-done.21.refs_1_ = f32[1024,256]{1,0:T(8,128)S(1)} collective-permute-done((f32[1024,256]{1,0:T(8,128)S(1)}, f32[1024,256]{1,0:T(8,128)S(1)}, u32[]{:S(2)}, u32[]{:S(2)}) %collective-permute-start.21) | collective-permute-done | bytes 1048608 | tf_op jit(solution)/shard_map/ppermute | solution.py:201
  112.0 3.9 %collective-permute-done.16.refs_3_ = f32[512,256]{1,0:T(8,128)S(1)} collective-permute-done((f32[512,256]{1,0:T(8,128)S(1)}, f32[512,256]{1,0:T(8,128)S(1)}, u32[]{:S(2)}, u32[]{:S(2)}) %collective-permute-start.16) | collective-permute-done | bytes 524320 | tf_op jit(solution)/shard_map/ppermute | solution.py:201
  115.9 4.2 %shard_map.70 = (f32[512,256]{1,0:T(8,128)}, f32[512,256]{1,0:T(8,128)S(1)}, f32[512,256]{1,0:T(8,128)}, f32[512,256]{1,0:T(8,128)}, f32[512,256]{1,0:T(8,128)}) custom-call(s32[4]{0:T(128)S(1)} %pad_add_fusion.where_ref, f32[512,256]{1,0:T(8,128)S(1)} %get-tuple-element.47.refs_0_, f32[512,256]{1,0:T(8,128)S(1)} %collective-permute-done.14.refs_1_, ...), custom_call_target="tpu_custom_call" | custom-call | flops 805306368 | bytes 6291456 | tf_op jit(solution)/shard_map/pallas_call | solution.py:36
  120.8 7.9 %collective-permute-start.24 = (f32[512,256]{1,0:T(8,128)}, f32[512,256]{1,0:T(8,128)}, u32[]{:S(2)}, u32[]{:S(2)}) collective-permute-start(f32[512,256]{1,0:T(8,128)} %get-tuple-element.56), channel_id=1, source_target_pairs={{0,4},{1,5},{10,14},{11,15},{16,20},{17,21},{26,30},{27,31}} | collective-permute-start | bytes 1572872 | tf_op jit(solution)/shard_map/ppermute | solution.py:201
  132.7 5.1 %shard_map.71 = (f32[1024,128]{1,0:T(8,128)S(1)}, f32[1024,128]{1,0:T(8,128)S(1)}, f32[1024,128]{1,0:T(8,128)S(1)}, f32[1024,128]{1,0:T(8,128)S(1)}) custom-call(s32[6]{0:T(128)S(1)} %stack.51.where_ref, f32[1024,256]{1,0:T(8,128)S(1)} %copy-done.1, f32[1024,256]{1,0:T(8,128)S(1)} %copy-done.12, f32[512,256]{1,0:T(8,128)} %get-tuple-element.46.refs_2_, ...), custom_call_target="tpu_custom_call" | custom-call | flops 1610612736 | bytes 5242880 | tf_op jit(solution)/shard_map/pallas_call | solution.py:36
  140.2 2.5 %collective-permute-start.29 = (f32[512,256]{1,0:T(8,128)S(1)}, f32[512,256]{1,0:T(8,128)}, u32[]{:S(2)}, u32[]{:S(2)}) collective-permute-start(f32[512,256]{1,0:T(8,128)S(1)} %add_add_fusion.refs_2_), channel_id=1, source_target_pairs={{0,16},{1,17},{2,18},{3,19},{4,20},{5,21},{6,22},{7,23},{8,24},{9,... | collective-permute-start | bytes 1572872 | tf_op jit(solution)/shard_map/ppermute | solution.py:201
  142.8 7.3 %collective-permute-done.29.refs_4_ = f32[512,256]{1,0:T(8,128)} collective-permute-done((f32[512,256]{1,0:T(8,128)S(1)}, f32[512,256]{1,0:T(8,128)}, u32[]{:S(2)}, u32[]{:S(2)}) %collective-permute-start.29) | collective-permute-done | bytes 524320 | tf_op jit(solution)/shard_map/ppermute | solution.py:201
  151.4 7.4 %collective-permute-start.28 = (f32[2,512,128]{2,1,0:T(8,128)S(1)}, f32[2,512,128]{2,1,0:T(8,128)S(1)}, u32[]{:S(2)}, u32[]{:S(2)}) collective-permute-start(f32[2,512,128]{2,1,0:T(8,128)S(1)} %fusion), channel_id=1, source_target_pairs={{0,0},{1,1},{2,8},{3,9},{4,16},{5,17},{6,24},{7,25},{8,2},{9,3},{1... | collective-permute-start | bytes 1572872 | tf_op jit(solution)/shard_map/ppermute | solution.py:201
  158.8 5.4 %shard_map.72 = (f32[1024,128]{1,0:T(8,128)S(1)}, f32[1024,128]{1,0:T(8,128)S(1)}, f32[1024,128]{1,0:T(8,128)S(1)}, f32[1024,128]{1,0:T(8,128)S(1)}) custom-call(s32[6]{0:T(128)S(1)} %stack.51.where_ref, f32[1024,256]{1,0:T(8,128)S(1)} %get-tuple-element.52.refs_0_, f32[1024,256]{1,0:T(8,128)S(1)} %collective-permute-done.21.refs_1_, ...), custom_call_target="tpu_custom_call" | custom-call | flops 1610612736 | bytes 8388608 | tf_op jit(solution)/shard_map/pallas_call | solution.py:36
  164.9 17.3 %collective-permute-done.28 = f32[2,512,128]{2,1,0:T(8,128)S(1)} collective-permute-done((f32[2,512,128]{2,1,0:T(8,128)S(1)}, f32[2,512,128]{2,1,0:T(8,128)S(1)}, u32[]{:S(2)}, u32[]{:S(2)}) %collective-permute-start.28) | collective-permute-done | bytes 524320 | tf_op jit(solution)/shard_map/ppermute | solution.py:201
  183.0 9.9 %collective-permute-done.31 = f32[1024,128]{1,0:T(8,128)S(1)} collective-permute-done((f32[1024,128]{1,0:T(8,128)S(1)}, f32[1024,128]{1,0:T(8,128)S(1)}, u32[]{:S(2)}, u32[]{:S(2)}) %collective-permute-start.31) | collective-permute-done | bytes 524320 | tf_op jit(solution)/shard_map/ppermute | solution.py:201
  192.9 16.7 %collective-permute-done.33 = f32[1024,128]{1,0:T(8,128)S(1)} collective-permute-done((f32[1024,128]{1,0:T(8,128)S(1)}, f32[1024,128]{1,0:T(8,128)S(1)}, u32[]{:S(2)}, u32[]{:S(2)}) %collective-permute-start.33) | collective-permute-done | bytes 524320 | tf_op jit(solution)/shard_map/ppermute | solution.py:201
  (96 shorter events, 41.1 us)
Async XLA Ops:
  2.0 20.8 %collective-permute-start.2 = (f32[512,256]{1,0:T(8,128)S(1)}, f32[512,256]{1,0:T(8,128)S(1)}, u32[]{:S(2)}, u32[]{:S(2)}) collective-permute-start(f32[512,256]{1,0:T(8,128)S(1)} %get-tuple-element.71.refs_0_), channel_id=1, source_target_pairs={{0,16},{1,17},{2,18},{3,19},{4,20},{5,21},{6,22},{7,23},{8,24},{9,... | collective-permute-start | bytes 1572872 | tf_op jit(solution)/shard_map/ppermute | solution.py:201
  2.1 20.7 %collective-permute-start.1 = (f32[512,256]{1,0:T(8,128)S(1)}, f32[512,256]{1,0:T(8,128)S(1)}, u32[]{:S(2)}, u32[]{:S(2)}) collective-permute-start(f32[512,256]{1,0:T(8,128)S(1)} %get-tuple-element.71.refs_0_), channel_id=1, source_target_pairs={{0,1},{1,0},{2,3},{3,2},{4,5},{5,4},{6,7},{7,6},{8,9},{9,8},{10,11... | collective-permute-start | bytes 1572872 | tf_op jit(solution)/shard_map/ppermute | solution.py:201
  4.9 17.9 %collective-permute-start = (f32[512,128]{1,0:T(8,128)S(1)}, f32[512,128]{1,0:T(8,128)}, u32[]{:S(2)}, u32[]{:S(2)}) collective-permute-start(f32[512,128]{1,0:T(8,128)S(1)} %get-tuple-element.73), channel_id=1, source_target_pairs={{0,0},{1,1},{2,8},{3,9},{4,16},{5,17},{6,24},{7,25},{8,2},{9,3},{1... | collective-permute-start | bytes 786440 | tf_op jit(solution)/shard_map/ppermute | solution.py:201
  10.3 30.5 %collective-permute-start.5 = (f32[512,256]{1,0:T(8,128)S(1)}, f32[512,256]{1,0:T(8,128)S(1)}, u32[]{:S(2)}, u32[]{:S(2)}) collective-permute-start(f32[512,256]{1,0:T(8,128)S(1)} %get-tuple-element.71.refs_0_), channel_id=1, source_target_pairs={{0,17},{1,16},{2,19},{3,18},{4,21},{5,20},{6,23},{7,22},{8,25},{9,... | collective-permute-start | bytes 1572872 | tf_op jit(solution)/shard_map/ppermute | solution.py:201
  22.8 18.0 %collective-permute-start.7 = (f32[512,128]{1,0:T(8,128)}, f32[512,128]{1,0:T(8,128)S(1)}, u32[]{:S(2)}, u32[]{:S(2)}) collective-permute-start(f32[512,128]{1,0:T(8,128)} %get-tuple-element.36), channel_id=1, source_target_pairs={{0,0},{1,1},{2,8},{3,9},{4,16},{5,17},{6,24},{7,25},{8,2},{9,3},{1... | collective-permute-start | bytes 786440 | tf_op jit(solution)/shard_map/ppermute | solution.py:201
  27.1 21.3 %collective-permute-start.3 = (f32[512,256]{1,0:T(8,128)S(1)}, f32[512,256]{1,0:T(8,128)S(1)}, u32[]{:S(2)}, u32[]{:S(2)}) collective-permute-start(f32[512,256]{1,0:T(8,128)S(1)} %copy-done.10), channel_id=1, source_target_pairs={{0,1},{1,0},{2,3},{3,2},{4,5},{5,4},{6,7},{7,6},{8,9},{9,8},{10,11... | collective-permute-start | bytes 1572872 | tf_op jit(solution)/shard_map/ppermute | solution.py:201
  45.4 13.0 %collective-permute-start.10 = (f32[512,256]{1,0:T(8,128)S(1)}, f32[512,256]{1,0:T(8,128)S(1)}, u32[]{:S(2)}, u32[]{:S(2)}) collective-permute-start(f32[512,256]{1,0:T(8,128)S(1)} %get-tuple-element.42), channel_id=1, source_target_pairs={{0,4},{1,5},{10,14},{11,15},{16,20},{17,21},{26,30},{27,31}} | collective-permute-start | bytes 1572872 | tf_op jit(solution)/shard_map/ppermute | solution.py:201
  47.6 26.9 %collective-permute-start.12 = (f32[1024,256]{1,0:T(8,128)S(1)}, f32[1024,256]{1,0:T(8,128)S(1)}, u32[]{:S(2)}, u32[]{:S(2)}) collective-permute-start(f32[1024,256]{1,0:T(8,128)S(1)} %get-tuple-element.44.refs_0_), channel_id=1, source_target_pairs={{0,1},{1,0},{2,3},{3,2},{4,5},{5,4},{6,7},{7,6},{8,9},{9,8},{10,11... | collective-permute-start | bytes 3145736 | tf_op jit(solution)/shard_map/ppermute | solution.py:201
  48.4 12.7 %collective-permute-start.4 = (f32[512,256]{1,0:T(8,128)S(1)}, f32[512,256]{1,0:T(8,128)S(1)}, u32[]{:S(2)}, u32[]{:S(2)}) collective-permute-start(f32[512,256]{1,0:T(8,128)S(1)} %copy-done.10), channel_id=1, source_target_pairs={{0,16},{1,17},{2,18},{3,19},{4,20},{5,21},{6,22},{7,23},{8,24},{9,... | collective-permute-start | bytes 1572872 | tf_op jit(solution)/shard_map/ppermute | solution.py:201
  50.4 21.9 %collective-permute-start.8 = (f32[512,256]{1,0:T(8,128)S(1)}, f32[512,256]{1,0:T(8,128)S(1)}, u32[]{:S(2)}, u32[]{:S(2)}) collective-permute-start(f32[512,256]{1,0:T(8,128)S(1)} %collective-permute-done.3.refs_1_), channel_id=1, source_target_pairs={{0,16},{1,17},{2,18},{3,19},{4,20},{5,21},{6,22},{7,23},{8,24},{9,... | collective-permute-start | bytes 1572872 | tf_op jit(solution)/shard_map/ppermute | solution.py:201
  58.5 16.9 %collective-permute-start.13 = (f32[512,256]{1,0:T(8,128)S(1)}, f32[512,256]{1,0:T(8,128)S(1)}, u32[]{:S(2)}, u32[]{:S(2)}) collective-permute-start(f32[512,256]{1,0:T(8,128)S(1)} %add_add_fusion.2.refs_4_), channel_id=1, source_target_pairs={{0,8},{1,9},{2,10},{3,11},{4,12},{5,13},{6,14},{7,15},{8,0},{9,1},... | collective-permute-start | bytes 1572872 | tf_op jit(solution)/shard_map/ppermute | solution.py:201
  72.3 17.9 %collective-permute-start.14 = (f32[512,256]{1,0:T(8,128)S(1)}, f32[512,256]{1,0:T(8,128)S(1)}, u32[]{:S(2)}, u32[]{:S(2)}) collective-permute-start(f32[512,256]{1,0:T(8,128)S(1)} %get-tuple-element.47.refs_0_), channel_id=1, source_target_pairs={{0,1},{1,0},{2,3},{3,2},{4,5},{5,4},{6,7},{7,6},{8,9},{9,8},{10,11... | collective-permute-start | bytes 1572872 | tf_op jit(solution)/shard_map/ppermute | solution.py:201
  78.5 16.2 %collective-permute-start.18 = (f32[512,256]{1,0:T(8,128)S(1)}, f32[512,256]{1,0:T(8,128)S(1)}, u32[]{:S(2)}, u32[]{:S(2)}) collective-permute-start(f32[512,256]{1,0:T(8,128)S(1)} %get-tuple-element.49), channel_id=1, source_target_pairs={{2,4},{3,5},{6,0},{7,1},{8,14},{9,15},{12,10},{13,11},{18,20},{19,... | collective-permute-start | bytes 1572872 | tf_op jit(solution)/shard_map/ppermute | solution.py:201
  79.8 22.6 %collective-permute-start.19 = (f32[512,256]{1,0:T(8,128)S(1)}, f32[512,256]{1,0:T(8,128)S(1)}, u32[]{:S(2)}, u32[]{:S(2)}) collective-permute-start(f32[512,256]{1,0:T(8,128)S(1)} %get-tuple-element.50), channel_id=1, source_target_pairs={{0,4},{1,5},{4,0},{5,1},{10,14},{11,15},{14,10},{15,11},{16,20},{1... | collective-permute-start | bytes 1572872 | tf_op jit(solution)/shard_map/ppermute | solution.py:201
  86.8 19.0 %collective-permute-start.20 = (f32[512,256]{1,0:T(8,128)S(1)}, f32[512,256]{1,0:T(8,128)S(1)}, u32[]{:S(2)}, u32[]{:S(2)}) collective-permute-start(f32[512,256]{1,0:T(8,128)S(1)} %get-tuple-element.51), channel_id=1, source_target_pairs={{2,0},{3,1},{6,4},{7,5},{8,10},{9,11},{12,14},{13,15},{18,16},{19,... | collective-permute-start | bytes 1572872 | tf_op jit(solution)/shard_map/ppermute | solution.py:201
  88.1 21.5 %collective-permute-start.21 = (f32[1024,256]{1,0:T(8,128)S(1)}, f32[1024,256]{1,0:T(8,128)S(1)}, u32[]{:S(2)}, u32[]{:S(2)}) collective-permute-start(f32[1024,256]{1,0:T(8,128)S(1)} %get-tuple-element.52.refs_0_), channel_id=1, source_target_pairs={{0,1},{1,0},{2,3},{3,2},{4,5},{5,4},{6,7},{7,6},{8,9},{9,8},{10,11... | collective-permute-start | bytes 3145736 | tf_op jit(solution)/shard_map/ppermute | solution.py:201
  90.2 21.8 %collective-permute-start.15 = (f32[512,256]{1,0:T(8,128)S(1)}, f32[512,256]{1,0:T(8,128)S(1)}, u32[]{:S(2)}, u32[]{:S(2)}) collective-permute-start(f32[512,256]{1,0:T(8,128)S(1)} %get-tuple-element.47.refs_0_), channel_id=1, source_target_pairs={{0,16},{1,17},{2,18},{3,19},{4,20},{5,21},{6,22},{7,23},{8,24},{9,... | collective-permute-start | bytes 1572872 | tf_op jit(solution)/shard_map/ppermute | solution.py:201
  94.7 21.2 %collective-permute-start.16 = (f32[512,256]{1,0:T(8,128)S(1)}, f32[512,256]{1,0:T(8,128)S(1)}, u32[]{:S(2)}, u32[]{:S(2)}) collective-permute-start(f32[512,256]{1,0:T(8,128)S(1)} %collective-permute-done.14.refs_1_), channel_id=1, source_target_pairs={{0,16},{1,17},{2,18},{3,19},{4,20},{5,21},{6,22},{7,23},{8,24},{9,... | collective-permute-start | bytes 1572872 | tf_op jit(solution)/shard_map/ppermute | solution.py:201
  109.7 20.6 %collective-permute-start.26 = (f32[512,256]{1,0:T(8,128)}, f32[512,256]{1,0:T(8,128)}, u32[]{:S(2)}, u32[]{:S(2)}) collective-permute-start(f32[512,256]{1,0:T(8,128)} %get-tuple-element.46.refs_2_), channel_id=1, source_target_pairs={{0,16},{1,17},{2,18},{3,19},{4,20},{5,21},{6,22},{7,23},{8,24},{9,... | collective-permute-start | bytes 1572872 | tf_op jit(solution)/shard_map/ppermute | solution.py:201
  120.1 17.7 %collective-permute-start.23 = (f32[512,256]{1,0:T(8,128)}, f32[512,256]{1,0:T(8,128)S(1)}, u32[]{:S(2)}, u32[]{:S(2)}) collective-permute-start(f32[512,256]{1,0:T(8,128)} %get-tuple-element.55), channel_id=1, source_target_pairs={{2,4},{3,5},{8,14},{9,15},{18,20},{19,21},{24,30},{25,31}} | collective-permute-start | bytes 1572872 | tf_op jit(solution)/shard_map/ppermute | solution.py:201
  120.8 17.1 %collective-permute-start.24 = (f32[512,256]{1,0:T(8,128)}, f32[512,256]{1,0:T(8,128)}, u32[]{:S(2)}, u32[]{:S(2)}) collective-permute-start(f32[512,256]{1,0:T(8,128)} %get-tuple-element.56), channel_id=1, source_target_pairs={{0,4},{1,5},{10,14},{11,15},{16,20},{17,21},{26,30},{27,31}} | collective-permute-start | bytes 1572872 | tf_op jit(solution)/shard_map/ppermute | solution.py:201
  151.4 30.8 %collective-permute-start.28 = (f32[2,512,128]{2,1,0:T(8,128)S(1)}, f32[2,512,128]{2,1,0:T(8,128)S(1)}, u32[]{:S(2)}, u32[]{:S(2)}) collective-permute-start(f32[2,512,128]{2,1,0:T(8,128)S(1)} %fusion), channel_id=1, source_target_pairs={{0,0},{1,1},{2,8},{3,9},{4,16},{5,17},{6,24},{7,25},{8,2},{9,3},{1... | collective-permute-start | bytes 1572872 | tf_op jit(solution)/shard_map/ppermute | solution.py:201
  164.2 18.6 %collective-permute-start.32 = (f32[1024,128]{1,0:T(8,128)S(1)}, f32[1024,128]{1,0:T(8,128)S(1)}, u32[]{:S(2)}, u32[]{:S(2)}) collective-permute-start(f32[1024,128]{1,0:T(8,128)S(1)} %get-tuple-element.67), channel_id=1, source_target_pairs={{0,2},{1,3},{2,0},{3,1},{4,6},{5,7},{6,4},{7,5},{8,10},{9,11},{10,... | collective-permute-start | bytes 1572872 | tf_op jit(solution)/shard_map/ppermute | solution.py:201
  182.9 26.7 %collective-permute-start.33 = (f32[1024,128]{1,0:T(8,128)S(1)}, f32[1024,128]{1,0:T(8,128)S(1)}, u32[]{:S(2)}, u32[]{:S(2)}) collective-permute-start(f32[1024,128]{1,0:T(8,128)S(1)} %add.101), channel_id=1, source_target_pairs={{0,4},{1,5},{2,6},{3,7},{4,0},{5,1},{6,2},{7,3},{8,12},{9,13},{10,... | collective-permute-start | bytes 1572872 | tf_op jit(solution)/shard_map/ppermute | solution.py:201
  (27 other events, 306.0 us)

commit v3 on v2

--- a/solution.py
+++ b/solution.py
@@ -63,7 +63,10 @@
             lanes = pl.ds(pl.multiple_of(side * width, width), width)
             arrivals.append(start(given[i], vector_ref.at[:, lanes], given_sems.at[i]))
         arrivals += [start(ref, given_ref.at[i], given_sems.at[2 + i]) for i, ref in enumerate(given[2:])]
-    copies = [start(pieces[i], matrix_ref.at[place], sems.at[i]) for i, place in enumerate(places)]
+    copies = []
+    for i, (k, o, row) in enumerate(places):
+        part = matrix_ref.at[k, o, pl.ds(row, pieces[i].shape[0])]
+        copies.append(start(pieces[i], part, sems.at[i]))
     offset = where_ref[shards]
     for copy in arrivals:
         copy.wait()
@@ -93,8 +96,8 @@
 
 
 def stage(blocks, where, matrix, *given, record):
-    shards = len(matrix) * 2 // blocks
-    rows, depth = matrix[0, 0].shape
+    rows, depth = matrix[0, 0, 0].shape
+    shards = 1 + max(o for _, o, _ in matrix)
     width = given[0].shape[1] * (2 if record else 1)
     outs = [shape(F32, shards * depth, width)] + [shape(F32, rows, width)] * blocks
     scratch = [
@@ -111,10 +114,10 @@
     return found[0], list(found[1:])
 
 
-def panel_kernel(shards, blocks, parts, where_ref, *refs):
+def panel_kernel(shards, blocks, parts, wanted, where_ref, *refs):
     panels, pairs = refs[:shards], refs[shards:shards + blocks // 2 * parts]
-    earlier = refs[shards + len(pairs):-blocks - 9]
-    outs = refs[-blocks - 9:-9]
+    earlier = refs[shards + len(pairs):-len(wanted) - 9]
+    outs = refs[-len(wanted) - 9:-9]
     panel_ref, pair_ref, p_high, p_low, v_high, v_low, total_ref, sems, out_sems = refs[-9:]
     width, depth = total_ref.shape[2], panel_ref.shape[2]
     copies = [start(ref, pair_ref.at[i], sems.at[i]) for i, ref in enumerate(pairs)]
@@ -137,26 +140,26 @@
         copy.wait()
         p_high[:, o * depth:(o + 1) * depth], p_low[:, o * depth:(o + 1) * depth] = split(panel_ref[o])
     leaving = []
-    for d in reversed(range(blocks)):
+    for i, d in enumerate(wanted):
         k = where_ref[d]
         high, low = v_high[k], v_low[k]
         both = dot(p_high[...], jnp.concatenate([high, low], 1))
         total = both[:, :width] + (both[:, width:] + dot(p_low[...], high))
         if earlier:
-            loads[d].wait()
-            total = total_ref[d] + total
-        total_ref[d] = total
-        leaving.append(start(total_ref.at[d], outs[d], out_sems.at[d]))
+            loads[i].wait()
+            total = total_ref[i] + total
+        total_ref[i] = total
+        leaving.append(start(total_ref.at[i], outs[i], out_sems.at[i]))
     for copy in leaving:
         copy.wait()
 
 
-def panel_product(where, panel, pairs, earlier):
+def panel_product(where, panel, pairs, earlier, wanted):
     shards, blocks, parts = len(panel), len(pairs) * 2, len(pairs[0])
     rows, depth = panel[0].shape
     width = pairs[0][0].shape[1]
     given = [part for pair in pairs for part in pair]
-    outs = [shape(F32, rows, width // 2)] * blocks
+    outs = [shape(F32, rows, width // 2)] * len(wanted)
     scratch = [
         pltpu.VMEM((shards, rows, depth), F32),
         pltpu.VMEM((len(given), shards * depth, width), F32),
@@ -164,17 +167,23 @@
         pltpu.VMEM((rows, shards * depth), BF16),
         pltpu.VMEM((blocks, shards * depth, width // 2), BF16),
         pltpu.VMEM((blocks, shards * depth, width // 2), BF16),
-        pltpu.VMEM((blocks, rows, width // 2), F32),
+        pltpu.VMEM((len(wanted), rows, width // 2), F32),
         pltpu.SemaphoreType.DMA((len(given) + shards,)),
-        pltpu.SemaphoreType.DMA((blocks,)),
+        pltpu.SemaphoreType.DMA((len(wanted),)),
     ]
-    kernel = functools.partial(panel_kernel, shards, blocks, parts)
-    flops = 3 * blocks * rows * shards * depth * width
-    return list(call(kernel, outs, scratch, flops, where, *panel, *given, *earlier))
+    kernel = functools.partial(panel_kernel, shards, blocks, parts, wanted)
+    flops = 6 * len(wanted) * rows * shards * depth * width // 2
+    before = [earlier[d] for d in wanted] if earlier else []
+    found = call(kernel, outs, scratch, flops, where, *panel, *given, *before)
+    return dict(zip(wanted, found, strict=True))
 
 
 def after(value, *earlier):
     return lax.optimization_barrier((value, *earlier))[0]
+
+
+def whole(pieces):
+    return {(*place, 0): piece for place, piece in pieces.items()}
 
 
 def together(*values):
@@ -215,8 +224,10 @@
     def gather_row(self, pieces):
         found = dict(pieces)
         for k in range(2, self.rows, 2):
+            held = []
             for (_, o), piece in pieces.items():
-                found[k // 2, o] = self.row_bit(piece, k)
+                found[k // 2, o] = self.row_bit(after(piece, *held), k)
+                held = [found[k // 2, 0]]
         return found
 
     def send(self, blocks, two_way):
@@ -232,6 +243,24 @@
             total = total + block
         return total
 
+    def merged_send(self, blocks, two_way):
+        def target(d):
+            def to(r, a, b):
+                odd = (r ^ a) % 2
+                plane = a ^ d ^ odd
+                if not two_way and plane < a:
+                    return None
+                return (r, plane, b) if odd else (r ^ 1, plane, b)
+
+            return to
+
+        got = [self.move(blocks[d], target(d)) for d in reversed(range(2, self.rows, 2))]
+        got.append(self.move(
+            blocks[1],
+            lambda r, a, b: (r, a ^ 1, b) if (r ^ a) % 2 == 1 and (two_way or (a ^ 1) > a) else None,
+        ))
+        return sum(got, blocks[0])
+
     def both(self, total):
         return total, self.row_bit(total, 1)
 
@@ -264,41 +293,52 @@
         inverse_one = grid.gather_b(inv_diag[0])
         far = {(k // 2, 0): grid.row_bit(inv_diag[0], k) for k in range(2, rows, 2)}
         early = [record_one, *inverse_one.values(), *far.values()]
+        half = inv_diag.shape[1] // 2
+        inverse_one = {(*place, 0): piece for place, piece in (inverse_one | far).items()}
         for k in range(2, rows, 2):
             for o in range(1, shards):
-                far[k // 2, o] = grid.move(inv_diag[0], lambda r, a, b: (r ^ k, a, b ^ o))
-        inverse_one |= far
+                one, two = together(inverse_one[0, o, 0][:half], inverse_one[k // 2, 0, 0][half:])
+                early += [one, two]
+                inverse_one[k // 2, o, 0] = grid.row_bit(one, k)
+                inverse_one[k // 2, o, half] = grid.b_bit(two, o)
         held = after(coupling, *early)
         coupled = grid.gather_b(held)
         coupled |= {(k // 2, 0): grid.row_bit(held, k) for k in range(2, rows, 2)}
         record_two = grid.swap(after(top_rhs[1], *early))
         first_in = grid.both(record_one)
-        first_in = together(*first_in, record_two)[:2]
         _, blocks = run(inverse_one, *first_in, record=True)
+        blocks = together(*blocks, record_two)[:rows]
 
         for k in range(2, rows, 2):
             for o in range(1, shards):
-                coupled[k // 2, o] = grid.row_bit(after(coupled[0, o], blocks[0]), k)
+                coupled[k // 2, o] = grid.row_bit(after(coupled[0, o], coupled[k // 2, 0]), k)
         panel_one = grid.gather_b(after(panel[0], *inverse_one.values()))
         held = after(inv_diag[1], *coupled.values())
-        sums = list(grid.both(grid.send(blocks, False)))
-        sums[0] = after(sums[0], *panel_one.values())
-        first, blocks = run(coupled, *sums, record=False)
+        sums = list(grid.both(grid.merged_send(blocks, False)))
+        first, blocks = run(whole(coupled), *sums, record=False)
         inverse_two = grid.gather_row(grid.gather_b(held))
         panel_two = grid.gather_b(after(panel[1], *panel_one.values()))
         sums = list(grid.both(grid.send(blocks, True)))
-        sums[0] = after(sums[0], *panel_two.values())
+        sums[0] = after(sums[0], *panel_one.values())
         firsts = [[grid.row_bit(first, k) if k else first] for k in range(0, rows, 2)]
-        _, blocks = run(inverse_two, *grid.both(record_two), *sums, record=True)
-        earlier = panel_product(slots, list(panel_one.values()), firsts, [])
+        _, blocks = run(whole(inverse_two), *grid.both(record_two), *sums, record=True)
+        earlier = panel_product(slots, list(panel_one.values()), firsts, {}, list(range(rows)))
+        blocks[1] = after(blocks[1], *panel_two.values())
         total = grid.send(blocks, False)
-        total = after(total, *earlier)
-        seconds = [list(grid.both(grid.row_bit(total, k) if k else total)) for k in range(0, rows, 2)]
-        second = seconds[0][0] + seconds[0][1]
-        solved = grid.swap(lax.dynamic_slice_in_dim(jnp.stack([first, second]), r % 2 * width, width, 2))
-        blocks = panel_product(slots, list(panel_two.values()), seconds, earlier)
-        arrived = grid.pair_send(blocks, [solved])
-        return solved, rhs - sum(arrived[1:], arrived[0])
+        total = after(total, *earlier.values())
+        mine = functools.partial(lax.dynamic_slice_in_dim, start_index=r % 2 * width, slice_size=width, axis=1)
+        solved_one = grid.swap(after(mine(first), total))
+        far = [after(grid.row_bit(total, k), solved_one) for k in range(2, rows, 2)]
+        seconds = [list(grid.both(value)) for value in [total, *far]]
+        solved_two = grid.swap(mine(seconds[0][0] + seconds[0][1]))
+        sent = list(range(3, rows, 2))
+        ready = panel_product(slots, list(panel_two.values()), seconds, earlier, sent)
+        held = list(panel_two.values())
+        held[0] = after(held[0], *ready.values())
+        rest = [d for d in reversed(range(rows)) if d not in sent]
+        blocks = ready | panel_product(slots, held, seconds, earlier, rest)
+        arrived = grid.pair_send(blocks, [solved_two])
+        return jnp.stack([solved_one, solved_two]), rhs - sum(arrived[1:], arrived[0])
 
     in_specs = (
         P(None, "row", "col"),

time: 215 us -> 207 us (0.963); the launches traced: 211 us -> 205 us
  waiting for transfers between devices: 114 us -> 98.3 us
  starting transfers between devices: 62.8 us -> 70.8 us
  local copies, waits for them, and re-layouts: 7.44 us -> 9.9 us
    ppermute x34 -> x35, waiting for transfers between devices: 114 us -> 98.3 us  [move(): return lax.ppermute(value, ('row', 'col'), pairs)]
    ppermute x34 -> x35, starting transfers between devices: 62.8 us -> 70.8 us  [move(): return lax.ppermute(value, ('row', 'col'), pairs)]
    pallas_call x5 -> x6, Pallas kernels: 21.5 us -> 21.9 us  [call(): pl.pallas_call(kernel, out_shape=outs, in_specs=[SMEM] + [HBM] * len(oper...]
    unnamed x35 -> x40, local copies, waits for them, and re-layouts: 5.12 us -> 5.17 us
  transfers between devices with their start and end apart: 34 -> 35, of which waited for: 14 -> 16; matrix products, arithmetic and copies ran while one was open for 1% -> 2% of each run, Pallas kernels for 10% -> 10%
where the time goes in v3:
time: 207 us; the launch traced here: 205 us
  waiting for transfers between devices  98.3 us (47%)
  starting transfers between devices  70.8 us (34%)
  Pallas kernels  21.9 us (11%)
  local copies, waits for them, and re-layouts  9.9 us (5%)
  other arithmetic  3.49 us (2%)
    ppermute x35, waiting for transfers between devices, move(): return lax.ppermute(value, ('row', 'col'), pairs)  98.3 us
    ppermute x35, starting transfers between devices, move(): return lax.ppermute(value, ('row', 'col'), pairs)  70.8 us
    pallas_call x6, Pallas kernels, call(): pl.pallas_call(kernel, out_shape=outs, in_specs=[SMEM] + [HBM] * len(oper...  21.9 us
    unnamed x40, local copies, waits for them, and re-layouts  5.17 us
  transfers between devices with their start and end apart: 35, of which 16 were waited for; matrix products, arithmetic and copies ran while one was open for 2% of the time, Pallas kernels for 10%

profile of v3, /device:TPU:2, one launch (start us, length us, event | category | flops | bytes accessed | tf_op | source)
XLA Modules:
  0.0 205.5 jit_solution(16487078211393586682)
XLA Ops:
  4.9 5.4 %collective-permute-start = (f32[512,128]{1,0:T(8,128)S(1)}, f32[512,128]{1,0:T(8,128)S(1)}, u32[]{:S(2)}, u32[]{:S(2)}) collective-permute-start(f32[512,128]{1,0:T(8,128)S(1)} %get-tuple-element.83), channel_id=1, source_target_pairs={{0,0},{1,1},{2,8},{3,9},{4,16},{5,17},{6,24},{7,25},{8,2},{9,3},{1... | collective-permute-start | bytes 786440 | tf_op jit(solution)/shard_map/ppermute | solution.py:210
  10.3 12.4 %collective-permute-done.refs_5_ = f32[512,128]{1,0:T(8,128)S(1)} collective-permute-done((f32[512,128]{1,0:T(8,128)S(1)}, f32[512,128]{1,0:T(8,128)S(1)}, u32[]{:S(2)}, u32[]{:S(2)}) %collective-permute-start) | collective-permute-done | bytes 262176 | tf_op jit(solution)/shard_map/ppermute | solution.py:210
  24.7 3.6 %collective-permute-start.9 = (f32[512,128]{1,0:T(8,128)}, f32[512,128]{1,0:T(8,128)S(1)}, u32[]{:S(2)}, u32[]{:S(2)}) collective-permute-start(f32[512,128]{1,0:T(8,128)} %get-tuple-element.47), channel_id=1, source_target_pairs={{0,0},{1,1},{2,8},{3,9},{4,16},{5,17},{6,24},{7,25},{8,2},{9,3},{1... | collective-permute-start | bytes 786440 | tf_op jit(solution)/shard_map/ppermute | solution.py:210
  30.0 3.4 %collective-permute-done.6.refs_3_ = f32[256,256]{1,0:T(8,128)} collective-permute-done((f32[256,256]{1,0:T(8,128)}, f32[256,256]{1,0:T(8,128)}, u32[]{:S(2)}, u32[]{:S(2)}) %collective-permute-start.6) | collective-permute-done | bytes 262176 | tf_op jit(solution)/shard_map/ppermute | solution.py:210
  33.6 3.9 %shard_map.68 = (f32[512,256]{1,0:T(8,128)}, f32[512,256]{1,0:T(8,128)S(1)}, f32[512,256]{1,0:T(8,128)S(1)}, f32[512,256]{1,0:T(8,128)S(1)}, f32[512,256]{1,0:T(8,128)}) custom-call(s32[4]{0:T(128)S(1)} %pad_add_fusion.where_ref, f32[512,256]{1,0:T(8,128)S(1)} %get-tuple-element.80.refs_0_, f32[512,256]{1,0:T(8,128)S(1)} %collective-permute-done.1.refs_1_, ...), custom_call_target="tpu_custom_call" | custom-call | flops 805306368 | bytes 5242880 | tf_op jit(solution)/shard_map/pallas_call | solution.py:36
  37.5 4.7 %collective-permute-done.9.refs_4_ = f32[512,128]{1,0:T(8,128)S(1)} collective-permute-done((f32[512,128]{1,0:T(8,128)}, f32[512,128]{1,0:T(8,128)S(1)}, u32[]{:S(2)}, u32[]{:S(2)}) %collective-permute-start.9) | collective-permute-done | bytes 262176 | tf_op jit(solution)/shard_map/ppermute | solution.py:210
  45.9 4.1 %collective-permute-done.4.refs_2_ = f32[512,256]{1,0:T(8,128)S(1)} collective-permute-done((f32[512,256]{1,0:T(8,128)S(1)}, f32[512,256]{1,0:T(8,128)S(1)}, u32[]{:S(2)}, u32[]{:S(2)}) %collective-permute-start.4) | collective-permute-done | bytes 524320 | tf_op jit(solution)/shard_map/ppermute | solution.py:210
  50.3 6.2 %collective-permute-done.10 = f32[512,256]{1,0:T(8,128)S(1)} collective-permute-done((f32[512,256]{1,0:T(8,128)S(1)}, f32[512,256]{1,0:T(8,128)S(1)}, u32[]{:S(2)}, u32[]{:S(2)}) %collective-permute-start.10) | collective-permute-done | bytes 524320 | tf_op jit(solution)/shard_map/ppermute | solution.py:210
  56.7 3.3 %collective-permute-start.12 = (f32[512,256]{1,0:T(8,128)S(1)}, f32[512,256]{1,0:T(8,128)S(1)}, u32[]{:S(2)}, u32[]{:S(2)}) collective-permute-start(f32[512,256]{1,0:T(8,128)S(1)} %add_add_fusion.2.refs_4_), channel_id=1, source_target_pairs={{0,8},{1,9},{2,10},{3,11},{4,12},{5,13},{6,14},{7,15},{8,0},{9,1},... | collective-permute-start | bytes 1572872 | tf_op jit(solution)/shard_map/ppermute | solution.py:210
  60.0 4.0 %collective-permute-done.5.refs_3_ = f32[512,256]{1,0:T(8,128)S(1)} collective-permute-done((f32[512,256]{1,0:T(8,128)S(1)}, f32[512,256]{1,0:T(8,128)S(1)}, u32[]{:S(2)}, u32[]{:S(2)}) %collective-permute-start.5) | collective-permute-done | bytes 524320 | tf_op jit(solution)/shard_map/ppermute | solution.py:210
  65.1 3.1 %shard_map.69 = (f32[512,256]{1,0:T(8,128)}, f32[512,256]{1,0:T(8,128)S(1)}, f32[512,256]{1,0:T(8,128)S(1)}, f32[512,256]{1,0:T(8,128)S(1)}, f32[512,256]{1,0:T(8,128)S(1)}) custom-call(s32[4]{0:T(128)S(1)} %pad_add_fusion.where_ref, f32[512,256]{1,0:T(8,128)S(1)} %copy-done.11, f32[512,256]{1,0:T(8,128)S(1)} %collective-permute-done.3.refs_1_, ...), custom_call_target="tpu_custom_call" | custom-call | flops 805306368 | bytes 5767168 | tf_op jit(solution)/shard_map/pallas_call | solution.py:36
  69.5 8.4 %collective-permute-start.18 = (f32[512,256]{1,0:T(8,128)S(1)}, f32[512,256]{1,0:T(8,128)S(1)}, u32[]{:S(2)}, u32[]{:S(2)}) collective-permute-start(f32[512,256]{1,0:T(8,128)S(1)} %get-tuple-element.56), channel_id=1, source_target_pairs={{0,4},{1,5},{4,0},{5,1},{10,14},{11,15},{14,10},{15,11},{16,20},{1... | collective-permute-start | bytes 1572872 | tf_op jit(solution)/shard_map/ppermute | solution.py:210
  81.9 3.9 %collective-permute-start.15 = (f32[512,256]{1,0:T(8,128)S(1)}, f32[512,256]{1,0:T(8,128)S(1)}, u32[]{:S(2)}, u32[]{:S(2)}) collective-permute-start(f32[512,256]{1,0:T(8,128)S(1)} %collective-permute-done.13.refs_1_), channel_id=1, source_target_pairs={{0,16},{1,17},{2,18},{3,19},{4,20},{5,21},{6,22},{7,23},{8,24},{9,... | collective-permute-start | bytes 1572872 | tf_op jit(solution)/shard_map/ppermute | solution.py:210
  85.8 14.3 %collective-permute-done.18 = f32[512,256]{1,0:T(8,128)S(1)} collective-permute-done((f32[512,256]{1,0:T(8,128)S(1)}, f32[512,256]{1,0:T(8,128)S(1)}, u32[]{:S(2)}, u32[]{:S(2)}) %collective-permute-start.18) | collective-permute-done | bytes 524320 | tf_op jit(solution)/shard_map/ppermute | solution.py:210
  102.7 4.2 %shard_map.70 = (f32[512,256]{1,0:T(8,128)}, f32[512,256]{1,0:T(8,128)S(1)}, f32[512,256]{1,0:T(8,128)}, f32[512,256]{1,0:T(8,128)}, f32[512,256]{1,0:T(8,128)}) custom-call(s32[4]{0:T(128)S(1)} %pad_add_fusion.where_ref, f32[512,256]{1,0:T(8,128)S(1)} %get-tuple-element.52.refs_0_, f32[512,256]{1,0:T(8,128)S(1)} %collective-permute-done.13.refs_1_, ...), custom_call_target="tpu_custom_call" | custom-call | flops 805306368 | bytes 6291456 | tf_op jit(solution)/shard_map/pallas_call | solution.py:36
  108.4 4.6 %collective-permute-start.23 = (f32[512,256]{1,0:T(8,128)}, f32[512,256]{1,0:T(8,128)S(1)}, u32[]{:S(2)}, u32[]{:S(2)}) collective-permute-start(f32[512,256]{1,0:T(8,128)} %get-tuple-element.62), channel_id=1, source_target_pairs={{0,4},{1,5},{10,14},{11,15},{16,20},{17,21},{26,30},{27,31}} | collective-permute-start | bytes 1572872 | tf_op jit(solution)/shard_map/ppermute | solution.py:210
  117.7 5.1 %shard_map.71 = (f32[1024,128]{1,0:T(8,128)S(1)}, f32[1024,128]{1,0:T(8,128)S(1)}, f32[1024,128]{1,0:T(8,128)S(1)}, f32[1024,128]{1,0:T(8,128)S(1)}) custom-call(s32[6]{0:T(128)S(1)} %stack.50.where_ref, f32[1024,256]{1,0:T(8,128)S(1)} %copy-done.1, f32[1024,256]{1,0:T(8,128)S(1)} %copy-done.15, f32[512,256]{1,0:T(8,128)} %get-tuple-element.51.refs_2_, ...), custom_call_target="tpu_custom_call" | custom-call | flops 1610612736 | bytes 5242880 | tf_op jit(solution)/shard_map/pallas_call | solution.py:36
  130.6 12.7 %collective-permute-start.27 = (f32[512,128]{1,0:T(8,128)S(1)}, f32[512,128]{1,0:T(8,128)S(1)}, u32[]{:S(2)}, u32[]{:S(2)}) collective-permute-start(f32[512,128]{1,0:T(8,128)S(1)} %constant_dynamic-slice_fusion), channel_id=1, source_target_pairs={{0,0},{1,1},{2,8},{3,9},{4,16},{5,17},{6,24},{7,25},{8,2},{9,3},{1... | collective-permute-start | bytes 786440 | tf_op jit(solution)/shard_map/ppermute | solution.py:210
  143.4 8.6 %collective-permute-done.27 = f32[512,128]{1,0:T(8,128)S(1)} collective-permute-done((f32[512,128]{1,0:T(8,128)S(1)}, f32[512,128]{1,0:T(8,128)S(1)}, u32[]{:S(2)}, u32[]{:S(2)}) %collective-permute-start.27) | collective-permute-done | bytes 262176 | tf_op jit(solution)/shard_map/ppermute | solution.py:210
  162.1 3.7 %shard_map.73 = (f32[1024,128]{1,0:T(8,128)S(1)}, f32[1024,128]{1,0:T(8,128)S(1)}, f32[1024,128]{1,0:T(8,128)S(1)}) custom-call(s32[6]{0:T(128)S(1)} %stack.50.where_ref, f32[1024,256]{1,0:T(8,128)S(1)} %get-tuple-element.73.refs_0_, f32[1024,256]{1,0:T(8,128)S(1)} %collective-permute-done.24.refs_1_, f32[512,256]{1,0:T(8,128)S(1)} %add_add_fusion.refs_2_, ...), custom_call_target="tpu_custom_call" | custom-call | flops 1207959552 | bytes 7340032 | tf_op jit(solution)/shard_map/pallas_call | solution.py:36
  165.8 10.7 %collective-permute-done.29 = f32[512,128]{1,0:T(8,128)S(1)} collective-permute-done((f32[512,128]{1,0:T(8,128)S(1)}, f32[512,128]{1,0:T(8,128)S(1)}, u32[]{:S(2)}, u32[]{:S(2)}) %collective-permute-start.29) | collective-permute-done | bytes 262176 | tf_op jit(solution)/shard_map/ppermute | solution.py:210
  176.5 4.2 %collective-permute-start.34 = (f32[1024,128]{1,0:T(8,128)S(1)}, f32[1024,128]{1,0:T(8,128)S(1)}, u32[]{:S(2)}, u32[]{:S(2)}) collective-permute-start(f32[1024,128]{1,0:T(8,128)S(1)} %add.98), channel_id=1, source_target_pairs={{0,4},{1,5},{2,6},{3,7},{4,0},{5,1},{6,2},{7,3},{8,12},{9,13},{10,... | collective-permute-start | bytes 1572872 | tf_op jit(solution)/shard_map/ppermute | solution.py:210
  181.6 17.4 %collective-permute-done.32 = f32[1024,128]{1,0:T(8,128)S(1)} collective-permute-done((f32[1024,128]{1,0:T(8,128)S(1)}, f32[1024,128]{1,0:T(8,128)S(1)}, u32[]{:S(2)}, u32[]{:S(2)}) %collective-permute-start.32) | collective-permute-done | bytes 524320 | tf_op jit(solution)/shard_map/ppermute | solution.py:210
  199.0 5.6 %collective-permute-done.34 = f32[1024,128]{1,0:T(8,128)S(1)} collective-permute-done((f32[1024,128]{1,0:T(8,128)S(1)}, f32[1024,128]{1,0:T(8,128)S(1)}, u32[]{:S(2)}, u32[]{:S(2)}) %collective-permute-start.34) | collective-permute-done | bytes 524320 | tf_op jit(solution)/shard_map/ppermute | solution.py:210
  (107 shorter events, 46.7 us)
Async XLA Ops:
  2.0 20.7 %collective-permute-start.1 = (f32[512,256]{1,0:T(8,128)S(1)}, f32[512,256]{1,0:T(8,128)S(1)}, u32[]{:S(2)}, u32[]{:S(2)}) collective-permute-start(f32[512,256]{1,0:T(8,128)S(1)} %get-tuple-element.80.refs_0_), channel_id=1, source_target_pairs={{0,1},{1,0},{2,3},{3,2},{4,5},{5,4},{6,7},{7,6},{8,9},{9,8},{10,11... | collective-permute-start | bytes 1572872 | tf_op jit(solution)/shard_map/ppermute | solution.py:210
  3.6 19.9 %collective-permute-start.2 = (f32[512,256]{1,0:T(8,128)S(1)}, f32[512,256]{1,0:T(8,128)S(1)}, u32[]{:S(2)}, u32[]{:S(2)}) collective-permute-start(f32[512,256]{1,0:T(8,128)S(1)} %get-tuple-element.80.refs_0_), channel_id=1, source_target_pairs={{0,16},{1,17},{2,18},{3,19},{4,20},{5,21},{6,22},{7,23},{8,24},{9,... | collective-permute-start | bytes 1572872 | tf_op jit(solution)/shard_map/ppermute | solution.py:210
  4.9 17.8 %collective-permute-start = (f32[512,128]{1,0:T(8,128)S(1)}, f32[512,128]{1,0:T(8,128)S(1)}, u32[]{:S(2)}, u32[]{:S(2)}) collective-permute-start(f32[512,128]{1,0:T(8,128)S(1)} %get-tuple-element.83), channel_id=1, source_target_pairs={{0,0},{1,1},{2,8},{3,9},{4,16},{5,17},{6,24},{7,25},{8,2},{9,3},{1... | collective-permute-start | bytes 786440 | tf_op jit(solution)/shard_map/ppermute | solution.py:210
  24.7 17.5 %collective-permute-start.9 = (f32[512,128]{1,0:T(8,128)}, f32[512,128]{1,0:T(8,128)S(1)}, u32[]{:S(2)}, u32[]{:S(2)}) collective-permute-start(f32[512,128]{1,0:T(8,128)} %get-tuple-element.47), channel_id=1, source_target_pairs={{0,0},{1,1},{2,8},{3,9},{4,16},{5,17},{6,24},{7,25},{8,2},{9,3},{1... | collective-permute-start | bytes 786440 | tf_op jit(solution)/shard_map/ppermute | solution.py:210
  28.4 17.5 %collective-permute-start.3 = (f32[512,256]{1,0:T(8,128)S(1)}, f32[512,256]{1,0:T(8,128)S(1)}, u32[]{:S(2)}, u32[]{:S(2)}) collective-permute-start(f32[512,256]{1,0:T(8,128)S(1)} %copy-done.10), channel_id=1, source_target_pairs={{0,1},{1,0},{2,3},{3,2},{4,5},{5,4},{6,7},{7,6},{8,9},{9,8},{10,11... | collective-permute-start | bytes 1572872 | tf_op jit(solution)/shard_map/ppermute | solution.py:210
  30.0 20.1 %collective-permute-start.4 = (f32[512,256]{1,0:T(8,128)S(1)}, f32[512,256]{1,0:T(8,128)S(1)}, u32[]{:S(2)}, u32[]{:S(2)}) collective-permute-start(f32[512,256]{1,0:T(8,128)S(1)} %copy-done.10), channel_id=1, source_target_pairs={{0,16},{1,17},{2,18},{3,19},{4,20},{5,21},{6,22},{7,23},{8,24},{9,... | collective-permute-start | bytes 1572872 | tf_op jit(solution)/shard_map/ppermute | solution.py:210
  44.4 33.6 %collective-permute-start.20 = (f32[1024,256]{1,0:T(8,128)S(1)}, f32[1024,256]{1,0:T(8,128)S(1)}, u32[]{:S(2)}, u32[]{:S(2)}) collective-permute-start(f32[1024,256]{1,0:T(8,128)S(1)} %get-tuple-element.58.refs_0_), channel_id=1, source_target_pairs={{0,1},{1,0},{2,3},{3,2},{4,5},{5,4},{6,7},{7,6},{8,9},{9,8},{10,11... | collective-permute-start | bytes 3145736 | tf_op jit(solution)/shard_map/ppermute | solution.py:210
  50.1 14.0 %collective-permute-start.5 = (f32[512,256]{1,0:T(8,128)S(1)}, f32[512,256]{1,0:T(8,128)S(1)}, u32[]{:S(2)}, u32[]{:S(2)}) collective-permute-start(f32[512,256]{1,0:T(8,128)S(1)} %collective-permute-done.3.refs_1_), channel_id=1, source_target_pairs={{0,16},{1,17},{2,18},{3,19},{4,20},{5,21},{6,22},{7,23},{8,24},{9,... | collective-permute-start | bytes 1572872 | tf_op jit(solution)/shard_map/ppermute | solution.py:210
  64.0 16.3 %collective-permute-start.13 = (f32[512,256]{1,0:T(8,128)S(1)}, f32[512,256]{1,0:T(8,128)S(1)}, u32[]{:S(2)}, u32[]{:S(2)}) collective-permute-start(f32[512,256]{1,0:T(8,128)S(1)} %get-tuple-element.52.refs_0_), channel_id=1, source_target_pairs={{0,1},{1,0},{2,3},{3,2},{4,5},{5,4},{6,7},{7,6},{8,9},{9,8},{10,11... | collective-permute-start | bytes 1572872 | tf_op jit(solution)/shard_map/ppermute | solution.py:210
  64.8 17.0 %collective-permute-start.14 = (f32[512,256]{1,0:T(8,128)S(1)}, f32[512,256]{1,0:T(8,128)S(1)}, u32[]{:S(2)}, u32[]{:S(2)}) collective-permute-start(f32[512,256]{1,0:T(8,128)S(1)} %get-tuple-element.52.refs_0_), channel_id=1, source_target_pairs={{0,16},{1,17},{2,18},{3,19},{4,20},{5,21},{6,22},{7,23},{8,24},{9,... | collective-permute-start | bytes 1572872 | tf_op jit(solution)/shard_map/ppermute | solution.py:210
  68.2 17.6 %collective-permute-start.19 = (f32[512,256]{1,0:T(8,128)S(1)}, f32[512,256]{1,0:T(8,128)S(1)}, u32[]{:S(2)}, u32[]{:S(2)}) collective-permute-start(f32[512,256]{1,0:T(8,128)S(1)} %get-tuple-element.57), channel_id=1, source_target_pairs={{2,0},{3,1},{6,4},{7,5},{8,10},{9,11},{12,14},{13,15},{18,16},{19,... | collective-permute-start | bytes 1572872 | tf_op jit(solution)/shard_map/ppermute | solution.py:210
  69.5 30.6 %collective-permute-start.18 = (f32[512,256]{1,0:T(8,128)S(1)}, f32[512,256]{1,0:T(8,128)S(1)}, u32[]{:S(2)}, u32[]{:S(2)}) collective-permute-start(f32[512,256]{1,0:T(8,128)S(1)} %get-tuple-element.56), channel_id=1, source_target_pairs={{0,4},{1,5},{4,0},{5,1},{10,14},{11,15},{14,10},{15,11},{16,20},{1... | collective-permute-start | bytes 1572872 | tf_op jit(solution)/shard_map/ppermute | solution.py:210
  77.9 22.2 %collective-permute-start.17 = (f32[512,256]{1,0:T(8,128)S(1)}, f32[512,256]{1,0:T(8,128)S(1)}, u32[]{:S(2)}, u32[]{:S(2)}) collective-permute-start(f32[512,256]{1,0:T(8,128)S(1)} %get-tuple-element.55), channel_id=1, source_target_pairs={{2,4},{3,5},{6,0},{7,1},{8,14},{9,15},{12,10},{13,11},{18,20},{19,... | collective-permute-start | bytes 1572872 | tf_op jit(solution)/shard_map/ppermute | solution.py:210
  80.3 27.4 %collective-permute-start.24 = (f32[1024,256]{1,0:T(8,128)S(1)}, f32[1024,256]{1,0:T(8,128)S(1)}, u32[]{:S(2)}, u32[]{:S(2)}) collective-permute-start(f32[1024,256]{1,0:T(8,128)S(1)} %get-tuple-element.73.refs_0_), channel_id=1, source_target_pairs={{0,1},{1,0},{2,3},{3,2},{4,5},{5,4},{6,7},{7,6},{8,9},{9,8},{10,11... | collective-permute-start | bytes 3145736 | tf_op jit(solution)/shard_map/ppermute | solution.py:210
  81.9 20.9 %collective-permute-start.15 = (f32[512,256]{1,0:T(8,128)S(1)}, f32[512,256]{1,0:T(8,128)S(1)}, u32[]{:S(2)}, u32[]{:S(2)}) collective-permute-start(f32[512,256]{1,0:T(8,128)S(1)} %collective-permute-done.13.refs_1_), channel_id=1, source_target_pairs={{0,16},{1,17},{2,18},{3,19},{4,20},{5,21},{6,22},{7,23},{8,24},{9,... | collective-permute-start | bytes 1572872 | tf_op jit(solution)/shard_map/ppermute | solution.py:210
  100.8 14.4 %collective-permute-start.26 = (f32[512,256]{1,0:T(8,128)}, f32[512,256]{1,0:T(8,128)}, u32[]{:S(2)}, u32[]{:S(2)}) collective-permute-start(f32[512,256]{1,0:T(8,128)} %get-tuple-element.51.refs_2_), channel_id=1, source_target_pairs={{0,16},{1,17},{2,18},{3,19},{4,20},{5,21},{6,22},{7,23},{8,24},{9,... | collective-permute-start | bytes 1572872 | tf_op jit(solution)/shard_map/ppermute | solution.py:210
  107.8 15.0 %collective-permute-start.25 = (f32[512,256]{1,0:T(8,128)}, f32[512,256]{1,0:T(8,128)S(1)}, u32[]{:S(2)}, u32[]{:S(2)}) collective-permute-start(f32[512,256]{1,0:T(8,128)} %get-tuple-element.65), channel_id=1, source_target_pairs={{8,10},{9,11},{12,14},{13,15},{24,26},{25,27},{28,30},{29,31}} | collective-permute-start | bytes 1572872 | tf_op jit(solution)/shard_map/ppermute | solution.py:210
  108.4 17.3 %collective-permute-start.23 = (f32[512,256]{1,0:T(8,128)}, f32[512,256]{1,0:T(8,128)S(1)}, u32[]{:S(2)}, u32[]{:S(2)}) collective-permute-start(f32[512,256]{1,0:T(8,128)} %get-tuple-element.62), channel_id=1, source_target_pairs={{0,4},{1,5},{10,14},{11,15},{16,20},{17,21},{26,30},{27,31}} | collective-permute-start | bytes 1572872 | tf_op jit(solution)/shard_map/ppermute | solution.py:210
  128.0 24.1 %collective-permute-start.30 = (f32[512,256]{1,0:T(8,128)S(1)}, f32[512,256]{1,0:T(8,128)S(1)}, u32[]{:S(2)}, u32[]{:S(2)}) collective-permute-start(f32[512,256]{1,0:T(8,128)S(1)} %add_add_fusion.refs_2_), channel_id=1, source_target_pairs={{0,16},{1,17},{2,18},{3,19},{4,20},{5,21},{6,22},{7,23},{8,24},{9,... | collective-permute-start | bytes 1572872 | tf_op jit(solution)/shard_map/ppermute | solution.py:210
  130.6 21.5 %collective-permute-start.27 = (f32[512,128]{1,0:T(8,128)S(1)}, f32[512,128]{1,0:T(8,128)S(1)}, u32[]{:S(2)}, u32[]{:S(2)}) collective-permute-start(f32[512,128]{1,0:T(8,128)S(1)} %constant_dynamic-slice_fusion), channel_id=1, source_target_pairs={{0,0},{1,1},{2,8},{3,9},{4,16},{5,17},{6,24},{7,25},{8,2},{9,3},{1... | collective-permute-start | bytes 786440 | tf_op jit(solution)/shard_map/ppermute | solution.py:210
  157.0 19.5 %collective-permute-start.33 = (f32[1024,128]{1,0:T(8,128)S(1)}, f32[1024,128]{1,0:T(8,128)S(1)}, u32[]{:S(2)}, u32[]{:S(2)}) collective-permute-start(f32[1024,128]{1,0:T(8,128)S(1)} %shard_map.72), channel_id=1, source_target_pairs={{0,2},{1,3},{2,0},{3,1},{4,6},{5,7},{6,4},{7,5},{8,10},{9,11},{10,... | collective-permute-start | bytes 1572872 | tf_op jit(solution)/shard_map/ppermute | solution.py:210
  159.4 17.1 %collective-permute-start.29 = (f32[512,128]{1,0:T(8,128)S(1)}, f32[512,128]{1,0:T(8,128)S(1)}, u32[]{:S(2)}, u32[]{:S(2)}) collective-permute-start(f32[512,128]{1,0:T(8,128)S(1)} %dynamic-slice_add_fusion), channel_id=1, source_target_pairs={{0,0},{1,1},{2,8},{3,9},{4,16},{5,17},{6,24},{7,25},{8,2},{9,3},{1... | collective-permute-start | bytes 786440 | tf_op jit(solution)/shard_map/ppermute | solution.py:210
  176.5 22.5 %collective-permute-start.32 = (f32[1024,128]{1,0:T(8,128)S(1)}, f32[1024,128]{1,0:T(8,128)S(1)}, u32[]{:S(2)}, u32[]{:S(2)}) collective-permute-start(f32[1024,128]{1,0:T(8,128)S(1)} %get-tuple-element.76), channel_id=1, source_target_pairs={{0,2},{1,3},{2,0},{3,1},{4,6},{5,7},{6,4},{7,5},{8,10},{9,11},{10,... | collective-permute-start | bytes 1572872 | tf_op jit(solution)/shard_map/ppermute | solution.py:210
  176.5 28.0 %collective-permute-start.34 = (f32[1024,128]{1,0:T(8,128)S(1)}, f32[1024,128]{1,0:T(8,128)S(1)}, u32[]{:S(2)}, u32[]{:S(2)}) collective-permute-start(f32[1024,128]{1,0:T(8,128)S(1)} %add.98), channel_id=1, source_target_pairs={{0,4},{1,5},{2,6},{3,7},{4,0},{5,1},{6,2},{7,3},{8,12},{9,13},{10,... | collective-permute-start | bytes 1572872 | tf_op jit(solution)/shard_map/ppermute | solution.py:210
  (31 other events, 373.2 us)

commit v4 on v3

--- a/solution.py
+++ b/solution.py
@@ -50,10 +50,11 @@
     return copy
 
 
-def stage_kernel(places, shards, blocks, record, where_ref, *refs):
+def stage_kernel(places, shards, blocks, record, keep, where_ref, *refs):
     count = len(places)
-    pieces, given = refs[:count], refs[count:-blocks - 7]
-    vector_out, outs = refs[-blocks - 7], refs[-blocks - 6:-6]
+    outs = blocks // 2 + 1
+    pieces, given = refs[:count], refs[count:-outs - keep - 6]
+    vector_out, out_refs = refs[-outs - 7], refs[-outs - 6:-6]
     matrix_ref, given_ref, vector_ref, product_ref, sems, given_sems = refs[-6:]
     arrivals = [start(ref, given_ref.at[i], given_sems.at[i]) for i, ref in enumerate(given)] if not record else []
     core = where_ref[shards + 1]
@@ -68,38 +69,36 @@
         part = matrix_ref.at[k, o, pl.ds(row, pieces[i].shape[0])]
         copies.append(start(pieces[i], part, sems.at[i]))
     offset = where_ref[shards]
+    odd = lax.rem(offset, 2) == 1
+    product_ref[blocks // 2] = jnp.zeros_like(product_ref[blocks // 2])
     for copy in arrivals:
         copy.wait()
     if not record:
         vector_ref[...] = given_ref[0] + given_ref[1]
     elif len(given) > 2:
         vector_ref[...] = vector_ref[...] - (given_ref[0] + given_ref[1])
-    leaving = [start(vector_ref, vector_out, given_sems.at[0])]
-    product_ref[blocks // 2] = jnp.zeros_like(product_ref[blocks // 2])
+    leaving = [start(vector_ref, vector_out, given_sems.at[0])] if keep else []
     depth = vector_ref.shape[0] // shards
     parts = [
         split(vector_ref[pl.ds(pl.multiple_of(where_ref[o] * depth, depth), depth), :]) for o in range(shards)
     ]
-    for k in range(blocks // 2):
-        for i, place in enumerate(places):
-            if place[0] == k:
-                copies[i].wait()
+    for copy in copies:
+        copy.wait()
+    for i in reversed(range(blocks // 2)):
+        k = jnp.bitwise_xor(offset, 2 * i) // 2
         sums = [product(split(matrix_ref[k, o]), parts[o]) for o in range(shards)]
-        product_ref[k] = sum(sums[1:], sums[0])
-    for d in range(blocks):
-        k = jnp.bitwise_xor(offset, d) // 2
-        if d == 0:
-            k = jnp.where(lax.rem(offset, 2) == 1, blocks // 2, k)
-        leaving.append(start(product_ref.at[k], outs[d], sems.at[d]))
+        product_ref[i] = sum(sums[1:], sums[0])
+        leaving.append(start(product_ref.at[i], out_refs[1 + i], sems.at[1 + i]))
+    leaving.append(start(product_ref.at[jnp.where(odd, blocks // 2, 0)], out_refs[0], sems.at[0]))
     for copy in leaving:
         copy.wait()
 
 
-def stage(blocks, where, matrix, *given, record):
+def stage(blocks, where, matrix, *given, record, keep=False):
     rows, depth = matrix[0, 0, 0].shape
     shards = 1 + max(o for _, o, _ in matrix)
     width = given[0].shape[1] * (2 if record else 1)
-    outs = [shape(F32, shards * depth, width)] + [shape(F32, rows, width)] * blocks
+    outs = [shape(F32, shards * depth, width)] * keep + [shape(F32, rows, width)] * (blocks // 2 + 1)
     scratch = [
         pltpu.VMEM((blocks // 2, shards, rows, depth), F32),
         pltpu.VMEM((2, shards * depth, width), F32),
@@ -108,10 +107,11 @@
         pltpu.SemaphoreType.DMA((max(len(matrix), blocks),)),
         pltpu.SemaphoreType.DMA((4,)),
     ]
-    kernel = functools.partial(stage_kernel, list(matrix), shards, blocks, record)
+    kernel = functools.partial(stage_kernel, list(matrix), shards, blocks, record, keep)
     flops = 3 * blocks * rows * shards * depth * width
-    found = call(kernel, outs, scratch, flops, where, *matrix.values(), *given)
-    return found[0], list(found[1:])
+    found = list(call(kernel, outs, scratch, flops, where, *matrix.values(), *given))
+    vector = found.pop(0) if keep else None
+    return vector, [found[0]] + [found[1 + d // 2] for d in range(1, blocks)]
 
 
 def panel_kernel(shards, blocks, parts, wanted, where_ref, *refs):
@@ -172,7 +172,7 @@
         pltpu.SemaphoreType.DMA((len(wanted),)),
     ]
     kernel = functools.partial(panel_kernel, shards, blocks, parts, wanted)
-    flops = 6 * len(wanted) * rows * shards * depth * width // 2
+    flops = 9 * len(wanted) * rows * shards * depth * width
     before = [earlier[d] for d in wanted] if earlier else []
     found = call(kernel, outs, scratch, flops, where, *panel, *given, *before)
     return dict(zip(wanted, found, strict=True))
@@ -268,7 +268,7 @@
         sums = {d: blocks[d] for d in range(0, self.rows, 2)}
         for d in reversed(range(3, self.rows, 2)):
             sums[d - 1] = sums[d - 1] + self.move(blocks[d], lambda r, a, b: (r, a ^ 1, b))
-        got = [self.move(after(blocks[1], *last), lambda r, a, b: (r, a ^ 1, b))]
+        got = [self.move(after(blocks[1], *last, *[sums[d] for d in sums if d]), lambda r, a, b: (r, a ^ 1, b))]
         for d in reversed(range(2, self.rows, 2)):
             got.append(self.move(sums[d], lambda r, a, b: (r, a ^ d, b)))
         return [blocks[0], *got]
@@ -315,7 +315,7 @@
         panel_one = grid.gather_b(after(panel[0], *inverse_one.values()))
         held = after(inv_diag[1], *coupled.values())
         sums = list(grid.both(grid.merged_send(blocks, False)))
-        first, blocks = run(whole(coupled), *sums, record=False)
+        first, blocks = run(whole(coupled), *sums, record=False, keep=True)
         inverse_two = grid.gather_row(grid.gather_b(held))
         panel_two = grid.gather_b(after(panel[1], *panel_one.values()))
         sums = list(grid.both(grid.send(blocks, True)))

time: 207 us -> 203 us (0.981); the launches traced: 205 us -> 199 us
  waiting for transfers between devices: 98.3 us -> 93.3 us
    ppermute x35, waiting for transfers between devices: 98.3 us -> 93.3 us  [move(): return lax.ppermute(value, ('row', 'col'), pairs)]
    unnamed x40 -> x32, local copies, waits for them, and re-layouts: 5.17 us -> 5.3 us
  transfers between devices with their start and end apart: 35 -> 35, of which waited for: 16 -> 17; matrix products, arithmetic and copies ran while one was open for 2% -> 2% of each run, Pallas kernels for 10% -> 9%
where the time goes in v4:
time: 203 us; the launch traced here: 199 us
  waiting for transfers between devices  93.3 us (46%)
  starting transfers between devices  70.5 us (35%)
  Pallas kernels  20.7 us (10%)
  local copies, waits for them, and re-layouts  10.1 us (5%)
  other arithmetic  3.62 us (2%)
    ppermute x35, waiting for transfers between devices, move(): return lax.ppermute(value, ('row', 'col'), pairs)  93.3 us
    ppermute x35, starting transfers between devices, move(): return lax.ppermute(value, ('row', 'col'), pairs)  70.5 us
    pallas_call x6, Pallas kernels, call(): pl.pallas_call(kernel, out_shape=outs, in_specs=[SMEM] + [HBM] * len(oper...  20.7 us
    unnamed x32, local copies, waits for them, and re-layouts  5.3 us
  transfers between devices with their start and end apart: 35, of which 17 were waited for; matrix products, arithmetic and copies ran while one was open for 2% of the time, Pallas kernels for 9%

profile of v4, /device:TPU:2, one launch (start us, length us, event | category | flops | bytes accessed | tf_op | source)
XLA Modules:
  0.0 199.2 jit_solution(11842255825829833329)
XLA Ops:
  4.9 5.4 %collective-permute-start = (f32[512,128]{1,0:T(8,128)S(1)}, f32[512,128]{1,0:T(8,128)S(1)}, u32[]{:S(2)}, u32[]{:S(2)}) collective-permute-start(f32[512,128]{1,0:T(8,128)S(1)} %get-tuple-element.79), channel_id=1, source_target_pairs={{0,0},{1,1},{2,8},{3,9},{4,16},{5,17},{6,24},{7,25},{8,2},{9,3},{1... | collective-permute-start | bytes 786440 | tf_op jit(solution)/shard_map/ppermute | solution.py:210
  10.3 12.4 %collective-permute-done.refs_5_ = f32[512,128]{1,0:T(8,128)S(1)} collective-permute-done((f32[512,128]{1,0:T(8,128)S(1)}, f32[512,128]{1,0:T(8,128)S(1)}, u32[]{:S(2)}, u32[]{:S(2)}) %collective-permute-start) | collective-permute-done | bytes 262176 | tf_op jit(solution)/shard_map/ppermute | solution.py:210
  24.6 3.6 %collective-permute-start.9 = (f32[512,128]{1,0:T(8,128)}, f32[512,128]{1,0:T(8,128)S(1)}, u32[]{:S(2)}, u32[]{:S(2)}) collective-permute-start(f32[512,128]{1,0:T(8,128)} %get-tuple-element.45), channel_id=1, source_target_pairs={{0,0},{1,1},{2,8},{3,9},{4,16},{5,17},{6,24},{7,25},{8,2},{9,3},{1... | collective-permute-start | bytes 786440 | tf_op jit(solution)/shard_map/ppermute | solution.py:210
  30.0 3.4 %collective-permute-done.6.refs_3_ = f32[256,256]{1,0:T(8,128)} collective-permute-done((f32[256,256]{1,0:T(8,128)}, f32[256,256]{1,0:T(8,128)}, u32[]{:S(2)}, u32[]{:S(2)}) %collective-permute-start.6) | collective-permute-done | bytes 262176 | tf_op jit(solution)/shard_map/ppermute | solution.py:210
  33.6 3.8 %shard_map.68 = (f32[512,256]{1,0:T(8,128)S(1)}, f32[512,256]{1,0:T(8,128)S(1)}, f32[512,256]{1,0:T(8,128)S(1)}) custom-call(s32[4]{0:T(128)S(1)} %pad_add_fusion.where_ref, f32[512,256]{1,0:T(8,128)S(1)} %get-tuple-element.76.refs_0_, f32[512,256]{1,0:T(8,128)S(1)} %collective-permute-done.1.refs_1_, f32[512,256]{1,0:T(8,128)S(1)} %collective-permute-done.2.refs_2_, ...), custom_call_target="tpu_custom_call" | custom-call | flops 805306368 | bytes 4194304 | tf_op jit(solution)/shard_map/pallas_call | solution.py:36
  37.4 4.7 %collective-permute-done.9.refs_4_ = f32[512,128]{1,0:T(8,128)S(1)} collective-permute-done((f32[512,128]{1,0:T(8,128)}, f32[512,128]{1,0:T(8,128)S(1)}, u32[]{:S(2)}, u32[]{:S(2)}) %collective-permute-start.9) | collective-permute-done | bytes 262176 | tf_op jit(solution)/shard_map/ppermute | solution.py:210
  45.9 4.1 %collective-permute-done.4.refs_2_ = f32[512,256]{1,0:T(8,128)S(1)} collective-permute-done((f32[512,256]{1,0:T(8,128)S(1)}, f32[512,256]{1,0:T(8,128)S(1)}, u32[]{:S(2)}, u32[]{:S(2)}) %collective-permute-start.4) | collective-permute-done | bytes 524320 | tf_op jit(solution)/shard_map/ppermute | solution.py:210
  50.3 6.3 %collective-permute-done.10 = f32[512,256]{1,0:T(8,128)S(1)} collective-permute-done((f32[512,256]{1,0:T(8,128)S(1)}, f32[512,256]{1,0:T(8,128)S(1)}, u32[]{:S(2)}, u32[]{:S(2)}) %collective-permute-start.10) | collective-permute-done | bytes 524320 | tf_op jit(solution)/shard_map/ppermute | solution.py:210
  56.7 3.3 %collective-permute-start.12 = (f32[512,256]{1,0:T(8,128)S(1)}, f32[512,256]{1,0:T(8,128)S(1)}, u32[]{:S(2)}, u32[]{:S(2)}) collective-permute-start(f32[512,256]{1,0:T(8,128)S(1)} %add_add_fusion.2.refs_4_), channel_id=1, source_target_pairs={{0,8},{1,9},{2,10},{3,11},{4,12},{5,13},{6,14},{7,15},{8,0},{9,1},... | collective-permute-start | bytes 1572872 | tf_op jit(solution)/shard_map/ppermute | solution.py:210
  60.0 4.1 %collective-permute-done.5.refs_3_ = f32[512,256]{1,0:T(8,128)S(1)} collective-permute-done((f32[512,256]{1,0:T(8,128)S(1)}, f32[512,256]{1,0:T(8,128)S(1)}, u32[]{:S(2)}, u32[]{:S(2)}) %collective-permute-start.5) | collective-permute-done | bytes 524320 | tf_op jit(solution)/shard_map/ppermute | solution.py:210
  65.1 3.0 %shard_map.69 = (f32[512,256]{1,0:T(8,128)}, f32[512,256]{1,0:T(8,128)S(1)}, f32[512,256]{1,0:T(8,128)S(1)}, f32[512,256]{1,0:T(8,128)S(1)}) custom-call(s32[4]{0:T(128)S(1)} %pad_add_fusion.where_ref, f32[512,256]{1,0:T(8,128)S(1)} %copy-done.2, f32[512,256]{1,0:T(8,128)S(1)} %collective-permute-done.3.refs_1_, ...), custom_call_target="tpu_custom_call" | custom-call | flops 805306368 | bytes 5242880 | tf_op jit(solution)/shard_map/pallas_call | solution.py:36
  69.5 8.4 %collective-permute-start.18 = (f32[512,256]{1,0:T(8,128)S(1)}, f32[512,256]{1,0:T(8,128)S(1)}, u32[]{:S(2)}, u32[]{:S(2)}) collective-permute-start(f32[512,256]{1,0:T(8,128)S(1)} %get-tuple-element.53), channel_id=1, source_target_pairs={{0,4},{1,5},{4,0},{5,1},{10,14},{11,15},{14,10},{15,11},{16,20},{1... | collective-permute-start | bytes 1572872 | tf_op jit(solution)/shard_map/ppermute | solution.py:210
  82.1 3.6 %collective-permute-start.15 = (f32[512,256]{1,0:T(8,128)S(1)}, f32[512,256]{1,0:T(8,128)S(1)}, u32[]{:S(2)}, u32[]{:S(2)}) collective-permute-start(f32[512,256]{1,0:T(8,128)S(1)} %collective-permute-done.13.refs_1_), channel_id=1, source_target_pairs={{0,16},{1,17},{2,18},{3,19},{4,20},{5,21},{6,22},{7,23},{8,24},{9,... | collective-permute-start | bytes 1572872 | tf_op jit(solution)/shard_map/ppermute | solution.py:210
  85.8 13.8 %collective-permute-done.18 = f32[512,256]{1,0:T(8,128)S(1)} collective-permute-done((f32[512,256]{1,0:T(8,128)S(1)}, f32[512,256]{1,0:T(8,128)S(1)}, u32[]{:S(2)}, u32[]{:S(2)}) %collective-permute-start.18) | collective-permute-done | bytes 524320 | tf_op jit(solution)/shard_map/ppermute | solution.py:210
  103.3 3.0 %shard_map.70 = (f32[512,256]{1,0:T(8,128)S(1)}, f32[512,256]{1,0:T(8,128)}, f32[512,256]{1,0:T(8,128)}) custom-call(s32[4]{0:T(128)S(1)} %pad_add_fusion.where_ref, f32[512,256]{1,0:T(8,128)S(1)} %get-tuple-element.50.refs_0_, f32[512,256]{1,0:T(8,128)S(1)} %collective-permute-done.13.refs_1_, f32[512,256]{1,0:T(8,128)S(1)} %collective-permute-done.14.refs_2_, ...), custom_call_target="tpu_custom_call" | custom-call | flops 805306368 | bytes 5242880 | tf_op jit(solution)/shard_map/pallas_call | solution.py:36
  107.8 5.7 %collective-permute-start.23 = (f32[512,256]{1,0:T(8,128)}, f32[512,256]{1,0:T(8,128)}, u32[]{:S(2)}, u32[]{:S(2)}) collective-permute-start(f32[512,256]{1,0:T(8,128)} %get-tuple-element.58), channel_id=1, source_target_pairs={{0,4},{1,5},{10,14},{11,15},{16,20},{17,21},{26,30},{27,31}} | collective-permute-start | bytes 1572872 | tf_op jit(solution)/shard_map/ppermute | solution.py:210
  117.5 5.1 %shard_map.71 = (f32[1024,128]{1,0:T(8,128)S(1)}, f32[1024,128]{1,0:T(8,128)S(1)}, f32[1024,128]{1,0:T(8,128)S(1)}, f32[1024,128]{1,0:T(8,128)S(1)}) custom-call(s32[6]{0:T(128)S(1)} %stack.50.where_ref, f32[1024,256]{1,0:T(8,128)S(1)} %copy-done.1, f32[1024,256]{1,0:T(8,128)S(1)} %copy-done.6, f32[512,256]{1,0:T(8,128)} %get-tuple-element.49.refs_2_, ...), custom_call_target="tpu_custom_call" | custom-call | flops 4831838208 | bytes 5242880 | tf_op jit(solution)/shard_map/pallas_call | solution.py:36
  129.2 13.3 %collective-permute-start.27 = (f32[512,128]{1,0:T(8,128)S(1)}, f32[512,128]{1,0:T(8,128)S(1)}, u32[]{:S(2)}, u32[]{:S(2)}) collective-permute-start(f32[512,128]{1,0:T(8,128)S(1)} %constant_dynamic-slice_fusion), channel_id=1, source_target_pairs={{0,0},{1,1},{2,8},{3,9},{4,16},{5,17},{6,24},{7,25},{8,2},{9,3},{1... | collective-permute-start | bytes 786440 | tf_op jit(solution)/shard_map/ppermute | solution.py:210
  142.6 7.5 %collective-permute-done.27 = f32[512,128]{1,0:T(8,128)S(1)} collective-permute-done((f32[512,128]{1,0:T(8,128)S(1)}, f32[512,128]{1,0:T(8,128)S(1)}, u32[]{:S(2)}, u32[]{:S(2)}) %collective-permute-start.27) | collective-permute-done | bytes 262176 | tf_op jit(solution)/shard_map/ppermute | solution.py:210
  160.2 3.7 %shard_map.73 = (f32[1024,128]{1,0:T(8,128)S(1)}, f32[1024,128]{1,0:T(8,128)S(1)}, f32[1024,128]{1,0:T(8,128)S(1)}) custom-call(s32[6]{0:T(128)S(1)} %stack.50.where_ref, f32[1024,256]{1,0:T(8,128)S(1)} %get-tuple-element.69.refs_0_, f32[1024,256]{1,0:T(8,128)S(1)} %collective-permute-done.24.refs_1_, f32[512,256]{1,0:T(8,128)S(1)} %add_add_fusion.refs_2_, ...), custom_call_target="tpu_custom_call" | custom-call | flops 3623878656 | bytes 7340032 | tf_op jit(solution)/shard_map/pallas_call | solution.py:36
  163.9 5.5 %collective-permute-done.32 = f32[1024,128]{1,0:T(8,128)S(1)} collective-permute-done((f32[1024,128]{1,0:T(8,128)S(1)}, f32[1024,128]{1,0:T(8,128)S(1)}, u32[]{:S(2)}, u32[]{:S(2)}) %collective-permute-start.32) | collective-permute-done | bytes 524320 | tf_op jit(solution)/shard_map/ppermute | solution.py:210
  171.8 3.3 %collective-permute-done.29 = f32[512,128]{1,0:T(8,128)S(1)} collective-permute-done((f32[512,128]{1,0:T(8,128)S(1)}, f32[512,128]{1,0:T(8,128)S(1)}, u32[]{:S(2)}, u32[]{:S(2)}) %collective-permute-start.29) | collective-permute-done | bytes 262176 | tf_op jit(solution)/shard_map/ppermute | solution.py:210
  175.9 19.2 %collective-permute-done.34 = f32[1024,128]{1,0:T(8,128)S(1)} collective-permute-done((f32[1024,128]{1,0:T(8,128)S(1)}, f32[1024,128]{1,0:T(8,128)S(1)}, u32[]{:S(2)}, u32[]{:S(2)}) %collective-permute-start.34) | collective-permute-done | bytes 524320 | tf_op jit(solution)/shard_map/ppermute | solution.py:210
  195.1 3.2 %collective-permute-done.33 = f32[1024,128]{1,0:T(8,128)S(1)} collective-permute-done((f32[1024,128]{1,0:T(8,128)S(1)}, f32[1024,128]{1,0:T(8,128)S(1)}, u32[]{:S(2)}, u32[]{:S(2)}) %collective-permute-start.33) | collective-permute-done | bytes 524320 | tf_op jit(solution)/shard_map/ppermute | solution.py:210
  (99 shorter events, 48.7 us)
Async XLA Ops:
  2.0 20.7 %collective-permute-start.1 = (f32[512,256]{1,0:T(8,128)S(1)}, f32[512,256]{1,0:T(8,128)S(1)}, u32[]{:S(2)}, u32[]{:S(2)}) collective-permute-start(f32[512,256]{1,0:T(8,128)S(1)} %get-tuple-element.76.refs_0_), channel_id=1, source_target_pairs={{0,1},{1,0},{2,3},{3,2},{4,5},{5,4},{6,7},{7,6},{8,9},{9,8},{10,11... | collective-permute-start | bytes 1572872 | tf_op jit(solution)/shard_map/ppermute | solution.py:210
  3.6 19.8 %collective-permute-start.2 = (f32[512,256]{1,0:T(8,128)S(1)}, f32[512,256]{1,0:T(8,128)S(1)}, u32[]{:S(2)}, u32[]{:S(2)}) collective-permute-start(f32[512,256]{1,0:T(8,128)S(1)} %get-tuple-element.76.refs_0_), channel_id=1, source_target_pairs={{0,16},{1,17},{2,18},{3,19},{4,20},{5,21},{6,22},{7,23},{8,24},{9,... | collective-permute-start | bytes 1572872 | tf_op jit(solution)/shard_map/ppermute | solution.py:210
  4.9 17.8 %collective-permute-start = (f32[512,128]{1,0:T(8,128)S(1)}, f32[512,128]{1,0:T(8,128)S(1)}, u32[]{:S(2)}, u32[]{:S(2)}) collective-permute-start(f32[512,128]{1,0:T(8,128)S(1)} %get-tuple-element.79), channel_id=1, source_target_pairs={{0,0},{1,1},{2,8},{3,9},{4,16},{5,17},{6,24},{7,25},{8,2},{9,3},{1... | collective-permute-start | bytes 786440 | tf_op jit(solution)/shard_map/ppermute | solution.py:210
  24.6 17.5 %collective-permute-start.9 = (f32[512,128]{1,0:T(8,128)}, f32[512,128]{1,0:T(8,128)S(1)}, u32[]{:S(2)}, u32[]{:S(2)}) collective-permute-start(f32[512,128]{1,0:T(8,128)} %get-tuple-element.45), channel_id=1, source_target_pairs={{0,0},{1,1},{2,8},{3,9},{4,16},{5,17},{6,24},{7,25},{8,2},{9,3},{1... | collective-permute-start | bytes 786440 | tf_op jit(solution)/shard_map/ppermute | solution.py:210
  28.4 17.5 %collective-permute-start.3 = (f32[512,256]{1,0:T(8,128)S(1)}, f32[512,256]{1,0:T(8,128)S(1)}, u32[]{:S(2)}, u32[]{:S(2)}) collective-permute-start(f32[512,256]{1,0:T(8,128)S(1)} %copy-done.2), channel_id=1, source_target_pairs={{0,1},{1,0},{2,3},{3,2},{4,5},{5,4},{6,7},{7,6},{8,9},{9,8},{10,11... | collective-permute-start | bytes 1572872 | tf_op jit(solution)/shard_map/ppermute | solution.py:210
  30.0 20.1 %collective-permute-start.4 = (f32[512,256]{1,0:T(8,128)S(1)}, f32[512,256]{1,0:T(8,128)S(1)}, u32[]{:S(2)}, u32[]{:S(2)}) collective-permute-start(f32[512,256]{1,0:T(8,128)S(1)} %copy-done.2), channel_id=1, source_target_pairs={{0,16},{1,17},{2,18},{3,19},{4,20},{5,21},{6,22},{7,23},{8,24},{9,... | collective-permute-start | bytes 1572872 | tf_op jit(solution)/shard_map/ppermute | solution.py:210
  44.3 33.5 %collective-permute-start.20 = (f32[1024,256]{1,0:T(8,128)S(1)}, f32[1024,256]{1,0:T(8,128)S(1)}, u32[]{:S(2)}, u32[]{:S(2)}) collective-permute-start(f32[1024,256]{1,0:T(8,128)S(1)} %get-tuple-element.55.refs_0_), channel_id=1, source_target_pairs={{0,1},{1,0},{2,3},{3,2},{4,5},{5,4},{6,7},{7,6},{8,9},{9,8},{10,11... | collective-permute-start | bytes 3145736 | tf_op jit(solution)/shard_map/ppermute | solution.py:210
  50.1 14.0 %collective-permute-start.5 = (f32[512,256]{1,0:T(8,128)S(1)}, f32[512,256]{1,0:T(8,128)S(1)}, u32[]{:S(2)}, u32[]{:S(2)}) collective-permute-start(f32[512,256]{1,0:T(8,128)S(1)} %collective-permute-done.3.refs_1_), channel_id=1, source_target_pairs={{0,16},{1,17},{2,18},{3,19},{4,20},{5,21},{6,22},{7,23},{8,24},{9,... | collective-permute-start | bytes 1572872 | tf_op jit(solution)/shard_map/ppermute | solution.py:210
  64.0 16.3 %collective-permute-start.13 = (f32[512,256]{1,0:T(8,128)S(1)}, f32[512,256]{1,0:T(8,128)S(1)}, u32[]{:S(2)}, u32[]{:S(2)}) collective-permute-start(f32[512,256]{1,0:T(8,128)S(1)} %get-tuple-element.50.refs_0_), channel_id=1, source_target_pairs={{0,1},{1,0},{2,3},{3,2},{4,5},{5,4},{6,7},{7,6},{8,9},{9,8},{10,11... | collective-permute-start | bytes 1572872 | tf_op jit(solution)/shard_map/ppermute | solution.py:210
  64.8 17.3 %collective-permute-start.14 = (f32[512,256]{1,0:T(8,128)S(1)}, f32[512,256]{1,0:T(8,128)S(1)}, u32[]{:S(2)}, u32[]{:S(2)}) collective-permute-start(f32[512,256]{1,0:T(8,128)S(1)} %get-tuple-element.50.refs_0_), channel_id=1, source_target_pairs={{0,16},{1,17},{2,18},{3,19},{4,20},{5,21},{6,22},{7,23},{8,24},{9,... | collective-permute-start | bytes 1572872 | tf_op jit(solution)/shard_map/ppermute | solution.py:210
  68.2 17.6 %collective-permute-start.19 = (f32[512,256]{1,0:T(8,128)S(1)}, f32[512,256]{1,0:T(8,128)S(1)}, u32[]{:S(2)}, u32[]{:S(2)}) collective-permute-start(f32[512,256]{1,0:T(8,128)S(1)} %get-tuple-element.54), channel_id=1, source_target_pairs={{2,0},{3,1},{6,4},{7,5},{8,10},{9,11},{12,14},{13,15},{18,16},{19,... | collective-permute-start | bytes 1572872 | tf_op jit(solution)/shard_map/ppermute | solution.py:210
  69.5 30.1 %collective-permute-start.18 = (f32[512,256]{1,0:T(8,128)S(1)}, f32[512,256]{1,0:T(8,128)S(1)}, u32[]{:S(2)}, u32[]{:S(2)}) collective-permute-start(f32[512,256]{1,0:T(8,128)S(1)} %get-tuple-element.53), channel_id=1, source_target_pairs={{0,4},{1,5},{4,0},{5,1},{10,14},{11,15},{14,10},{15,11},{16,20},{1... | collective-permute-start | bytes 1572872 | tf_op jit(solution)/shard_map/ppermute | solution.py:210
  78.8 20.8 %collective-permute-start.17 = (f32[512,256]{1,0:T(8,128)S(1)}, f32[512,256]{1,0:T(8,128)S(1)}, u32[]{:S(2)}, u32[]{:S(2)}) collective-permute-start(f32[512,256]{1,0:T(8,128)S(1)} %get-tuple-element.53), channel_id=1, source_target_pairs={{2,4},{3,5},{6,0},{7,1},{8,14},{9,15},{12,10},{13,11},{18,20},{19,... | collective-permute-start | bytes 1572872 | tf_op jit(solution)/shard_map/ppermute | solution.py:210
  80.3 26.0 %collective-permute-start.24 = (f32[1024,256]{1,0:T(8,128)S(1)}, f32[1024,256]{1,0:T(8,128)S(1)}, u32[]{:S(2)}, u32[]{:S(2)}) collective-permute-start(f32[1024,256]{1,0:T(8,128)S(1)} %get-tuple-element.69.refs_0_), channel_id=1, source_target_pairs={{0,1},{1,0},{2,3},{3,2},{4,5},{5,4},{6,7},{7,6},{8,9},{9,8},{10,11... | collective-permute-start | bytes 3145736 | tf_op jit(solution)/shard_map/ppermute | solution.py:210
  82.1 21.1 %collective-permute-start.15 = (f32[512,256]{1,0:T(8,128)S(1)}, f32[512,256]{1,0:T(8,128)S(1)}, u32[]{:S(2)}, u32[]{:S(2)}) collective-permute-start(f32[512,256]{1,0:T(8,128)S(1)} %collective-permute-done.13.refs_1_), channel_id=1, source_target_pairs={{0,16},{1,17},{2,18},{3,19},{4,20},{5,21},{6,22},{7,23},{8,24},{9,... | collective-permute-start | bytes 1572872 | tf_op jit(solution)/shard_map/ppermute | solution.py:210
  99.8 15.2 %collective-permute-start.26 = (f32[512,256]{1,0:T(8,128)}, f32[512,256]{1,0:T(8,128)}, u32[]{:S(2)}, u32[]{:S(2)}) collective-permute-start(f32[512,256]{1,0:T(8,128)} %get-tuple-element.49.refs_2_), channel_id=1, source_target_pairs={{0,16},{1,17},{2,18},{3,19},{4,20},{5,21},{6,22},{7,23},{8,24},{9,... | collective-permute-start | bytes 1572872 | tf_op jit(solution)/shard_map/ppermute | solution.py:210
  106.3 17.0 %collective-permute-start.25 = (f32[512,256]{1,0:T(8,128)}, f32[512,256]{1,0:T(8,128)}, u32[]{:S(2)}, u32[]{:S(2)}) collective-permute-start(f32[512,256]{1,0:T(8,128)} %get-tuple-element.61), channel_id=1, source_target_pairs={{8,10},{9,11},{12,14},{13,15},{24,26},{25,27},{28,30},{29,31}} | collective-permute-start | bytes 1572872 | tf_op jit(solution)/shard_map/ppermute | solution.py:210
  107.8 17.6 %collective-permute-start.23 = (f32[512,256]{1,0:T(8,128)}, f32[512,256]{1,0:T(8,128)}, u32[]{:S(2)}, u32[]{:S(2)}) collective-permute-start(f32[512,256]{1,0:T(8,128)} %get-tuple-element.58), channel_id=1, source_target_pairs={{0,4},{1,5},{10,14},{11,15},{16,20},{17,21},{26,30},{27,31}} | collective-permute-start | bytes 1572872 | tf_op jit(solution)/shard_map/ppermute | solution.py:210
  126.9 23.2 %collective-permute-start.30 = (f32[512,256]{1,0:T(8,128)S(1)}, f32[512,256]{1,0:T(8,128)S(1)}, u32[]{:S(2)}, u32[]{:S(2)}) collective-permute-start(f32[512,256]{1,0:T(8,128)S(1)} %add_add_fusion.refs_2_), channel_id=1, source_target_pairs={{0,16},{1,17},{2,18},{3,19},{4,20},{5,21},{6,22},{7,23},{8,24},{9,... | collective-permute-start | bytes 1572872 | tf_op jit(solution)/shard_map/ppermute | solution.py:210
  129.2 20.9 %collective-permute-start.27 = (f32[512,128]{1,0:T(8,128)S(1)}, f32[512,128]{1,0:T(8,128)S(1)}, u32[]{:S(2)}, u32[]{:S(2)}) collective-permute-start(f32[512,128]{1,0:T(8,128)S(1)} %constant_dynamic-slice_fusion), channel_id=1, source_target_pairs={{0,0},{1,1},{2,8},{3,9},{4,16},{5,17},{6,24},{7,25},{8,2},{9,3},{1... | collective-permute-start | bytes 786440 | tf_op jit(solution)/shard_map/ppermute | solution.py:210
  155.1 14.3 %collective-permute-start.32 = (f32[1024,128]{1,0:T(8,128)S(1)}, f32[1024,128]{1,0:T(8,128)S(1)}, u32[]{:S(2)}, u32[]{:S(2)}) collective-permute-start(f32[1024,128]{1,0:T(8,128)S(1)} %shard_map.72), channel_id=1, source_target_pairs={{0,2},{1,3},{2,0},{3,1},{4,6},{5,7},{6,4},{7,5},{8,10},{9,11},{10,... | collective-permute-start | bytes 1572872 | tf_op jit(solution)/shard_map/ppermute | solution.py:210
  157.2 17.9 %collective-permute-start.29 = (f32[512,128]{1,0:T(8,128)S(1)}, f32[512,128]{1,0:T(8,128)S(1)}, u32[]{:S(2)}, u32[]{:S(2)}) collective-permute-start(f32[512,128]{1,0:T(8,128)S(1)} %dynamic-slice_add_fusion), channel_id=1, source_target_pairs={{0,0},{1,1},{2,8},{3,9},{4,16},{5,17},{6,24},{7,25},{8,2},{9,3},{1... | collective-permute-start | bytes 786440 | tf_op jit(solution)/shard_map/ppermute | solution.py:210
  169.5 25.6 %collective-permute-start.34 = (f32[1024,128]{1,0:T(8,128)S(1)}, f32[1024,128]{1,0:T(8,128)S(1)}, u32[]{:S(2)}, u32[]{:S(2)}) collective-permute-start(f32[1024,128]{1,0:T(8,128)S(1)} %add.97), channel_id=1, source_target_pairs={{0,4},{1,5},{2,6},{3,7},{4,0},{5,1},{6,2},{7,3},{8,12},{9,13},{10,... | collective-permute-start | bytes 1572872 | tf_op jit(solution)/shard_map/ppermute | solution.py:210
  175.1 23.2 %collective-permute-start.33 = (f32[1024,128]{1,0:T(8,128)S(1)}, f32[1024,128]{1,0:T(8,128)S(1)}, u32[]{:S(2)}, u32[]{:S(2)}) collective-permute-start(f32[1024,128]{1,0:T(8,128)S(1)} %get-tuple-element.73), channel_id=1, source_target_pairs={{0,2},{1,3},{2,0},{3,1},{4,6},{5,7},{6,4},{7,5},{8,10},{9,11},{10,... | collective-permute-start | bytes 1572872 | tf_op jit(solution)/shard_map/ppermute | solution.py:210
  (27 other events, 250.3 us)

commit v5 on v4

--- a/solution.py
+++ b/solution.py
@@ -95,7 +95,8 @@
 
 
 def stage(blocks, where, matrix, *given, record, keep=False):
-    rows, depth = matrix[0, 0, 0].shape
+    depth = matrix[0, 0, 0].shape[1]
+    rows = sum(piece.shape[0] for (k, o, _), piece in matrix.items() if k == o == 0)
     shards = 1 + max(o for _, o, _ in matrix)
     width = given[0].shape[1] * (2 if record else 1)
     outs = [shape(F32, shards * depth, width)] * keep + [shape(F32, rows, width)] * (blocks // 2 + 1)
@@ -290,17 +291,22 @@
         width = top_rhs.shape[2]
 
         record_one = grid.swap(top_rhs[0])
-        inverse_one = grid.gather_b(inv_diag[0])
-        far = {(k // 2, 0): grid.row_bit(inv_diag[0], k) for k in range(2, rows, 2)}
-        early = [record_one, *inverse_one.values(), *far.values()]
         half = inv_diag.shape[1] // 2
-        inverse_one = {(*place, 0): piece for place, piece in (inverse_one | far).items()}
+        top, bottom = inv_diag[0][:half], inv_diag[0][half:]
+        inverse_one = {(0, 0, 0): top, (0, 0, half): bottom}
+        for o in range(1, shards):
+            inverse_one[0, o, 0] = grid.b_bit(top, o)
+        for k in range(2, rows, 2):
+            inverse_one[k // 2, 0, half] = grid.row_bit(bottom, k)
+        early = [record_one, *inverse_one.values()]
         for k in range(2, rows, 2):
             for o in range(1, shards):
-                one, two = together(inverse_one[0, o, 0][:half], inverse_one[k // 2, 0, 0][half:])
-                early += [one, two]
-                inverse_one[k // 2, o, 0] = grid.row_bit(one, k)
-                inverse_one[k // 2, o, half] = grid.b_bit(two, o)
+                inverse_one[k // 2, o, 0] = grid.row_bit(inverse_one[0, o, 0], k)
+                inverse_one[k // 2, o, half] = grid.b_bit(inverse_one[k // 2, 0, half], o)
+        for o in range(1, shards):
+            inverse_one[0, o, half] = grid.b_bit(bottom, o)
+        for k in range(2, rows, 2):
+            inverse_one[k // 2, 0, 0] = grid.row_bit(top, k)
         held = after(coupling, *early)
         coupled = grid.gather_b(held)
         coupled |= {(k // 2, 0): grid.row_bit(held, k) for k in range(2, rows, 2)}

time: 203 us -> 201 us (level)
  local copies, waits for them, and re-layouts: 10.1 us -> 14.7 us
  waiting for transfers between devices: 93.3 us -> 89.7 us
    unnamed x32 -> x44, local copies, waits for them, and re-layouts: 5.3 us -> 10.5 us
    ppermute x35 -> x37, waiting for transfers between devices: 93.3 us -> 89.7 us  [move(): return lax.ppermute(value, ('row', 'col'), pairs)]
    ppermute x35 -> x37, starting transfers between devices: 70.5 us -> 69.2 us  [move(): return lax.ppermute(value, ('row', 'col'), pairs)]
  transfers between devices with their start and end apart: 35 -> 37, of which waited for: 17 -> 17; matrix products, arithmetic and copies ran while one was open for 2% -> 2% of each run, Pallas kernels for 9% -> 9%
where the time goes in v5:
time: 201 us; the launch traced here: 198 us
  waiting for transfers between devices  89.7 us (45%)
  starting transfers between devices  69.2 us (34%)
  Pallas kernels  19.7 us (10%)
  local copies, waits for them, and re-layouts  14.7 us (7%)
  other arithmetic  3.83 us (2%)
    ppermute x37, waiting for transfers between devices, move(): return lax.ppermute(value, ('row', 'col'), pairs)  89.7 us
    ppermute x37, starting transfers between devices, move(): return lax.ppermute(value, ('row', 'col'), pairs)  69.2 us
    pallas_call x6, Pallas kernels, call(): pl.pallas_call(kernel, out_shape=outs, in_specs=[SMEM] + [HBM] * len(oper...  19.7 us
    unnamed x44, local copies, waits for them, and re-layouts  10.5 us
  transfers between devices with their start and end apart: 37, of which 17 were waited for; matrix products, arithmetic and copies ran while one was open for 2% of the time, Pallas kernels for 9%

profile of v5, /device:TPU:2, one launch (start us, length us, event | category | flops | bytes accessed | tf_op | source)
XLA Modules:
  0.0 198.1 jit_solution(3020622339905746565)
XLA Ops:
  5.7 5.4 %collective-permute-start = (f32[512,128]{1,0:T(8,128)S(1)}, f32[512,128]{1,0:T(8,128)S(1)}, u32[]{:S(2)}, u32[]{:S(2)}) collective-permute-start(f32[512,128]{1,0:T(8,128)S(1)} %get-tuple-element.75), channel_id=1, source_target_pairs={{0,0},{1,1},{2,8},{3,9},{4,16},{5,17},{6,24},{7,25},{8,2},{9,3},{1... | collective-permute-start | bytes 786440 | tf_op jit(solution)/shard_map/ppermute | solution.py:211
  15.2 8.4 %collective-permute-done.refs_8_ = f32[512,128]{1,0:T(8,128)S(1)} collective-permute-done((f32[512,128]{1,0:T(8,128)S(1)}, f32[512,128]{1,0:T(8,128)S(1)}, u32[]{:S(2)}, u32[]{:S(2)}) %collective-permute-start) | collective-permute-done | bytes 262176 | tf_op jit(solution)/shard_map/ppermute | solution.py:211
  23.6 3.4 %collective-permute-start.11 = (f32[512,128]{1,0:T(8,128)}, f32[512,128]{1,0:T(8,128)S(1)}, u32[]{:S(2)}, u32[]{:S(2)}) collective-permute-start(f32[512,128]{1,0:T(8,128)} %get-tuple-element.41), channel_id=1, source_target_pairs={{0,0},{1,1},{2,8},{3,9},{4,16},{5,17},{6,24},{7,25},{8,2},{9,3},{1... | collective-permute-start | bytes 786440 | tf_op jit(solution)/shard_map/ppermute | solution.py:211
  27.7 3.6 %collective-permute-done.6.refs_4_ = f32[256,256]{1,0:T(8,128)S(1)} collective-permute-done((f32[256,256]{1,0:T(8,128)S(1)}, f32[256,256]{1,0:T(8,128)S(1)}, u32[]{:S(2)}, u32[]{:S(2)}) %collective-permute-start.6) | collective-permute-done | bytes 262176 | tf_op jit(solution)/shard_map/ppermute | solution.py:211
  34.6 3.0 %shard_map.68 = (f32[512,256]{1,0:T(8,128)S(1)}, f32[512,256]{1,0:T(8,128)S(1)}, f32[512,256]{1,0:T(8,128)S(1)}) custom-call(s32[4]{0:T(128)S(1)} %pad_add_fusion.where_ref, f32[256,256]{1,0:T(8,128)S(1)} %get-tuple-element.73.refs_0_, f32[256,256]{1,0:T(8,128)S(1)} %get-tuple-element.72.refs_1_, f32[256,256]{1,0:T(8,128)S(1)} %collective-permute-done.1.refs_2_, ...), custom_call_target="tpu_custom_call" | custom-call | flops 805306368 | bytes 4194304 | tf_op jit(solution)/shard_map/pallas_call | solution.py:36
  37.6 3.1 %collective-permute-done.11.refs_4_ = f32[512,128]{1,0:T(8,128)S(1)} collective-permute-done((f32[512,128]{1,0:T(8,128)}, f32[512,128]{1,0:T(8,128)S(1)}, u32[]{:S(2)}, u32[]{:S(2)}) %collective-permute-start.11) | collective-permute-done | bytes 262176 | tf_op jit(solution)/shard_map/ppermute | solution.py:211
  43.5 6.3 %collective-permute-done.4.refs_2_ = f32[512,256]{1,0:T(8,128)S(1)} collective-permute-done((f32[512,256]{1,0:T(8,128)S(1)}, f32[512,256]{1,0:T(8,128)S(1)}, u32[]{:S(2)}, u32[]{:S(2)}) %collective-permute-start.4) | collective-permute-done | bytes 524320 | tf_op jit(solution)/shard_map/ppermute | solution.py:211
  49.9 5.2 %collective-permute-done.12 = f32[512,256]{1,0:T(8,128)S(1)} collective-permute-done((f32[512,256]{1,0:T(8,128)S(1)}, f32[512,256]{1,0:T(8,128)S(1)}, u32[]{:S(2)}, u32[]{:S(2)}) %collective-permute-start.12) | collective-permute-done | bytes 524320 | tf_op jit(solution)/shard_map/ppermute | solution.py:211
  55.2 3.9 %collective-permute-start.14 = (f32[512,256]{1,0:T(8,128)S(1)}, f32[512,256]{1,0:T(8,128)S(1)}, u32[]{:S(2)}, u32[]{:S(2)}) collective-permute-start(f32[512,256]{1,0:T(8,128)S(1)} %add_add_fusion.2.refs_4_), channel_id=1, source_target_pairs={{0,8},{1,9},{2,10},{3,11},{4,12},{5,13},{6,14},{7,15},{8,0},{9,1},... | collective-permute-start | bytes 1572872 | tf_op jit(solution)/shard_map/ppermute | solution.py:211
  59.1 4.3 %collective-permute-done.5.refs_3_ = f32[512,256]{1,0:T(8,128)S(1)} collective-permute-done((f32[512,256]{1,0:T(8,128)S(1)}, f32[512,256]{1,0:T(8,128)S(1)}, u32[]{:S(2)}, u32[]{:S(2)}) %collective-permute-start.5) | collective-permute-done | bytes 524320 | tf_op jit(solution)/shard_map/ppermute | solution.py:211
  64.6 3.0 %shard_map.69 = (f32[512,256]{1,0:T(8,128)}, f32[512,256]{1,0:T(8,128)S(1)}, f32[512,256]{1,0:T(8,128)S(1)}, f32[512,256]{1,0:T(8,128)S(1)}) custom-call(s32[4]{0:T(128)S(1)} %pad_add_fusion.where_ref, f32[512,256]{1,0:T(8,128)S(1)} %copy-done.2, f32[512,256]{1,0:T(8,128)S(1)} %collective-permute-done.3.refs_1_, ...), custom_call_target="tpu_custom_call" | custom-call | flops 805306368 | bytes 5242880 | tf_op jit(solution)/shard_map/pallas_call | solution.py:36
  68.9 6.7 %collective-permute-start.20 = (f32[512,256]{1,0:T(8,128)S(1)}, f32[512,256]{1,0:T(8,128)S(1)}, u32[]{:S(2)}, u32[]{:S(2)}) collective-permute-start(f32[512,256]{1,0:T(8,128)S(1)} %get-tuple-element.49), channel_id=1, source_target_pairs={{0,4},{1,5},{4,0},{5,1},{10,14},{11,15},{14,10},{15,11},{16,20},{1... | collective-permute-start | bytes 1572872 | tf_op jit(solution)/shard_map/ppermute | solution.py:211
  79.9 3.9 %collective-permute-start.17 = (f32[512,256]{1,0:T(8,128)S(1)}, f32[512,256]{1,0:T(8,128)S(1)}, u32[]{:S(2)}, u32[]{:S(2)}) collective-permute-start(f32[512,256]{1,0:T(8,128)S(1)} %collective-permute-done.15.refs_1_), channel_id=1, source_target_pairs={{0,16},{1,17},{2,18},{3,19},{4,20},{5,21},{6,22},{7,23},{8,24},{9,... | collective-permute-start | bytes 1572872 | tf_op jit(solution)/shard_map/ppermute | solution.py:211
  83.9 13.4 %collective-permute-done.20 = f32[512,256]{1,0:T(8,128)S(1)} collective-permute-done((f32[512,256]{1,0:T(8,128)S(1)}, f32[512,256]{1,0:T(8,128)S(1)}, u32[]{:S(2)}, u32[]{:S(2)}) %collective-permute-start.20) | collective-permute-done | bytes 524320 | tf_op jit(solution)/shard_map/ppermute | solution.py:211
  99.9 3.0 %shard_map.70 = (f32[512,256]{1,0:T(8,128)S(1)}, f32[512,256]{1,0:T(8,128)}, f32[512,256]{1,0:T(8,128)}) custom-call(s32[4]{0:T(128)S(1)} %pad_add_fusion.where_ref, f32[512,256]{1,0:T(8,128)S(1)} %slice_bitcast_fusion.2.refs_0_, f32[512,256]{1,0:T(8,128)S(1)} %collective-permute-done.15.refs_1_, f32[512,256]{1,0:T(8,128)S(1)} %collective-permute-done.16.refs_2_, ...), custom_call_target="tpu_custom_call" | custom-call | flops 805306368 | bytes 5242880 | tf_op jit(solution)/shard_map/pallas_call | solution.py:36
  105.7 5.5 %collective-permute-start.25 = (f32[512,256]{1,0:T(8,128)}, f32[512,256]{1,0:T(8,128)}, u32[]{:S(2)}, u32[]{:S(2)}) collective-permute-start(f32[512,256]{1,0:T(8,128)} %get-tuple-element.54), channel_id=1, source_target_pairs={{0,4},{1,5},{10,14},{11,15},{16,20},{17,21},{26,30},{27,31}} | collective-permute-start | bytes 1572872 | tf_op jit(solution)/shard_map/ppermute | solution.py:211
  117.1 4.9 %shard_map.71 = (f32[1024,128]{1,0:T(8,128)S(1)}, f32[1024,128]{1,0:T(8,128)S(1)}, f32[1024,128]{1,0:T(8,128)S(1)}, f32[1024,128]{1,0:T(8,128)S(1)}) custom-call(s32[6]{0:T(128)S(1)} %stack.50.where_ref, f32[1024,256]{1,0:T(8,128)S(1)} %copy-done.1, f32[1024,256]{1,0:T(8,128)S(1)} %copy-done.6, f32[512,256]{1,0:T(8,128)} %get-tuple-element.45.refs_2_, ...), custom_call_target="tpu_custom_call" | custom-call | flops 4831838208 | bytes 5242880 | tf_op jit(solution)/shard_map/pallas_call | solution.py:36
  127.4 13.4 %collective-permute-start.29 = (f32[512,128]{1,0:T(8,128)S(1)}, f32[512,128]{1,0:T(8,128)S(1)}, u32[]{:S(2)}, u32[]{:S(2)}) collective-permute-start(f32[512,128]{1,0:T(8,128)S(1)} %constant_dynamic-slice_fusion), channel_id=1, source_target_pairs={{0,0},{1,1},{2,8},{3,9},{4,16},{5,17},{6,24},{7,25},{8,2},{9,3},{1... | collective-permute-start | bytes 786440 | tf_op jit(solution)/shard_map/ppermute | solution.py:211
  140.8 7.1 %collective-permute-done.29 = f32[512,128]{1,0:T(8,128)S(1)} collective-permute-done((f32[512,128]{1,0:T(8,128)S(1)}, f32[512,128]{1,0:T(8,128)S(1)}, u32[]{:S(2)}, u32[]{:S(2)}) %collective-permute-start.29) | collective-permute-done | bytes 262176 | tf_op jit(solution)/shard_map/ppermute | solution.py:211
  158.8 3.7 %shard_map.73 = (f32[1024,128]{1,0:T(8,128)S(1)}, f32[1024,128]{1,0:T(8,128)S(1)}, f32[1024,128]{1,0:T(8,128)S(1)}) custom-call(s32[6]{0:T(128)S(1)} %stack.50.where_ref, f32[1024,256]{1,0:T(8,128)S(1)} %get-tuple-element.65.refs_0_, f32[1024,256]{1,0:T(8,128)S(1)} %collective-permute-done.26.refs_1_, f32[512,256]{1,0:T(8,128)S(1)} %add_add_fusion.refs_2_, ...), custom_call_target="tpu_custom_call" | custom-call | flops 3623878656 | bytes 7340032 | tf_op jit(solution)/shard_map/pallas_call | solution.py:36
  162.5 5.6 %collective-permute-done.34 = f32[1024,128]{1,0:T(8,128)S(1)} collective-permute-done((f32[1024,128]{1,0:T(8,128)S(1)}, f32[1024,128]{1,0:T(8,128)S(1)}, u32[]{:S(2)}, u32[]{:S(2)}) %collective-permute-start.34) | collective-permute-done | bytes 524320 | tf_op jit(solution)/shard_map/ppermute | solution.py:211
  170.2 3.6 %collective-permute-done.31 = f32[512,128]{1,0:T(8,128)S(1)} collective-permute-done((f32[512,128]{1,0:T(8,128)S(1)}, f32[512,128]{1,0:T(8,128)S(1)}, u32[]{:S(2)}, u32[]{:S(2)}) %collective-permute-start.31) | collective-permute-done | bytes 262176 | tf_op jit(solution)/shard_map/ppermute | solution.py:211
  174.6 19.3 %collective-permute-done.36 = f32[1024,128]{1,0:T(8,128)S(1)} collective-permute-done((f32[1024,128]{1,0:T(8,128)S(1)}, f32[1024,128]{1,0:T(8,128)S(1)}, u32[]{:S(2)}, u32[]{:S(2)}) %collective-permute-start.36) | collective-permute-done | bytes 524320 | tf_op jit(solution)/shard_map/ppermute | solution.py:211
  193.9 3.3 %collective-permute-done.35 = f32[1024,128]{1,0:T(8,128)S(1)} collective-permute-done((f32[1024,128]{1,0:T(8,128)S(1)}, f32[1024,128]{1,0:T(8,128)S(1)}, u32[]{:S(2)}, u32[]{:S(2)}) %collective-permute-start.35) | collective-permute-done | bytes 524320 | tf_op jit(solution)/shard_map/ppermute | solution.py:211
  (114 shorter events, 53.9 us)
Async XLA Ops:
  5.7 17.9 %collective-permute-start = (f32[512,128]{1,0:T(8,128)S(1)}, f32[512,128]{1,0:T(8,128)S(1)}, u32[]{:S(2)}, u32[]{:S(2)}) collective-permute-start(f32[512,128]{1,0:T(8,128)S(1)} %get-tuple-element.75), channel_id=1, source_target_pairs={{0,0},{1,1},{2,8},{3,9},{4,16},{5,17},{6,24},{7,25},{8,2},{9,3},{1... | collective-permute-start | bytes 786440 | tf_op jit(solution)/shard_map/ppermute | solution.py:211
  11.6 15.5 %collective-permute-start.9 = (f32[256,256]{1,0:T(8,128)S(1)}, f32[256,256]{1,0:T(8,128)S(1)}, u32[]{:S(2)}, u32[]{:S(2)}) collective-permute-start(f32[256,256]{1,0:T(8,128)S(1)} %get-tuple-element.73.refs_0_), channel_id=1, source_target_pairs={{0,16},{1,17},{2,18},{3,19},{4,20},{5,21},{6,22},{7,23},{8,24},{9,... | collective-permute-start | bytes 786440 | tf_op jit(solution)/shard_map/ppermute | solution.py:211
  11.7 19.6 %collective-permute-start.6 = (f32[256,256]{1,0:T(8,128)S(1)}, f32[256,256]{1,0:T(8,128)S(1)}, u32[]{:S(2)}, u32[]{:S(2)}) collective-permute-start(f32[256,256]{1,0:T(8,128)S(1)} %collective-permute-done.1.refs_2_), channel_id=1, source_target_pairs={{0,16},{1,17},{2,18},{3,19},{4,20},{5,21},{6,22},{7,23},{8,24},{9,... | collective-permute-start | bytes 786440 | tf_op jit(solution)/shard_map/ppermute | solution.py:211
  13.7 17.6 %collective-permute-start.7 = (f32[256,256]{1,0:T(8,128)S(1)}, f32[256,256]{1,0:T(8,128)S(1)}, u32[]{:S(2)}, u32[]{:S(2)}) collective-permute-start(f32[256,256]{1,0:T(8,128)S(1)} %collective-permute-done.2.refs_3_), channel_id=1, source_target_pairs={{0,1},{1,0},{2,3},{3,2},{4,5},{5,4},{6,7},{7,6},{8,9},{9,8},{10,11... | collective-permute-start | bytes 786440 | tf_op jit(solution)/shard_map/ppermute | solution.py:211
  23.6 17.1 %collective-permute-start.11 = (f32[512,128]{1,0:T(8,128)}, f32[512,128]{1,0:T(8,128)S(1)}, u32[]{:S(2)}, u32[]{:S(2)}) collective-permute-start(f32[512,128]{1,0:T(8,128)} %get-tuple-element.41), channel_id=1, source_target_pairs={{0,0},{1,1},{2,8},{3,9},{4,16},{5,17},{6,24},{7,25},{8,2},{9,3},{1... | collective-permute-start | bytes 786440 | tf_op jit(solution)/shard_map/ppermute | solution.py:211
  27.1 16.4 %collective-permute-start.3 = (f32[512,256]{1,0:T(8,128)S(1)}, f32[512,256]{1,0:T(8,128)S(1)}, u32[]{:S(2)}, u32[]{:S(2)}) collective-permute-start(f32[512,256]{1,0:T(8,128)S(1)} %copy-done.2), channel_id=1, source_target_pairs={{0,1},{1,0},{2,3},{3,2},{4,5},{5,4},{6,7},{7,6},{8,9},{9,8},{10,11... | collective-permute-start | bytes 1572872 | tf_op jit(solution)/shard_map/ppermute | solution.py:211
  31.3 18.6 %collective-permute-start.4 = (f32[512,256]{1,0:T(8,128)S(1)}, f32[512,256]{1,0:T(8,128)S(1)}, u32[]{:S(2)}, u32[]{:S(2)}) collective-permute-start(f32[512,256]{1,0:T(8,128)S(1)} %copy-done.2), channel_id=1, source_target_pairs={{0,16},{1,17},{2,18},{3,19},{4,20},{5,21},{6,22},{7,23},{8,24},{9,... | collective-permute-start | bytes 1572872 | tf_op jit(solution)/shard_map/ppermute | solution.py:211
  42.9 32.7 %collective-permute-start.22 = (f32[1024,256]{1,0:T(8,128)S(1)}, f32[1024,256]{1,0:T(8,128)S(1)}, u32[]{:S(2)}, u32[]{:S(2)}) collective-permute-start(f32[1024,256]{1,0:T(8,128)S(1)} %get-tuple-element.51.refs_0_), channel_id=1, source_target_pairs={{0,1},{1,0},{2,3},{3,2},{4,5},{5,4},{6,7},{7,6},{8,9},{9,8},{10,11... | collective-permute-start | bytes 3145736 | tf_op jit(solution)/shard_map/ppermute | solution.py:211
  63.4 16.0 %collective-permute-start.15 = (f32[512,256]{1,0:T(8,128)S(1)}, f32[512,256]{1,0:T(8,128)S(1)}, u32[]{:S(2)}, u32[]{:S(2)}) collective-permute-start(f32[512,256]{1,0:T(8,128)S(1)} %slice_bitcast_fusion.2.refs_0_), channel_id=1, source_target_pairs={{0,1},{1,0},{2,3},{3,2},{4,5},{5,4},{6,7},{7,6},{8,9},{9,8},{10,11... | collective-permute-start | bytes 1572872 | tf_op jit(solution)/shard_map/ppermute | solution.py:211
  64.3 15.6 %collective-permute-start.16 = (f32[512,256]{1,0:T(8,128)S(1)}, f32[512,256]{1,0:T(8,128)S(1)}, u32[]{:S(2)}, u32[]{:S(2)}) collective-permute-start(f32[512,256]{1,0:T(8,128)S(1)} %slice_bitcast_fusion.2.refs_0_), channel_id=1, source_target_pairs={{0,16},{1,17},{2,18},{3,19},{4,20},{5,21},{6,22},{7,23},{8,24},{9,... | collective-permute-start | bytes 1572872 | tf_op jit(solution)/shard_map/ppermute | solution.py:211
  67.6 16.2 %collective-permute-start.21 = (f32[512,256]{1,0:T(8,128)S(1)}, f32[512,256]{1,0:T(8,128)S(1)}, u32[]{:S(2)}, u32[]{:S(2)}) collective-permute-start(f32[512,256]{1,0:T(8,128)S(1)} %get-tuple-element.50), channel_id=1, source_target_pairs={{2,0},{3,1},{6,4},{7,5},{8,10},{9,11},{12,14},{13,15},{18,16},{19,... | collective-permute-start | bytes 1572872 | tf_op jit(solution)/shard_map/ppermute | solution.py:211
  68.9 28.3 %collective-permute-start.20 = (f32[512,256]{1,0:T(8,128)S(1)}, f32[512,256]{1,0:T(8,128)S(1)}, u32[]{:S(2)}, u32[]{:S(2)}) collective-permute-start(f32[512,256]{1,0:T(8,128)S(1)} %get-tuple-element.49), channel_id=1, source_target_pairs={{0,4},{1,5},{4,0},{5,1},{10,14},{11,15},{14,10},{15,11},{16,20},{1... | collective-permute-start | bytes 1572872 | tf_op jit(solution)/shard_map/ppermute | solution.py:211
  76.6 20.6 %collective-permute-start.19 = (f32[512,256]{1,0:T(8,128)S(1)}, f32[512,256]{1,0:T(8,128)S(1)}, u32[]{:S(2)}, u32[]{:S(2)}) collective-permute-start(f32[512,256]{1,0:T(8,128)S(1)} %get-tuple-element.49), channel_id=1, source_target_pairs={{2,4},{3,5},{6,0},{7,1},{8,14},{9,15},{12,10},{13,11},{18,20},{19,... | collective-permute-start | bytes 1572872 | tf_op jit(solution)/shard_map/ppermute | solution.py:211
  79.4 24.8 %collective-permute-start.26 = (f32[1024,256]{1,0:T(8,128)S(1)}, f32[1024,256]{1,0:T(8,128)S(1)}, u32[]{:S(2)}, u32[]{:S(2)}) collective-permute-start(f32[1024,256]{1,0:T(8,128)S(1)} %get-tuple-element.65.refs_0_), channel_id=1, source_target_pairs={{0,1},{1,0},{2,3},{3,2},{4,5},{5,4},{6,7},{7,6},{8,9},{9,8},{10,11... | collective-permute-start | bytes 3145736 | tf_op jit(solution)/shard_map/ppermute | solution.py:211
  79.9 19.9 %collective-permute-start.17 = (f32[512,256]{1,0:T(8,128)S(1)}, f32[512,256]{1,0:T(8,128)S(1)}, u32[]{:S(2)}, u32[]{:S(2)}) collective-permute-start(f32[512,256]{1,0:T(8,128)S(1)} %collective-permute-done.15.refs_1_), channel_id=1, source_target_pairs={{0,16},{1,17},{2,18},{3,19},{4,20},{5,21},{6,22},{7,23},{8,24},{9,... | collective-permute-start | bytes 1572872 | tf_op jit(solution)/shard_map/ppermute | solution.py:211
  97.5 15.3 %collective-permute-start.28 = (f32[512,256]{1,0:T(8,128)}, f32[512,256]{1,0:T(8,128)S(1)}, u32[]{:S(2)}, u32[]{:S(2)}) collective-permute-start(f32[512,256]{1,0:T(8,128)} %get-tuple-element.45.refs_2_), channel_id=1, source_target_pairs={{0,16},{1,17},{2,18},{3,19},{4,20},{5,21},{6,22},{7,23},{8,24},{9,... | collective-permute-start | bytes 1572872 | tf_op jit(solution)/shard_map/ppermute | solution.py:211
  104.2 18.6 %collective-permute-start.27 = (f32[512,256]{1,0:T(8,128)}, f32[512,256]{1,0:T(8,128)}, u32[]{:S(2)}, u32[]{:S(2)}) collective-permute-start(f32[512,256]{1,0:T(8,128)} %get-tuple-element.57), channel_id=1, source_target_pairs={{8,10},{9,11},{12,14},{13,15},{24,26},{25,27},{28,30},{29,31}} | collective-permute-start | bytes 1572872 | tf_op jit(solution)/shard_map/ppermute | solution.py:211
  105.7 17.5 %collective-permute-start.25 = (f32[512,256]{1,0:T(8,128)}, f32[512,256]{1,0:T(8,128)}, u32[]{:S(2)}, u32[]{:S(2)}) collective-permute-start(f32[512,256]{1,0:T(8,128)} %get-tuple-element.54), channel_id=1, source_target_pairs={{0,4},{1,5},{10,14},{11,15},{16,20},{17,21},{26,30},{27,31}} | collective-permute-start | bytes 1572872 | tf_op jit(solution)/shard_map/ppermute | solution.py:211
  124.9 23.1 %collective-permute-start.32 = (f32[512,256]{1,0:T(8,128)S(1)}, f32[512,256]{1,0:T(8,128)S(1)}, u32[]{:S(2)}, u32[]{:S(2)}) collective-permute-start(f32[512,256]{1,0:T(8,128)S(1)} %add_add_fusion.refs_2_), channel_id=1, source_target_pairs={{0,16},{1,17},{2,18},{3,19},{4,20},{5,21},{6,22},{7,23},{8,24},{9,... | collective-permute-start | bytes 1572872 | tf_op jit(solution)/shard_map/ppermute | solution.py:211
  127.4 20.6 %collective-permute-start.29 = (f32[512,128]{1,0:T(8,128)S(1)}, f32[512,128]{1,0:T(8,128)S(1)}, u32[]{:S(2)}, u32[]{:S(2)}) collective-permute-start(f32[512,128]{1,0:T(8,128)S(1)} %constant_dynamic-slice_fusion), channel_id=1, source_target_pairs={{0,0},{1,1},{2,8},{3,9},{4,16},{5,17},{6,24},{7,25},{8,2},{9,3},{1... | collective-permute-start | bytes 786440 | tf_op jit(solution)/shard_map/ppermute | solution.py:211
  153.0 15.2 %collective-permute-start.34 = (f32[1024,128]{1,0:T(8,128)S(1)}, f32[1024,128]{1,0:T(8,128)S(1)}, u32[]{:S(2)}, u32[]{:S(2)}) collective-permute-start(f32[1024,128]{1,0:T(8,128)S(1)} %shard_map.72), channel_id=1, source_target_pairs={{0,2},{1,3},{2,0},{3,1},{4,6},{5,7},{6,4},{7,5},{8,10},{9,11},{10,... | collective-permute-start | bytes 1572872 | tf_op jit(solution)/shard_map/ppermute | solution.py:211
  155.9 17.9 %collective-permute-start.31 = (f32[512,128]{1,0:T(8,128)S(1)}, f32[512,128]{1,0:T(8,128)S(1)}, u32[]{:S(2)}, u32[]{:S(2)}) collective-permute-start(f32[512,128]{1,0:T(8,128)S(1)} %dynamic-slice_add_fusion), channel_id=1, source_target_pairs={{0,0},{1,1},{2,8},{3,9},{4,16},{5,17},{6,24},{7,25},{8,2},{9,3},{1... | collective-permute-start | bytes 786440 | tf_op jit(solution)/shard_map/ppermute | solution.py:211
  168.2 25.7 %collective-permute-start.36 = (f32[1024,128]{1,0:T(8,128)S(1)}, f32[1024,128]{1,0:T(8,128)S(1)}, u32[]{:S(2)}, u32[]{:S(2)}) collective-permute-start(f32[1024,128]{1,0:T(8,128)S(1)} %add.97), channel_id=1, source_target_pairs={{0,4},{1,5},{2,6},{3,7},{4,0},{5,1},{6,2},{7,3},{8,12},{9,13},{10,... | collective-permute-start | bytes 1572872 | tf_op jit(solution)/shard_map/ppermute | solution.py:211
  173.8 23.4 %collective-permute-start.35 = (f32[1024,128]{1,0:T(8,128)S(1)}, f32[1024,128]{1,0:T(8,128)S(1)}, u32[]{:S(2)}, u32[]{:S(2)}) collective-permute-start(f32[1024,128]{1,0:T(8,128)S(1)} %get-tuple-element.69), channel_id=1, source_target_pairs={{0,2},{1,3},{2,0},{3,1},{4,6},{5,7},{6,4},{7,5},{8,10},{9,11},{10,... | collective-permute-start | bytes 1572872 | tf_op jit(solution)/shard_map/ppermute | solution.py:211
  (35 other events, 287.2 us)

commit v6 on v5

--- a/solution.py
+++ b/solution.py
@@ -310,7 +310,7 @@
         held = after(coupling, *early)
         coupled = grid.gather_b(held)
         coupled |= {(k // 2, 0): grid.row_bit(held, k) for k in range(2, rows, 2)}
-        record_two = grid.swap(after(top_rhs[1], *early))
+        record_two = grid.swap(after(top_rhs[1], record_one))
         first_in = grid.both(record_one)
         _, blocks = run(inverse_one, *first_in, record=True)
         blocks = together(*blocks, record_two)[:rows]
@@ -333,7 +333,7 @@
         total = grid.send(blocks, False)
         total = after(total, *earlier.values())
         mine = functools.partial(lax.dynamic_slice_in_dim, start_index=r % 2 * width, slice_size=width, axis=1)
-        solved_one = grid.swap(after(mine(first), total))
+        solved_one = grid.swap(mine(first))
         far = [after(grid.row_bit(total, k), solved_one) for k in range(2, rows, 2)]
         seconds = [list(grid.both(value)) for value in [total, *far]]
         solved_two = grid.swap(mine(seconds[0][0] + seconds[0][1]))

time: 201 us -> 201 us (level)
  no operation moved by 1% of the time
where the time goes in v6:
time: 201 us; the launch traced here: 198 us
  waiting for transfers between devices  89.7 us (45%)
  starting transfers between devices  69.2 us (34%)
  Pallas kernels  19.7 us (10%)
  local copies, waits for them, and re-layouts  14.7 us (7%)
  other arithmetic  3.83 us (2%)
    ppermute x37, waiting for transfers between devices, move(): return lax.ppermute(value, ('row', 'col'), pairs)  89.7 us
    ppermute x37, starting transfers between devices, move(): return lax.ppermute(value, ('row', 'col'), pairs)  69.2 us
    pallas_call x6, Pallas kernels, call(): pl.pallas_call(kernel, out_shape=outs, in_specs=[SMEM] + [HBM] * len(oper...  19.7 us
    unnamed x44, local copies, waits for them, and re-layouts  10.5 us
  transfers between devices with their start and end apart: 37, of which 17 were waited for; matrix products, arithmetic and copies ran while one was open for 2% of the time, Pallas kernels for 9%

profile of v6, /device:TPU:2, one launch (start us, length us, event | category | flops | bytes accessed | tf_op | source)
XLA Modules:
  0.0 198.1 jit_solution(3020622339905746565)
XLA Ops:
  5.7 5.4 %collective-permute-start = (f32[512,128]{1,0:T(8,128)S(1)}, f32[512,128]{1,0:T(8,128)S(1)}, u32[]{:S(2)}, u32[]{:S(2)}) collective-permute-start(f32[512,128]{1,0:T(8,128)S(1)} %get-tuple-element.73), channel_id=1, source_target_pairs={{0,0},{1,1},{2,8},{3,9},{4,16},{5,17},{6,24},{7,25},{8,2},{9,3},{1... | collective-permute-start | bytes 786440 | tf_op jit(solution)/shard_map/ppermute | solution.py:211
  15.2 8.4 %collective-permute-done.refs_8_ = f32[512,128]{1,0:T(8,128)S(1)} collective-permute-done((f32[512,128]{1,0:T(8,128)S(1)}, f32[512,128]{1,0:T(8,128)S(1)}, u32[]{:S(2)}, u32[]{:S(2)}) %collective-permute-start) | collective-permute-done | bytes 262176 | tf_op jit(solution)/shard_map/ppermute | solution.py:211
  23.6 3.4 %collective-permute-start.11 = (f32[512,128]{1,0:T(8,128)}, f32[512,128]{1,0:T(8,128)S(1)}, u32[]{:S(2)}, u32[]{:S(2)}) collective-permute-start(f32[512,128]{1,0:T(8,128)} %get-tuple-element.40), channel_id=1, source_target_pairs={{0,0},{1,1},{2,8},{3,9},{4,16},{5,17},{6,24},{7,25},{8,2},{9,3},{1... | collective-permute-start | bytes 786440 | tf_op jit(solution)/shard_map/ppermute | solution.py:211
  27.7 3.6 %collective-permute-done.6.refs_4_ = f32[256,256]{1,0:T(8,128)S(1)} collective-permute-done((f32[256,256]{1,0:T(8,128)S(1)}, f32[256,256]{1,0:T(8,128)S(1)}, u32[]{:S(2)}, u32[]{:S(2)}) %collective-permute-start.6) | collective-permute-done | bytes 262176 | tf_op jit(solution)/shard_map/ppermute | solution.py:211
  34.6 3.0 %shard_map.68 = (f32[512,256]{1,0:T(8,128)S(1)}, f32[512,256]{1,0:T(8,128)S(1)}, f32[512,256]{1,0:T(8,128)S(1)}) custom-call(s32[4]{0:T(128)S(1)} %pad_add_fusion.where_ref, f32[256,256]{1,0:T(8,128)S(1)} %get-tuple-element.71.refs_0_, f32[256,256]{1,0:T(8,128)S(1)} %get-tuple-element.70.refs_1_, f32[256,256]{1,0:T(8,128)S(1)} %collective-permute-done.1.refs_2_, ...), custom_call_target="tpu_custom_call" | custom-call | flops 805306368 | bytes 4194304 | tf_op jit(solution)/shard_map/pallas_call | solution.py:36
  37.6 3.1 %collective-permute-done.11.refs_4_ = f32[512,128]{1,0:T(8,128)S(1)} collective-permute-done((f32[512,128]{1,0:T(8,128)}, f32[512,128]{1,0:T(8,128)S(1)}, u32[]{:S(2)}, u32[]{:S(2)}) %collective-permute-start.11) | collective-permute-done | bytes 262176 | tf_op jit(solution)/shard_map/ppermute | solution.py:211
  43.5 6.3 %collective-permute-done.4.refs_2_ = f32[512,256]{1,0:T(8,128)S(1)} collective-permute-done((f32[512,256]{1,0:T(8,128)S(1)}, f32[512,256]{1,0:T(8,128)S(1)}, u32[]{:S(2)}, u32[]{:S(2)}) %collective-permute-start.4) | collective-permute-done | bytes 524320 | tf_op jit(solution)/shard_map/ppermute | solution.py:211
  49.9 5.2 %collective-permute-done.12 = f32[512,256]{1,0:T(8,128)S(1)} collective-permute-done((f32[512,256]{1,0:T(8,128)S(1)}, f32[512,256]{1,0:T(8,128)S(1)}, u32[]{:S(2)}, u32[]{:S(2)}) %collective-permute-start.12) | collective-permute-done | bytes 524320 | tf_op jit(solution)/shard_map/ppermute | solution.py:211
  55.2 3.9 %collective-permute-start.14 = (f32[512,256]{1,0:T(8,128)S(1)}, f32[512,256]{1,0:T(8,128)S(1)}, u32[]{:S(2)}, u32[]{:S(2)}) collective-permute-start(f32[512,256]{1,0:T(8,128)S(1)} %add_add_fusion.2.refs_4_), channel_id=1, source_target_pairs={{0,8},{1,9},{2,10},{3,11},{4,12},{5,13},{6,14},{7,15},{8,0},{9,1},... | collective-permute-start | bytes 1572872 | tf_op jit(solution)/shard_map/ppermute | solution.py:211
  59.1 4.3 %collective-permute-done.5.refs_3_ = f32[512,256]{1,0:T(8,128)S(1)} collective-permute-done((f32[512,256]{1,0:T(8,128)S(1)}, f32[512,256]{1,0:T(8,128)S(1)}, u32[]{:S(2)}, u32[]{:S(2)}) %collective-permute-start.5) | collective-permute-done | bytes 524320 | tf_op jit(solution)/shard_map/ppermute | solution.py:211
  64.6 3.0 %shard_map.69 = (f32[512,256]{1,0:T(8,128)}, f32[512,256]{1,0:T(8,128)S(1)}, f32[512,256]{1,0:T(8,128)S(1)}, f32[512,256]{1,0:T(8,128)S(1)}) custom-call(s32[4]{0:T(128)S(1)} %pad_add_fusion.where_ref, f32[512,256]{1,0:T(8,128)S(1)} %copy-done.2, f32[512,256]{1,0:T(8,128)S(1)} %collective-permute-done.3.refs_1_, ...), custom_call_target="tpu_custom_call" | custom-call | flops 805306368 | bytes 5242880 | tf_op jit(solution)/shard_map/pallas_call | solution.py:36
  68.9 6.7 %collective-permute-start.21 = (f32[512,256]{1,0:T(8,128)S(1)}, f32[512,256]{1,0:T(8,128)S(1)}, u32[]{:S(2)}, u32[]{:S(2)}) collective-permute-start(f32[512,256]{1,0:T(8,128)S(1)} %get-tuple-element.48), channel_id=1, source_target_pairs={{0,4},{1,5},{4,0},{5,1},{10,14},{11,15},{14,10},{15,11},{16,20},{1... | collective-permute-start | bytes 1572872 | tf_op jit(solution)/shard_map/ppermute | solution.py:211
  79.9 3.9 %collective-permute-start.18 = (f32[512,256]{1,0:T(8,128)S(1)}, f32[512,256]{1,0:T(8,128)S(1)}, u32[]{:S(2)}, u32[]{:S(2)}) collective-permute-start(f32[512,256]{1,0:T(8,128)S(1)} %collective-permute-done.16.refs_1_), channel_id=1, source_target_pairs={{0,16},{1,17},{2,18},{3,19},{4,20},{5,21},{6,22},{7,23},{8,24},{9,... | collective-permute-start | bytes 1572872 | tf_op jit(solution)/shard_map/ppermute | solution.py:211
  83.9 13.4 %collective-permute-done.21 = f32[512,256]{1,0:T(8,128)S(1)} collective-permute-done((f32[512,256]{1,0:T(8,128)S(1)}, f32[512,256]{1,0:T(8,128)S(1)}, u32[]{:S(2)}, u32[]{:S(2)}) %collective-permute-start.21) | collective-permute-done | bytes 524320 | tf_op jit(solution)/shard_map/ppermute | solution.py:211
  99.9 3.0 %shard_map.70 = (f32[512,256]{1,0:T(8,128)S(1)}, f32[512,256]{1,0:T(8,128)}, f32[512,256]{1,0:T(8,128)}) custom-call(s32[4]{0:T(128)S(1)} %pad_add_fusion.where_ref, f32[512,256]{1,0:T(8,128)S(1)} %slice_bitcast_fusion.2.refs_0_, f32[512,256]{1,0:T(8,128)S(1)} %collective-permute-done.16.refs_1_, f32[512,256]{1,0:T(8,128)S(1)} %collective-permute-done.17.refs_2_, ...), custom_call_target="tpu_custom_call" | custom-call | flops 805306368 | bytes 5242880 | tf_op jit(solution)/shard_map/pallas_call | solution.py:36
  105.7 5.5 %collective-permute-start.26 = (f32[512,256]{1,0:T(8,128)}, f32[512,256]{1,0:T(8,128)}, u32[]{:S(2)}, u32[]{:S(2)}) collective-permute-start(f32[512,256]{1,0:T(8,128)} %get-tuple-element.53), channel_id=1, source_target_pairs={{0,4},{1,5},{10,14},{11,15},{16,20},{17,21},{26,30},{27,31}} | collective-permute-start | bytes 1572872 | tf_op jit(solution)/shard_map/ppermute | solution.py:211
  117.1 4.9 %shard_map.71 = (f32[1024,128]{1,0:T(8,128)S(1)}, f32[1024,128]{1,0:T(8,128)S(1)}, f32[1024,128]{1,0:T(8,128)S(1)}, f32[1024,128]{1,0:T(8,128)S(1)}) custom-call(s32[6]{0:T(128)S(1)} %stack.51.where_ref, f32[1024,256]{1,0:T(8,128)S(1)} %copy-done.1, f32[1024,256]{1,0:T(8,128)S(1)} %copy-done.6, f32[512,256]{1,0:T(8,128)} %get-tuple-element.44.refs_2_, ...), custom_call_target="tpu_custom_call" | custom-call | flops 4831838208 | bytes 5242880 | tf_op jit(solution)/shard_map/pallas_call | solution.py:36
  127.4 13.4 %collective-permute-start.15 = (f32[512,128]{1,0:T(8,128)S(1)}, f32[512,128]{1,0:T(8,128)S(1)}, u32[]{:S(2)}, u32[]{:S(2)}) collective-permute-start(f32[512,128]{1,0:T(8,128)S(1)} %constant_dynamic-slice_fusion), channel_id=1, source_target_pairs={{0,0},{1,1},{2,8},{3,9},{4,16},{5,17},{6,24},{7,25},{8,2},{9,3},{1... | collective-permute-start | bytes 786440 | tf_op jit(solution)/shard_map/ppermute | solution.py:211
  140.8 7.1 %collective-permute-done.15 = f32[512,128]{1,0:T(8,128)S(1)} collective-permute-done((f32[512,128]{1,0:T(8,128)S(1)}, f32[512,128]{1,0:T(8,128)S(1)}, u32[]{:S(2)}, u32[]{:S(2)}) %collective-permute-start.15) | collective-permute-done | bytes 262176 | tf_op jit(solution)/shard_map/ppermute | solution.py:211
  158.8 3.7 %shard_map.73 = (f32[1024,128]{1,0:T(8,128)S(1)}, f32[1024,128]{1,0:T(8,128)S(1)}, f32[1024,128]{1,0:T(8,128)S(1)}) custom-call(s32[6]{0:T(128)S(1)} %stack.51.where_ref, f32[1024,256]{1,0:T(8,128)S(1)} %get-tuple-element.63.refs_0_, f32[1024,256]{1,0:T(8,128)S(1)} %collective-permute-done.27.refs_1_, f32[512,256]{1,0:T(8,128)S(1)} %add_add_fusion.refs_2_, ...), custom_call_target="tpu_custom_call" | custom-call | flops 3623878656 | bytes 7340032 | tf_op jit(solution)/shard_map/pallas_call | solution.py:36
  162.5 5.6 %collective-permute-done.34 = f32[1024,128]{1,0:T(8,128)S(1)} collective-permute-done((f32[1024,128]{1,0:T(8,128)S(1)}, f32[1024,128]{1,0:T(8,128)S(1)}, u32[]{:S(2)}, u32[]{:S(2)}) %collective-permute-start.34) | collective-permute-done | bytes 524320 | tf_op jit(solution)/shard_map/ppermute | solution.py:211
  170.2 3.6 %collective-permute-done.31 = f32[512,128]{1,0:T(8,128)S(1)} collective-permute-done((f32[512,128]{1,0:T(8,128)S(1)}, f32[512,128]{1,0:T(8,128)S(1)}, u32[]{:S(2)}, u32[]{:S(2)}) %collective-permute-start.31) | collective-permute-done | bytes 262176 | tf_op jit(solution)/shard_map/ppermute | solution.py:211
  174.6 19.3 %collective-permute-done.36 = f32[1024,128]{1,0:T(8,128)S(1)} collective-permute-done((f32[1024,128]{1,0:T(8,128)S(1)}, f32[1024,128]{1,0:T(8,128)S(1)}, u32[]{:S(2)}, u32[]{:S(2)}) %collective-permute-start.36) | collective-permute-done | bytes 524320 | tf_op jit(solution)/shard_map/ppermute | solution.py:211
  193.9 3.3 %collective-permute-done.35 = f32[1024,128]{1,0:T(8,128)S(1)} collective-permute-done((f32[1024,128]{1,0:T(8,128)S(1)}, f32[1024,128]{1,0:T(8,128)S(1)}, u32[]{:S(2)}, u32[]{:S(2)}) %collective-permute-start.35) | collective-permute-done | bytes 524320 | tf_op jit(solution)/shard_map/ppermute | solution.py:211
  (114 shorter events, 53.9 us)
Async XLA Ops:
  5.7 17.9 %collective-permute-start = (f32[512,128]{1,0:T(8,128)S(1)}, f32[512,128]{1,0:T(8,128)S(1)}, u32[]{:S(2)}, u32[]{:S(2)}) collective-permute-start(f32[512,128]{1,0:T(8,128)S(1)} %get-tuple-element.73), channel_id=1, source_target_pairs={{0,0},{1,1},{2,8},{3,9},{4,16},{5,17},{6,24},{7,25},{8,2},{9,3},{1... | collective-permute-start | bytes 786440 | tf_op jit(solution)/shard_map/ppermute | solution.py:211
  11.6 15.5 %collective-permute-start.9 = (f32[256,256]{1,0:T(8,128)S(1)}, f32[256,256]{1,0:T(8,128)S(1)}, u32[]{:S(2)}, u32[]{:S(2)}) collective-permute-start(f32[256,256]{1,0:T(8,128)S(1)} %get-tuple-element.71.refs_0_), channel_id=1, source_target_pairs={{0,16},{1,17},{2,18},{3,19},{4,20},{5,21},{6,22},{7,23},{8,24},{9,... | collective-permute-start | bytes 786440 | tf_op jit(solution)/shard_map/ppermute | solution.py:211
  11.7 19.6 %collective-permute-start.6 = (f32[256,256]{1,0:T(8,128)S(1)}, f32[256,256]{1,0:T(8,128)S(1)}, u32[]{:S(2)}, u32[]{:S(2)}) collective-permute-start(f32[256,256]{1,0:T(8,128)S(1)} %collective-permute-done.1.refs_2_), channel_id=1, source_target_pairs={{0,16},{1,17},{2,18},{3,19},{4,20},{5,21},{6,22},{7,23},{8,24},{9,... | collective-permute-start | bytes 786440 | tf_op jit(solution)/shard_map/ppermute | solution.py:211
  13.7 17.6 %collective-permute-start.7 = (f32[256,256]{1,0:T(8,128)S(1)}, f32[256,256]{1,0:T(8,128)S(1)}, u32[]{:S(2)}, u32[]{:S(2)}) collective-permute-start(f32[256,256]{1,0:T(8,128)S(1)} %collective-permute-done.2.refs_3_), channel_id=1, source_target_pairs={{0,1},{1,0},{2,3},{3,2},{4,5},{5,4},{6,7},{7,6},{8,9},{9,8},{10,11... | collective-permute-start | bytes 786440 | tf_op jit(solution)/shard_map/ppermute | solution.py:211
  23.6 17.1 %collective-permute-start.11 = (f32[512,128]{1,0:T(8,128)}, f32[512,128]{1,0:T(8,128)S(1)}, u32[]{:S(2)}, u32[]{:S(2)}) collective-permute-start(f32[512,128]{1,0:T(8,128)} %get-tuple-element.40), channel_id=1, source_target_pairs={{0,0},{1,1},{2,8},{3,9},{4,16},{5,17},{6,24},{7,25},{8,2},{9,3},{1... | collective-permute-start | bytes 786440 | tf_op jit(solution)/shard_map/ppermute | solution.py:211
  27.1 16.4 %collective-permute-start.3 = (f32[512,256]{1,0:T(8,128)S(1)}, f32[512,256]{1,0:T(8,128)S(1)}, u32[]{:S(2)}, u32[]{:S(2)}) collective-permute-start(f32[512,256]{1,0:T(8,128)S(1)} %copy-done.2), channel_id=1, source_target_pairs={{0,1},{1,0},{2,3},{3,2},{4,5},{5,4},{6,7},{7,6},{8,9},{9,8},{10,11... | collective-permute-start | bytes 1572872 | tf_op jit(solution)/shard_map/ppermute | solution.py:211
  31.3 18.6 %collective-permute-start.4 = (f32[512,256]{1,0:T(8,128)S(1)}, f32[512,256]{1,0:T(8,128)S(1)}, u32[]{:S(2)}, u32[]{:S(2)}) collective-permute-start(f32[512,256]{1,0:T(8,128)S(1)} %copy-done.2), channel_id=1, source_target_pairs={{0,16},{1,17},{2,18},{3,19},{4,20},{5,21},{6,22},{7,23},{8,24},{9,... | collective-permute-start | bytes 1572872 | tf_op jit(solution)/shard_map/ppermute | solution.py:211
  42.9 32.7 %collective-permute-start.23 = (f32[1024,256]{1,0:T(8,128)S(1)}, f32[1024,256]{1,0:T(8,128)S(1)}, u32[]{:S(2)}, u32[]{:S(2)}) collective-permute-start(f32[1024,256]{1,0:T(8,128)S(1)} %get-tuple-element.50.refs_0_), channel_id=1, source_target_pairs={{0,1},{1,0},{2,3},{3,2},{4,5},{5,4},{6,7},{7,6},{8,9},{9,8},{10,11... | collective-permute-start | bytes 3145736 | tf_op jit(solution)/shard_map/ppermute | solution.py:211
  63.4 16.0 %collective-permute-start.16 = (f32[512,256]{1,0:T(8,128)S(1)}, f32[512,256]{1,0:T(8,128)S(1)}, u32[]{:S(2)}, u32[]{:S(2)}) collective-permute-start(f32[512,256]{1,0:T(8,128)S(1)} %slice_bitcast_fusion.2.refs_0_), channel_id=1, source_target_pairs={{0,1},{1,0},{2,3},{3,2},{4,5},{5,4},{6,7},{7,6},{8,9},{9,8},{10,11... | collective-permute-start | bytes 1572872 | tf_op jit(solution)/shard_map/ppermute | solution.py:211
  64.3 15.6 %collective-permute-start.17 = (f32[512,256]{1,0:T(8,128)S(1)}, f32[512,256]{1,0:T(8,128)S(1)}, u32[]{:S(2)}, u32[]{:S(2)}) collective-permute-start(f32[512,256]{1,0:T(8,128)S(1)} %slice_bitcast_fusion.2.refs_0_), channel_id=1, source_target_pairs={{0,16},{1,17},{2,18},{3,19},{4,20},{5,21},{6,22},{7,23},{8,24},{9,... | collective-permute-start | bytes 1572872 | tf_op jit(solution)/shard_map/ppermute | solution.py:211
  67.6 16.2 %collective-permute-start.22 = (f32[512,256]{1,0:T(8,128)S(1)}, f32[512,256]{1,0:T(8,128)S(1)}, u32[]{:S(2)}, u32[]{:S(2)}) collective-permute-start(f32[512,256]{1,0:T(8,128)S(1)} %get-tuple-element.49), channel_id=1, source_target_pairs={{2,0},{3,1},{6,4},{7,5},{8,10},{9,11},{12,14},{13,15},{18,16},{19,... | collective-permute-start | bytes 1572872 | tf_op jit(solution)/shard_map/ppermute | solution.py:211
  68.9 28.3 %collective-permute-start.21 = (f32[512,256]{1,0:T(8,128)S(1)}, f32[512,256]{1,0:T(8,128)S(1)}, u32[]{:S(2)}, u32[]{:S(2)}) collective-permute-start(f32[512,256]{1,0:T(8,128)S(1)} %get-tuple-element.48), channel_id=1, source_target_pairs={{0,4},{1,5},{4,0},{5,1},{10,14},{11,15},{14,10},{15,11},{16,20},{1... | collective-permute-start | bytes 1572872 | tf_op jit(solution)/shard_map/ppermute | solution.py:211
  76.6 20.6 %collective-permute-start.20 = (f32[512,256]{1,0:T(8,128)S(1)}, f32[512,256]{1,0:T(8,128)S(1)}, u32[]{:S(2)}, u32[]{:S(2)}) collective-permute-start(f32[512,256]{1,0:T(8,128)S(1)} %get-tuple-element.48), channel_id=1, source_target_pairs={{2,4},{3,5},{6,0},{7,1},{8,14},{9,15},{12,10},{13,11},{18,20},{19,... | collective-permute-start | bytes 1572872 | tf_op jit(solution)/shard_map/ppermute | solution.py:211
  79.4 24.8 %collective-permute-start.27 = (f32[1024,256]{1,0:T(8,128)S(1)}, f32[1024,256]{1,0:T(8,128)S(1)}, u32[]{:S(2)}, u32[]{:S(2)}) collective-permute-start(f32[1024,256]{1,0:T(8,128)S(1)} %get-tuple-element.63.refs_0_), channel_id=1, source_target_pairs={{0,1},{1,0},{2,3},{3,2},{4,5},{5,4},{6,7},{7,6},{8,9},{9,8},{10,11... | collective-permute-start | bytes 3145736 | tf_op jit(solution)/shard_map/ppermute | solution.py:211
  79.9 19.9 %collective-permute-start.18 = (f32[512,256]{1,0:T(8,128)S(1)}, f32[512,256]{1,0:T(8,128)S(1)}, u32[]{:S(2)}, u32[]{:S(2)}) collective-permute-start(f32[512,256]{1,0:T(8,128)S(1)} %collective-permute-done.16.refs_1_), channel_id=1, source_target_pairs={{0,16},{1,17},{2,18},{3,19},{4,20},{5,21},{6,22},{7,23},{8,24},{9,... | collective-permute-start | bytes 1572872 | tf_op jit(solution)/shard_map/ppermute | solution.py:211
  97.5 15.3 %collective-permute-start.29 = (f32[512,256]{1,0:T(8,128)}, f32[512,256]{1,0:T(8,128)S(1)}, u32[]{:S(2)}, u32[]{:S(2)}) collective-permute-start(f32[512,256]{1,0:T(8,128)} %get-tuple-element.44.refs_2_), channel_id=1, source_target_pairs={{0,16},{1,17},{2,18},{3,19},{4,20},{5,21},{6,22},{7,23},{8,24},{9,... | collective-permute-start | bytes 1572872 | tf_op jit(solution)/shard_map/ppermute | solution.py:211
  104.2 18.6 %collective-permute-start.28 = (f32[512,256]{1,0:T(8,128)}, f32[512,256]{1,0:T(8,128)}, u32[]{:S(2)}, u32[]{:S(2)}) collective-permute-start(f32[512,256]{1,0:T(8,128)} %get-tuple-element.56), channel_id=1, source_target_pairs={{8,10},{9,11},{12,14},{13,15},{24,26},{25,27},{28,30},{29,31}} | collective-permute-start | bytes 1572872 | tf_op jit(solution)/shard_map/ppermute | solution.py:211
  105.7 17.5 %collective-permute-start.26 = (f32[512,256]{1,0:T(8,128)}, f32[512,256]{1,0:T(8,128)}, u32[]{:S(2)}, u32[]{:S(2)}) collective-permute-start(f32[512,256]{1,0:T(8,128)} %get-tuple-element.53), channel_id=1, source_target_pairs={{0,4},{1,5},{10,14},{11,15},{16,20},{17,21},{26,30},{27,31}} | collective-permute-start | bytes 1572872 | tf_op jit(solution)/shard_map/ppermute | solution.py:211
  124.9 23.1 %collective-permute-start.32 = (f32[512,256]{1,0:T(8,128)S(1)}, f32[512,256]{1,0:T(8,128)S(1)}, u32[]{:S(2)}, u32[]{:S(2)}) collective-permute-start(f32[512,256]{1,0:T(8,128)S(1)} %add_add_fusion.refs_2_), channel_id=1, source_target_pairs={{0,16},{1,17},{2,18},{3,19},{4,20},{5,21},{6,22},{7,23},{8,24},{9,... | collective-permute-start | bytes 1572872 | tf_op jit(solution)/shard_map/ppermute | solution.py:211
  127.4 20.6 %collective-permute-start.15 = (f32[512,128]{1,0:T(8,128)S(1)}, f32[512,128]{1,0:T(8,128)S(1)}, u32[]{:S(2)}, u32[]{:S(2)}) collective-permute-start(f32[512,128]{1,0:T(8,128)S(1)} %constant_dynamic-slice_fusion), channel_id=1, source_target_pairs={{0,0},{1,1},{2,8},{3,9},{4,16},{5,17},{6,24},{7,25},{8,2},{9,3},{1... | collective-permute-start | bytes 786440 | tf_op jit(solution)/shard_map/ppermute | solution.py:211
  153.0 15.2 %collective-permute-start.34 = (f32[1024,128]{1,0:T(8,128)S(1)}, f32[1024,128]{1,0:T(8,128)S(1)}, u32[]{:S(2)}, u32[]{:S(2)}) collective-permute-start(f32[1024,128]{1,0:T(8,128)S(1)} %shard_map.72), channel_id=1, source_target_pairs={{0,2},{1,3},{2,0},{3,1},{4,6},{5,7},{6,4},{7,5},{8,10},{9,11},{10,... | collective-permute-start | bytes 1572872 | tf_op jit(solution)/shard_map/ppermute | solution.py:211
  155.9 17.9 %collective-permute-start.31 = (f32[512,128]{1,0:T(8,128)S(1)}, f32[512,128]{1,0:T(8,128)S(1)}, u32[]{:S(2)}, u32[]{:S(2)}) collective-permute-start(f32[512,128]{1,0:T(8,128)S(1)} %dynamic-slice_add_fusion), channel_id=1, source_target_pairs={{0,0},{1,1},{2,8},{3,9},{4,16},{5,17},{6,24},{7,25},{8,2},{9,3},{1... | collective-permute-start | bytes 786440 | tf_op jit(solution)/shard_map/ppermute | solution.py:211
  168.2 25.7 %collective-permute-start.36 = (f32[1024,128]{1,0:T(8,128)S(1)}, f32[1024,128]{1,0:T(8,128)S(1)}, u32[]{:S(2)}, u32[]{:S(2)}) collective-permute-start(f32[1024,128]{1,0:T(8,128)S(1)} %add.97), channel_id=1, source_target_pairs={{0,4},{1,5},{2,6},{3,7},{4,0},{5,1},{6,2},{7,3},{8,12},{9,13},{10,... | collective-permute-start | bytes 1572872 | tf_op jit(solution)/shard_map/ppermute | solution.py:211
  173.8 23.4 %collective-permute-start.35 = (f32[1024,128]{1,0:T(8,128)S(1)}, f32[1024,128]{1,0:T(8,128)S(1)}, u32[]{:S(2)}, u32[]{:S(2)}) collective-permute-start(f32[1024,128]{1,0:T(8,128)S(1)} %get-tuple-element.67), channel_id=1, source_target_pairs={{0,2},{1,3},{2,0},{3,1},{4,6},{5,7},{6,4},{7,5},{8,10},{9,11},{10,... | collective-permute-start | bytes 1572872 | tf_op jit(solution)/shard_map/ppermute | solution.py:211
  (35 other events, 287.2 us)
